TPU v7x, 256 devices: a whole 4x4x8 slice. The times are simulated.
256 devices in a mesh: dp: 8 (over y_hi, x), pipe: 2 (over y_lo), tensor: 16 (over z, core).
Axes of the slice: x: 4, y: 4 (y_hi: 2, y_lo: 2; y = y_hi * 2 + y_lo), z: 8, core: 2. Of those that a mesh axis runs over, the one named last changes fastest.
Arguments:
- inputs: bfloat16 [2, 512, 8192], P(None, ('dp', 'tensor')), may hold values from -6 to 6
- positions: int32 [2, 512], P(None, 'dp'), may hold values from 0 to 63, as said below
- out_grads: bfloat16 [2, 512, 8192], P(None, ('dp', 'tensor')), may hold values from -6 to 6
- query_weight: bfloat16 [2, 8192, 4096], P('pipe', 'dp', 'tensor'), may hold values from -0.0625 to 0.0625
- key_value_weight: bfloat16 [2, 8192, 1024], P('pipe', 'dp', 'tensor'), may hold values from -0.0625 to 0.0625
- out_weight: bfloat16 [2, 4096, 8192], P('pipe', 'tensor', 'dp'), may hold values from -0.09375 to 0.09375
- query_stale: float32 [2, 8192, 4096], P('pipe', 'dp', 'tensor'), may hold values from -0.0625 to 0.0625
- key_value_previous_gradient: float32 [2, 8192, 1024], P('pipe', 'dp', 'tensor'), may hold values from -0.0625 to 0.0625
- out_stale: float32 [2, 4096, 8192], P('pipe', 'tensor', 'dp'), may hold values from -0.09375 to 0.09375
Outputs:
- section_outputs: bfloat16 [2, 2, 512, 8192], P('pipe', None, ('dp', 'tensor'))
- input_grads: bfloat16 [2, 2, 512, 8192], P('pipe', None, ('dp', 'tensor'))
- query_new: bfloat16 [2, 8192, 4096], P('pipe', 'dp', 'tensor')
- kv_new: bfloat16 [2, 8192, 1024], P('pipe', 'dp', 'tensor')
- out_new: bfloat16 [2, 4096, 8192], P('pipe', 'tensor', 'dp')
- query_grad: float32 [2, 8192, 4096], P('pipe', 'dp', 'tensor')
- kv_grad: float32 [2, 8192, 1024], P('pipe', 'dp', 'tensor')
- out_grad: float32 [2, 4096, 8192], P('pipe', 'tensor', 'dp')
Inputs may be any that keep to these rules, and one draw needn't show every extreme that they name: In each block of 64 tokens of a micro-batch, positions rise by one from token to token and fall back to 0 where a new document starts; every block begins at 0, and the first block of micro-batch 0 is one document.
All inputs are finite; a program needn't handle non-finite values.
Results may differ from a plain program's by a relative error of at most 0.035.
Values may be sent and summed in bfloat16 or wider, within the bound.
No kernel may reach another device: no remote copies, remote signals or barrier semaphores. Data moves between devices by JAX's collectives and lax.ppermute only.
A program may use at most 128 MiB of HBM per device.

v0:
```python
import math

import jax
import jax.numpy as jnp
from jax import lax
from jax.sharding import PartitionSpec as P

HEAD_SIZE = 128


EPS = 1e-05
THETA = 500000.0
LR = 0.5


def from_partner(value, axis, distance):
    mask = 2**distance
    pairs = [(source, source ^ mask) for source in range(lax.axis_size(axis))]
    return lax.ppermute(value, axis, pairs)


def saved_state(values):
    return lax.optimization_barrier(values.astype(jnp.bfloat16)).astype(jnp.float32)


def rms_scale(rows):
    return rows * lax.rsqrt(jnp.mean(rows * rows, axis=-1, keepdims=True) + EPS)


def rotate(values, positions, sign):
    half = values.shape[-1] // 2
    freqs = THETA ** (-2.0 * jnp.arange(half, dtype=jnp.float32) / values.shape[-1])
    angles = positions.astype(jnp.float32)[:, None] * freqs[None, :]
    cosine = jnp.cos(angles)[:, None, :]
    sine = sign * jnp.sin(angles)[:, None, :]
    first = values[..., :half]
    second = values[..., half:]
    return jnp.concatenate(
        [first * cosine - second * sine, second * cosine + first * sine], axis=-1
    )


def visible_keys(positions):
    index = jnp.arange(positions.shape[0], dtype=jnp.int32)
    lowest = index - positions
    return (index[None, :] <= index[:, None]) & (index[None, :] >= lowest[:, None])


def attend(queries, keys, values, visible):
    scores = jnp.einsum("qgh,kh->gqk", queries, keys, precision=lax.Precision.HIGHEST) / math.sqrt(
        queries.shape[-1]
    )
    scores = jnp.where(visible[None], scores, -1e30)
    weights = jnp.exp(scores)
    probs = weights / jnp.sum(weights, axis=-1, keepdims=True)
    probs = probs + lax.stop_gradient(saved_state(probs) - probs)
    return jnp.einsum("gqk,kh->qgh", probs, values, precision=lax.Precision.HIGHEST)


def gather_rows(stacked):
    return lax.all_gather(stacked, "tensor", axis=1, tiled=True)


def reduce_rows(term):
    return lax.psum_scatter(
        term.astype(jnp.bfloat16), "tensor", scatter_dimension=0, tiled=True
    ).astype(jnp.float32)


def cross_section(block):
    return from_partner(block, "pipe", 0)


def heads_of(normalized_rows, positions, full_q, full_kv, rank):
    token_list = normalized_rows.shape[0]
    cols = full_kv.shape[1]
    query_proj = jnp.dot(normalized_rows, full_q, preferred_element_type=jnp.float32)
    kv_part = jnp.dot(normalized_rows, full_kv, preferred_element_type=jnp.float32).astype(
        jnp.bfloat16
    )
    kv_all = gather_rows(kv_part.T[None])[0]
    head = rank * cols // (2 * HEAD_SIZE)
    block = lax.dynamic_slice_in_dim(kv_all, head * 2 * HEAD_SIZE, 2 * HEAD_SIZE, 0).T.astype(
        jnp.float32
    )
    keys = saved_state(rotate(block[:, None, :HEAD_SIZE], positions, 1.0))[:, 0]
    values = block[:, HEAD_SIZE:]
    queries = saved_state(rotate(query_proj.reshape(token_list, -1, HEAD_SIZE), positions, 1.0))
    return (queries, keys, values, head)


def forward_front(shard, positions, full_q, full_kv, rank):
    normalized_rows = gather_rows(rms_scale(shard.astype(jnp.float32)).astype(jnp.bfloat16)[None])[
        0
    ]
    queries, keys, values, head = heads_of(normalized_rows, positions, full_q, full_kv, rank)
    weighted = attend(queries, keys, values, visible_keys(positions))
    mixed = weighted.reshape(weighted.shape[0], -1).astype(jnp.bfloat16)
    return (normalized_rows, mixed)


def forward_rear(shard, mixed, full_o):
    reduced = reduce_rows(jnp.dot(mixed, full_o, preferred_element_type=jnp.float32))
    return (shard.astype(jnp.float32) + reduced).astype(jnp.bfloat16)


def backward_tick(
    shard, normalized_rows, positions, grad_shard, full_q, full_kv, full_o, rank, ranks
):
    token_list = normalized_rows.shape[0]
    cols = full_kv.shape[1]
    grad_full = gather_rows(grad_shard[None])[0]
    queries, keys, values, head = heads_of(normalized_rows, positions, full_q, full_kv, rank)
    visible = visible_keys(positions)
    weighted, pullback = jax.vjp(
        lambda first, second, third: attend(first, second, third, visible), queries, keys, values
    )
    mixed = weighted.reshape(token_list, -1).astype(jnp.bfloat16)
    d_mixed = jnp.dot(grad_full, full_o.T, preferred_element_type=jnp.float32).reshape(
        weighted.shape
    )
    d_query, d_key, d_value = pullback(d_mixed)
    dq_proj = rotate(d_query, positions, -1.0).reshape(token_list, -1).astype(jnp.bfloat16)
    dk_proj = rotate(d_key[:, None], positions, -1.0)[:, 0]
    contrib = jnp.concatenate([dk_proj, d_value], axis=1).T
    term = lax.dynamic_update_slice_in_dim(
        jnp.zeros((ranks * cols, token_list), jnp.float32), contrib, head * 2 * HEAD_SIZE, 0
    )
    dkv_rows = reduce_rows(term).astype(jnp.bfloat16)
    d_normed = jnp.dot(dq_proj, full_q.T, preferred_element_type=jnp.float32)
    d_normed = d_normed + jnp.dot(dkv_rows.T, full_kv.T, preferred_element_type=jnp.float32)
    d_rows = reduce_rows(d_normed)
    _, norm_pull = jax.vjp(rms_scale, shard.astype(jnp.float32))
    d_shard = (grad_shard.astype(jnp.float32) + norm_pull(d_rows)[0]).astype(jnp.bfloat16)
    return (d_shard, (normalized_rows, dq_proj, dkv_rows, mixed, grad_full))


def joined(leading, opening, middle, closing):
    early = [jnp.where(leading, second, first) for first, second in zip(opening, middle)]
    late = [jnp.where(leading, second, first) for first, second in zip(middle, closing)]
    normed_cat = jnp.concatenate([early[0], late[0]], axis=0)
    query_cat = jnp.concatenate([early[1], late[1]], axis=0)
    pair_cat = jnp.concatenate([early[2], late[2]], axis=1)
    mixed_cat = jnp.concatenate([early[3], late[3]], axis=0)
    grad_cat = jnp.concatenate([early[4], late[4]], axis=0)
    return (normed_cat, query_cat, pair_cat, mixed_cat, grad_cat)


def shards(
    inputs,
    positions,
    out_grads,
    query_weight,
    key_value_weight,
    out_weight,
    query_stale,
    key_value_previous_gradient,
    out_stale,
):
    ranks = lax.axis_size("tensor")
    rank = lax.axis_index("tensor")
    first = lax.axis_index("pipe") == 0
    query_new = (query_weight.astype(jnp.float32) - LR * query_stale).astype(jnp.bfloat16)
    kv_new = (key_value_weight.astype(jnp.float32) - LR * key_value_previous_gradient).astype(
        jnp.bfloat16
    )
    out_new = (out_weight.astype(jnp.float32) - LR * out_stale).astype(jnp.bfloat16)
    full_q, full_kv, full_o = (
        lax.all_gather(query_new[0], "dp", axis=0, tiled=True),
        lax.all_gather(kv_new[0], "dp", axis=0, tiled=True),
        lax.all_gather(out_new[0], "dp", axis=1, tiled=True),
    )
    normed_a, mixed_a = forward_front(inputs[0], positions[0], full_q, full_kv, rank)
    out_a = forward_rear(inputs[0], mixed_a, full_o)
    recv_a = cross_section(out_a)
    in_b = jnp.where(first, inputs[1], recv_a)
    pos_b = jnp.where(first, positions[1], positions[0])
    normed_b, mixed_b = forward_front(in_b, pos_b, full_q, full_kv, rank)
    out_b = forward_rear(in_b, mixed_b, full_o)
    recv_b = cross_section(out_b)
    in_c = jnp.where(first, inputs[1], recv_b)
    normed_c, mixed_c = forward_front(in_c, positions[1], full_q, full_kv, rank)
    out_c = forward_rear(in_c, mixed_c, full_o)
    section_out = jnp.where(first, jnp.stack([out_a, out_b]), jnp.stack([out_b, out_c]))
    silent = jnp.zeros_like(out_grads[0])
    back_one, parts_one = backward_tick(
        jnp.where(first, inputs[0], recv_a),
        jnp.where(first, normed_a, normed_b),
        positions[0],
        jnp.where(first, silent, out_grads[0]),
        full_q,
        full_kv,
        full_o,
        rank,
        ranks,
    )
    recv_c = cross_section(back_one)
    back_two, parts_two = backward_tick(
        jnp.where(first, inputs[0], recv_b),
        jnp.where(first, normed_a, normed_c),
        jnp.where(first, positions[0], positions[1]),
        jnp.where(first, recv_c, out_grads[1]),
        full_q,
        full_kv,
        full_o,
        rank,
        ranks,
    )
    recv_d = cross_section(back_two)
    back_three, parts_three = backward_tick(
        in_c,
        normed_b,
        positions[1],
        jnp.where(first, recv_d, silent),
        full_q,
        full_kv,
        full_o,
        rank,
        ranks,
    )
    input_grad = jnp.where(
        first, jnp.stack([back_two, back_three]), jnp.stack([back_one, back_two])
    )
    normed_cat, query_cat, pair_cat, mixed_cat, grad_cat = joined(
        first, parts_one, parts_two, parts_three
    )
    term_q = jnp.dot(normed_cat.T, query_cat, preferred_element_type=jnp.float32)
    term_kv = jnp.dot(normed_cat.T, pair_cat.T, preferred_element_type=jnp.float32)
    term_o = jnp.dot(mixed_cat.T, grad_cat, preferred_element_type=jnp.float32)
    grad_q, grad_kv, grad_o = (
        lax.psum_scatter(term_q.astype(jnp.bfloat16), "dp", scatter_dimension=0, tiled=True).astype(
            jnp.float32
        ),
        lax.psum_scatter(
            term_kv.astype(jnp.bfloat16), "dp", scatter_dimension=0, tiled=True
        ).astype(jnp.float32),
        lax.psum_scatter(term_o.astype(jnp.bfloat16), "dp", scatter_dimension=1, tiled=True).astype(
            jnp.float32
        ),
    )
    return (
        section_out[None],
        input_grad[None],
        query_new,
        kv_new,
        out_new,
        grad_q[None],
        grad_kv[None],
        grad_o[None],
    )


def solution(mesh):
    placed = (
        P(None, ("dp", "tensor"), None),
        P(None, "dp"),
        P(None, ("dp", "tensor"), None),
        P("pipe", "dp", "tensor"),
        P("pipe", "dp", "tensor"),
        P("pipe", "tensor", "dp"),
        P("pipe", "dp", "tensor"),
        P("pipe", "dp", "tensor"),
        P("pipe", "tensor", "dp"),
    )
    return jax.shard_map(
        shards,
        mesh=mesh,
        in_specs=placed,
        out_specs=(
            P("pipe", None, ("dp", "tensor"), None),
            P("pipe", None, ("dp", "tensor"), None),
            P("pipe", "dp", "tensor"),
            P("pipe", "dp", "tensor"),
            P("pipe", "tensor", "dp"),
            P("pipe", "dp", "tensor"),
            P("pipe", "dp", "tensor"),
            P("pipe", "tensor", "dp"),
        ),
        check_vma=False,
    )
```

profile of v0, /device:TPU:8, one launch (start us, length us, event | category | flops | bytes accessed | tf_op | source)
XLA Modules:
  0.0 1468.1 jit_solution(5343096857729335940)
XLA Ops:
  11.9 2.3 subtract_convert_fusion.1
  18.2 34.9 %all-gather.26.cloned.1.call-done = bf16[1,64,8192]{2,0,1:T(2,128)(2,1)} async-done(((bf16[1,4,8192]{2,0,1:T(2,128)(2,1)}), bf16[1,64,8192]{2,0,1:T(2,128)(2,1)}) %all-gather.26.cloned.1.call-update) | async-done | bytes 1048592 | tf_op jit(solution)/shard_map/all_gather | solution.py:61
  53.1 2.7 copy.241
  55.8 50.3 %all-gather.30.cloned.1.call-done = bf16[1,8192,64]{1,2,0:T(8,128)(2,1)} async-done(((bf16[1,1024,64]{1,2,0:T(8,128)(2,1)}), bf16[1,8192,64]{1,2,0:T(8,128)(2,1)}) %all-gather.30.cloned.1.call-update) | async-done | bytes 1048592 | tf_op jit(solution)/shard_map/all_gather | solution.py:170
  107.7 18.1 %all-gather.1 = bf16[1024,64]{1,0:T(8,128)(2,1)S(1)} all-gather(bf16[64,64]{1,0:T(8,128)(2,1)S(1)} %convolution_convert_fusion.16), channel_id=3, replica_groups=mesh['dp'=8,'pipe'=2,'tensor'=16] {'tensor'}, dimensions={0}, use_global_device_ids=true | all-gather | bytes 139264 | tf_op jit(solution)/shard_map/all_gather | solution.py:61
  126.1 58.8 %all-gather.32.cloned.1.call-done = bf16[1,8192,256]{2,1,0:T(8,128)(2,1)} async-done(((bf16[1,1024,256]{2,1,0:T(8,128)(2,1)}), bf16[1,8192,256]{2,1,0:T(8,128)(2,1)}) %all-gather.32.cloned.1.call-update) | async-done | bytes 4194320 | tf_op jit(solution)/shard_map/all_gather | solution.py:169
  184.9 6.4 copy.138
  191.3 3.6 fusion.32
  195.6 66.9 %all-gather.34.cloned.1.call-done = bf16[1,256,8192]{2,1,0:T(8,128)(2,1)} async-done(((bf16[1,256,1024]{2,1,0:T(8,128)(2,1)}), bf16[1,256,8192]{2,1,0:T(8,128)(2,1)}) %all-gather.34.cloned.1.call-update) | async-done | bytes 4194320 | tf_op jit(solution)/shard_map/all_gather | solution.py:171
  262.6 4.0 convolution_convert_fusion.5
  267.9 109.1 %all-reduce.13.cloned.1.call-done = bf16[64,8192]{1,0:T(8,128)(2,1)} async-done(((bf16[64,8192]{1,0:T(8,128)(2,1)}), bf16[64,8192]{1,0:T(8,128)(2,1)}) %all-reduce.13.cloned.1.call-update) | async-done | bytes 1048592
  379.4 2.9 collective-permute-done
  383.9 36.2 %all-gather.28.cloned.1.call-done = bf16[1,64,8192]{2,0,1:T(2,128)(2,1)} async-done(((bf16[1,4,8192]{2,0,1:T(2,128)(2,1)}), bf16[1,64,8192]{2,0,1:T(2,128)(2,1)}) %all-gather.28.cloned.1.call-update) | async-done | bytes 1048592 | tf_op jit(solution)/shard_map/all_gather | solution.py:61
  420.1 5.2 convolution_bitcast_fusion.8
  425.4 34.2 %all-gather.36.cloned.1.call-done = bf16[16,4,8192]{2,1,0:T(4,128)(2,1)} async-done(((bf16[1,4,8192]{2,1,0:T(4,128)(2,1)}), bf16[16,4,8192]{2,1,0:T(4,128)(2,1)}) %all-gather.36.cloned.1.call-update) | async-done | bytes 1048592 | tf_op jit(solution)/shard_map/all_gather | solution.py:61
  461.4 16.3 %all-gather.8 = bf16[1024,64]{1,0:T(8,128)(2,1)S(1)} all-gather(bf16[64,64]{1,0:T(8,128)(2,1)S(1)} %convolution_convert_fusion.13), channel_id=10, replica_groups=mesh['dp'=8,'pipe'=2,'tensor'=16] {'tensor'}, dimensions={0}, use_global_device_ids=true | all-gather | bytes 139264 | tf_op jit(solution)/shard_map/all_gather | solution.py:61
  478.7 15.9 %all-gather.5 = bf16[1024,64]{1,0:T(8,128)(2,1)S(1)} all-gather(bf16[64,64]{1,0:T(8,128)(2,1)S(1)} %convolution_convert_fusion.15), channel_id=7, replica_groups=mesh['dp'=8,'pipe'=2,'tensor'=16] {'tensor'}, dimensions={0}, use_global_device_ids=true | all-gather | bytes 139264 | tf_op jit(solution)/shard_map/all_gather | solution.py:61
  499.2 4.0 fusion.37
  509.0 4.0 fusion.253
  519.9 4.9 fusion.8
  526.6 46.6 %reduce-scatter.7.cloned.1.call-done = bf16[64,64]{1,0:T(8,128)(2,1)} async-done(((bf16[1024,64]{1,0:T(8,128)(2,1)}), bf16[64,64]{1,0:T(8,128)(2,1)}) %reduce-scatter.7.cloned.1.call-update) | async-done | bytes 8208 | tf_op jit(solution)/shard_map/reduce_scatter | solution.py:65
  573.2 3.0 fusion
  576.3 114.2 %all-reduce.19.cloned.1.call-done = (bf16[64,8192]{1,0:T(8,128)(2,1)}, bf16[64,8192]{1,0:T(8,128)(2,1)}) async-done(((bf16[64,8192]{1,0:T(8,128)(2,1)}, bf16[64,8192]{1,0:T(8,128)(2,1)}), (bf16[64,8192]{1,0:T(8,128)(2,1)}, bf16[64,8192]{1,0:T(8,128)(2,1)})) %all-reduce.19.cloned.1.call-update) | async-done | bytes 2097168
  692.8 3.0 collective-permute-done.1
  695.8 2.4 fusion.57
  703.9 2.4 collective-permute-done.2
  708.0 31.0 %all-gather.38.cloned.1.call-done = bf16[16,4,8192]{2,1,0:T(4,128)(2,1)} async-done(((bf16[1,4,8192]{2,1,0:T(4,128)(2,1)}), bf16[16,4,8192]{2,1,0:T(4,128)(2,1)}) %all-gather.38.cloned.1.call-update) | async-done | bytes 1048592 | tf_op jit(solution)/shard_map/all_gather | solution.py:61
  742.7 16.3 %all-gather.7 = bf16[1024,64]{1,0:T(8,128)(2,1)S(1)} all-gather(bf16[64,64]{1,0:T(8,128)(2,1)S(1)} %convolution_convert_fusion.14), channel_id=9, replica_groups=mesh['dp'=8,'pipe'=2,'tensor'=16] {'tensor'}, dimensions={0}, use_global_device_ids=true | all-gather | bytes 139264 | tf_op jit(solution)/shard_map/all_gather | solution.py:61
  760.7 15.9 %all-gather.10 = bf16[1024,64]{1,0:T(8,128)(2,1)S(1)} all-gather(bf16[64,64]{1,0:T(8,128)(2,1)S(1)} %convolution_convert_fusion.12), channel_id=12, replica_groups=mesh['dp'=8,'pipe'=2,'tensor'=16] {'tensor'}, dimensions={0}, use_global_device_ids=true | all-gather | bytes 139264 | tf_op jit(solution)/shard_map/all_gather | solution.py:61
  780.4 3.9 fusion.35
  787.4 3.6 convolution_bitcast_fusion.5
  795.0 4.9 fusion.6
  799.9 49.7 %reduce-scatter.9.cloned.1.call-done = bf16[64,64]{1,0:T(8,128)(2,1)} async-done(((bf16[1024,64]{1,0:T(8,128)(2,1)}), bf16[64,64]{1,0:T(8,128)(2,1)}) %reduce-scatter.9.cloned.1.call-update) | async-done | bytes 8208 | tf_op jit(solution)/shard_map/reduce_scatter | solution.py:65
  849.7 3.0 fusion.1
  854.7 108.2 %all-reduce.15.cloned.1.call-done = bf16[64,8192]{1,0:T(8,128)(2,1)} async-done(((bf16[64,8192]{1,0:T(8,128)(2,1)}), bf16[64,8192]{1,0:T(8,128)(2,1)}) %all-reduce.15.cloned.1.call-update) | async-done | bytes 1048592
  970.4 4.0 fusion.254
  978.7 31.4 %all-gather.42.cloned.1.call-done = bf16[16,4,8192]{2,1,0:T(4,128)(2,1)} async-done(((bf16[1,4,8192]{2,1,0:T(4,128)(2,1)}), bf16[16,4,8192]{2,1,0:T(4,128)(2,1)}) %all-gather.42.cloned.1.call-update) | async-done | bytes 1048592 | tf_op jit(solution)/shard_map/all_gather | solution.py:61
  1011.5 3.6 convolution_bitcast_fusion.2
  1021.2 4.9 fusion.10
  1026.2 48.9 %reduce-scatter.11.cloned.1.call-done = bf16[64,64]{1,0:T(8,128)(2,1)} async-done(((bf16[1024,64]{1,0:T(8,128)(2,1)}), bf16[64,64]{1,0:T(8,128)(2,1)}) %reduce-scatter.11.cloned.1.call-update) | async-done | bytes 8208 | tf_op jit(solution)/shard_map/reduce_scatter | solution.py:65
  1075.1 3.1 fusion.2
  1078.3 2.8 broadcast_select_fusion.2
  1083.8 4.5 convolution_convert_fusion.1
  1096.1 3.3 convolution_convert_fusion
  1099.4 92.9 %all-reduce.17.cloned.1.call-done = (bf16[64,8192]{1,0:T(8,128)(2,1)}, bf16[64,8192]{1,0:T(8,128)(2,1)}) async-done(((bf16[64,8192]{1,0:T(8,128)(2,1)}, bf16[64,8192]{1,0:T(8,128)(2,1)}), (bf16[64,8192]{1,0:T(8,128)(2,1)}, bf16[64,8192]{1,0:T(8,128)(2,1)})) %all-reduce.17.cloned.1.call-update) | async-done | bytes 2097168
  1195.6 77.5 %reduce-scatter.15.cloned.1.call-done = bf16[1024,64]{0,1:T(8,128)(2,1)} async-done(((bf16[8192,64]{0,1:T(8,128)(2,1)}), bf16[1024,64]{0,1:T(8,128)(2,1)}) %reduce-scatter.15.cloned.1.call-update) | async-done | bytes 131088 | tf_op jit(solution)/shard_map/reduce_scatter | solution.py:234
  1274.8 91.4 %reduce-scatter.13.cloned.1.call-done = bf16[1024,256]{1,0:T(8,128)(2,1)} async-done(((bf16[8192,256]{1,0:T(8,128)(2,1)}), bf16[1024,256]{1,0:T(8,128)(2,1)}) %reduce-scatter.13.cloned.1.call-update) | async-done | bytes 524304 | tf_op jit(solution)/shard_map/reduce_scatter | solution.py:231
  1368.2 91.0 %reduce-scatter.17.cloned.1.call-done = bf16[256,1024]{1,0:T(8,128)(2,1)} async-done(((bf16[256,8192]{1,0:T(8,128)(2,1)}), bf16[256,1024]{1,0:T(8,128)(2,1)}) %reduce-scatter.17.cloned.1.call-update) | async-done | bytes 524304 | tf_op jit(solution)/shard_map/reduce_scatter | solution.py:237
  (384 shorter events, 103.3 us)
Async XLA Ops:
  7.2 45.9 %all-gather.26.cloned.1.call-start = ((), (), s32[]{:S(2)}) async-start(), calls=%async_computation.6 | async-start | bytes 2228224 | tf_op jit(solution)/shard_map/all_gather | solution.py:61
  10.1 96.0 %all-gather.30.cloned.1.call-start = ((), (), s32[]{:S(2)}) async-start(), calls=%async_computation.14 | async-start | bytes 1179648 | tf_op jit(solution)/shard_map/all_gather | solution.py:170
  11.8 173.1 %all-gather.32.cloned.1.call-start = ((), (), s32[]{:S(2)}) async-start(), calls=%async_computation.15 | async-start | bytes 4718592 | tf_op jit(solution)/shard_map/all_gather | solution.py:169
  14.2 248.4 %all-gather.34.cloned.1.call-start = ((), (), s32[]{:S(2)}) async-start(), calls=%async_computation.16 | async-start | bytes 4718592 | tf_op jit(solution)/shard_map/all_gather | solution.py:171
  16.2 360.7 %all-reduce.13.cloned.1.call-start = ((), (), s32[]{:S(2)}) async-start(), calls=%async_computation.21 | async-start | bytes 2097152
  16.9 174.3 %copy-start.74 = (f32[64]{0:T(128)}, f32[64]{0:T(128)S(1)}, u32[]{:S(2)}) copy-start(f32[64]{0:T(128)S(1)} %convert_element_type.430) | copy-start | bytes 772
  16.9 174.3 %copy-start.88 = (f32[64]{0:T(128)}, f32[64]{0:T(128)S(1)}, u32[]{:S(2)}) copy-start(f32[64]{0:T(128)S(1)} %convert_element_type.396) | copy-start | bytes 772
  17.0 174.3 %copy-start.64 = (f32[64]{0:T(128)}, f32[64]{0:T(128)S(1)}, u32[]{:S(2)}) copy-start(f32[64]{0:T(128)S(1)} %multiply_power_fusion) | copy-start | bytes 772
  17.0 174.3 %copy-start.68 = (f32[64]{0:T(128)}, f32[64]{0:T(128)S(1)}, u32[]{:S(2)}) copy-start(f32[64]{0:T(128)S(1)} %get-tuple-element.94) | copy-start | bytes 772
  17.0 174.3 %copy-start.70 = (f32[64]{0:T(128)}, f32[64]{0:T(128)S(1)}, u32[]{:S(2)}) copy-start(f32[64]{0:T(128)S(1)} %get-tuple-element.95) | copy-start | bytes 772
  194.9 71.8 %copy-start.92 = (u32[256]{0:T(256)S(1)}, u32[256]{0:T(256)}, u32[]{:S(2)}) copy-start(u32[256]{0:T(256)} %constant.110) | copy-start | bytes 3076
  194.9 182.1 %copy-start.6 = (bf16[2,4,8192]{2,1,0:T(4,128)(2,1)S(1)}, bf16[2,4,8192]{2,1,0:T(4,128)(2,1)}, u32[]{:S(2)}) copy-start(bf16[2,4,8192]{2,1,0:T(4,128)(2,1)} %param.9) | copy-start | bytes 393220
  194.9 183.7 %copy-start.11 = (bf16[2,4,8192]{2,1,0:T(4,128)(2,1)S(1)}, bf16[2,4,8192]{2,1,0:T(4,128)(2,1)}, u32[]{:S(2)}) copy-start(bf16[2,4,8192]{2,1,0:T(4,128)(2,1)} %param.11) | copy-start | bytes 393220
  266.6 153.6 %all-gather.28.cloned.1.call-start = ((), (), s32[]{:S(2)}) async-start(), calls=%async_computation.7 | async-start | bytes 2228224 | tf_op jit(solution)/shard_map/all_gather | solution.py:61
  377.9 47.5 %copy-start.18 = (bf16[4,8192]{1,0:T(4,128)(2,1)}, bf16[4,8192]{1,0:T(4,128)(2,1)S(1)}, u32[]{:S(2)}) copy-start(bf16[4,8192]{1,0:T(4,128)(2,1)S(1)} %fusion.53) | copy-start | bytes 196612
  377.9 83.0 %copy-start.2 = (bf16[1,8192,64]{1,2,0:T(8,128)(2,1)S(1)}, bf16[1,8192,64]{1,2,0:T(8,128)(2,1)}, u32[]{:S(2)}) copy-start(bf16[1,8192,64]{1,2,0:T(8,128)(2,1)} %all-gather.30.cloned.1.call-done) | copy-start | bytes 3145732
  377.9 4.4 collective-permute-start
  379.4 80.2 %all-gather.36.cloned.1.call-start = ((), (), s32[]{:S(2)}) async-start(), calls=%async_computation.17 | async-start | bytes 1114112 | tf_op jit(solution)/shard_map/all_gather | solution.py:61
  383.2 190.0 %reduce-scatter.7.cloned.1.call-start = ((), (), s32[]{:S(2)}) async-start(), calls=%async_computation.8 | async-start | bytes 278528 | tf_op jit(solution)/shard_map/reduce_scatter | solution.py:65
  517.6 172.9 %all-reduce.19.cloned.1.call-start = ((), (), s32[]{:S(2)}) async-start(), calls=%async_computation.24 | async-start | bytes 4194304
  576.3 162.7 %all-gather.38.cloned.1.call-start = ((), (), s32[]{:S(2)}) async-start(), calls=%async_computation.18 | async-start | bytes 1114112 | tf_op jit(solution)/shard_map/all_gather | solution.py:61
  691.5 4.4 collective-permute-start.1
  692.8 99.8 %copy-start.62 = (pred[64,64]{0,1:T(8,128)(4,1)}, pred[64,64]{0,1:T(8,128)(4,1)S(1)}, u32[]{:S(2)}) copy-start(pred[64,64]{0,1:T(8,128)(4,1)S(1)} %fusion.215) | copy-start | bytes 12292
  700.2 85.8 %all-gather.40.cloned.1.call-start = ((), (), s32[]{:S(2)}) async-start(), calls=%async_computation.19 | async-start | bytes 1114112 | tf_op jit(solution)/shard_map/all_gather | solution.py:61
  702.0 4.4 collective-permute-start.2
  706.4 70.3 %copy-start.24 = (bf16[4,8192]{1,0:T(4,128)(2,1)}, bf16[4,8192]{1,0:T(4,128)(2,1)S(1)}, u32[]{:S(2)}) copy-start(bf16[4,8192]{1,0:T(4,128)(2,1)S(1)} %collective-permute-done.2) | copy-start | bytes 196612
  707.9 141.8 %reduce-scatter.9.cloned.1.call-start = ((), (), s32[]{:S(2)}) async-start(), calls=%async_computation.9 | async-start | bytes 278528 | tf_op jit(solution)/shard_map/reduce_scatter | solution.py:65
  794.1 168.9 %all-reduce.15.cloned.1.call-start = ((), (), s32[]{:S(2)}) async-start(), calls=%async_computation.22 | async-start | bytes 2097152
  795.0 57.8 %copy-start.12 = (bf16[64,2,64]{2,0,1:T(8,128)(2,1)}, bf16[64,2,64]{2,0,1:T(8,128)(2,1)S(1)}, u32[]{:S(2)}) copy-start(bf16[64,2,64]{2,0,1:T(8,128)(2,1)S(1)} %get-tuple-element.34) | copy-start | bytes 49156
  795.0 57.8 %copy-start.14 = (bf16[64,2,64]{2,0,1:T(8,128)(2,1)}, bf16[64,2,64]{2,0,1:T(8,128)(2,1)S(1)}, u32[]{:S(2)}) copy-start(bf16[64,2,64]{2,0,1:T(8,128)(2,1)S(1)} %get-tuple-element.35) | copy-start | bytes 49156
  799.9 167.2 %copy-start.4 = (bf16[16,4,8192]{2,1,0:T(4,128)(2,1)S(1)}, bf16[16,4,8192]{2,1,0:T(4,128)(2,1)}, u32[]{:S(2)}) copy-start(bf16[16,4,8192]{2,1,0:T(4,128)(2,1)} %all-gather.38.cloned.1.call-done) | copy-start | bytes 3145732
  852.8 121.7 %copy-start.58 = (bf16[64,1,64]{0,2,1:T(8,128)(2,1)S(1)}, bf16[64,1,64]{0,2,1:T(8,128)(2,1)}, u32[]{:S(2)}) copy-start(bf16[64,1,64]{0,2,1:T(8,128)(2,1)} %get-tuple-element.113) | copy-start | bytes 24580
  852.8 121.7 %copy-start.59 = (bf16[64,1,64]{0,2,1:T(8,128)(2,1)S(1)}, bf16[64,1,64]{0,2,1:T(8,128)(2,1)}, u32[]{:S(2)}) copy-start(bf16[64,1,64]{0,2,1:T(8,128)(2,1)} %get-tuple-element.114) | copy-start | bytes 24580
  852.8 121.7 %copy-start.16 = (f32[64,64]{1,0:T(8,128)S(1)}, f32[64,64]{1,0:T(8,128)}, u32[]{:S(2)}) copy-start(f32[64,64]{1,0:T(8,128)} %get-tuple-element.85) | copy-start | bytes 49156
  852.8 157.3 %all-gather.42.cloned.1.call-start = ((), (), s32[]{:S(2)}) async-start(), calls=%async_computation.20 | async-start | bytes 1114112 | tf_op jit(solution)/shard_map/all_gather | solution.py:61
  965.2 4.5 collective-permute-start.3
  970.3 104.8 %reduce-scatter.11.cloned.1.call-start = ((), (), s32[]{:S(2)}) async-start(), calls=%async_computation.10 | async-start | bytes 278528 | tf_op jit(solution)/shard_map/reduce_scatter | solution.py:65
  1020.1 172.2 %all-reduce.17.cloned.1.call-start = ((), (), s32[]{:S(2)}) async-start(), calls=%async_computation.23 | async-start | bytes 4194304
  1026.2 52.1 %copy-start.3 = (bf16[64,8192]{1,0:T(8,128)(2,1)S(1)}, bf16[64,8192]{1,0:T(8,128)(2,1)}, u32[]{:S(2)}) copy-start(bf16[64,8192]{1,0:T(8,128)(2,1)} %reshape.1199) | copy-start | bytes 3145732
  1078.3 194.9 %reduce-scatter.15.cloned.1.call-start = ((), (), s32[]{:S(2)}) async-start(), calls=%async_computation.12 | async-start | bytes 1179648 | tf_op jit(solution)/shard_map/reduce_scatter | solution.py:234
  1083.6 282.5 %reduce-scatter.13.cloned.1.call-start = ((), (), s32[]{:S(2)}) async-start(), calls=%async_computation.11 | async-start | bytes 4718592 | tf_op jit(solution)/shard_map/reduce_scatter | solution.py:231
  1088.4 370.8 %reduce-scatter.17.cloned.1.call-start = ((), (), s32[]{:S(2)}) async-start(), calls=%async_computation.13 | async-start | bytes 4718592 | tf_op jit(solution)/shard_map/reduce_scatter | solution.py:237
  1096.0 97.4 %copy-start.91 = (f32[4]{0:T(128)S(1)}, f32[4]{0:T(128)}, u32[]{:S(2)}) copy-start(f32[4]{0:T(128)} %copy-done.90) | copy-start | bytes 52
  1096.0 97.4 %copy-start.87 = (f32[4]{0:T(128)S(1)}, f32[4]{0:T(128)}, u32[]{:S(2)}) copy-start(f32[4]{0:T(128)} %copy-done.86) | copy-start | bytes 52
  1096.0 98.6 %copy-start.19 = (bf16[4,8192]{1,0:T(4,128)(2,1)S(1)}, bf16[4,8192]{1,0:T(4,128)(2,1)}, u32[]{:S(2)}) copy-start(bf16[4,8192]{1,0:T(4,128)(2,1)} %copy-done.18) | copy-start | bytes 196612
  1096.0 98.6 %copy-start.21 = (bf16[4,8192]{1,0:T(4,128)(2,1)S(1)}, bf16[4,8192]{1,0:T(4,128)(2,1)}, u32[]{:S(2)}) copy-start(bf16[4,8192]{1,0:T(4,128)(2,1)} %copy-done.20) | copy-start | bytes 196612
  1096.1 98.6 %copy-start.23 = (bf16[4,8192]{1,0:T(4,128)(2,1)S(1)}, bf16[4,8192]{1,0:T(4,128)(2,1)}, u32[]{:S(2)}) copy-start(bf16[4,8192]{1,0:T(4,128)(2,1)} %copy-done.22) | copy-start | bytes 196612
  1096.1 98.6 %copy-start.31 = (bf16[4,8192]{1,0:T(4,128)(2,1)S(1)}, bf16[4,8192]{1,0:T(4,128)(2,1)}, u32[]{:S(2)}) copy-start(bf16[4,8192]{1,0:T(4,128)(2,1)} %copy-done.30) | copy-start | bytes 196612
  (73 other events, 555.7 us)
Sparse Core Ops, SparseCore 0:
  10.4 42.6 all-gather.25
  56.3 49.7 all-gather.29
  109.3 75.5 all-gather.31
  187.9 74.5 all-gather.33
  266.7 110.2 all-reduce.12
  379.5 40.5 all-gather.27
  422.7 36.8 all-gather.35
  517.7 55.4 reduce-scatter.6
  576.4 114.0 all-reduce.18
  700.3 38.6 all-gather.37
  741.4 37.3 all-gather.39
  794.2 55.4 reduce-scatter.8
  852.9 110.0 all-reduce.14
  970.4 39.6 all-gather.41
  1020.2 54.8 reduce-scatter.10
  1078.4 113.9 all-reduce.16
  1196.6 76.4 reduce-scatter.14
  1277.2 88.9 reduce-scatter.12
  1370.3 88.8 reduce-scatter.16
where the time goes:
time: 1480 us; the launch traced here: 1470 us
  waiting for transfers between devices  1180 us (80%)
  matrix products  92.6 us (6%)
  blocking collectives  82.5 us (6%)
  other arithmetic  55.1 us (4%)
  local copies, waits for them, and re-layouts  34.8 us (2%)
  between operations  16.5 us (1%)
    unnamed x23, waiting for transfers between devices  425 us
    all_gather x6, waiting for transfers between devices, gather_rows(): return lax.all_gather(stacked, 'tensor', axis=1, tiled=True)  168 us
    reduce_scatter x3, waiting for transfers between devices, reduce_rows(): lax.psum_scatter(term.astype(jnp.bfloat16), 'tensor', scatter_dimension=0...  145 us
    reduce_scatter x1, waiting for transfers between devices, shards(): lax.psum_scatter(term_q.astype(jnp.bfloat16), 'dp', scatter_dimension=0,...  91.4 us
    reduce_scatter x1, waiting for transfers between devices, shards(): lax.psum_scatter(term_o.astype(jnp.bfloat16), 'dp', scatter_dimension=1,...  91 us
    all_gather x5, blocking collectives, gather_rows(): return lax.all_gather(stacked, 'tensor', axis=1, tiled=True)  82.5 us
    reduce_scatter x1, waiting for transfers between devices, shards(): lax.psum_scatter(term_kv.astype(jnp.bfloat16), 'dp', scatter_dimension=0,...  77.5 us
    all_gather x1, waiting for transfers between devices, shards(): lax.all_gather(out_new[0], 'dp', axis=1, tiled=True)  66.9 us
  transfers between devices with their start and end apart: 23, of which 22 were waited for; matrix products, arithmetic and copies ran while one was open for 7% of the time, Pallas kernels for 0%

commit v1 on v0

v1 whole, which is shorter than its diff:
```python
import math

import jax
import jax.numpy as jnp
from jax import lax
from jax.sharding import PartitionSpec as P

HEAD_SIZE = 128
EPS = 1e-05
THETA = 500000.0
LR = 0.5
BF = jnp.bfloat16
F32 = jnp.float32


def mm(a, b, ca=1, cb=0):
    return lax.dot_general(a, b, (((ca,), (cb,)), ((), ())), preferred_element_type=F32)


def swap(value, axis, mask):
    pairs = [(source, source ^ mask) for source in range(lax.axis_size(axis))]
    return lax.ppermute(value, axis, pairs)


def same_core(size):
    return [list(range(c, size, 2)) for c in range(2)]


def z_exchange(value):
    size = lax.axis_size("tensor")
    return lax.all_to_all(
        value, "tensor", 0, 0, axis_index_groups=same_core(size), tiled=True
    )


def dp_exchange(value):
    return lax.all_to_all(value, "dp", 0, 0, tiled=True)


def tile_rows(value, copies):
    return jnp.broadcast_to(value[None], (copies,) + value.shape).reshape(
        (copies * value.shape[0],) + value.shape[1:]
    )


def gather_z(rows, nz):
    mine = z_exchange(tile_rows(rows, nz))
    return mine, swap(mine, "tensor", 1)


def scatter_z(part_mine, part_other, nz):
    moved = swap(part_other.astype(BF), "tensor", 1)
    pair = (part_mine + moved.astype(F32)).astype(BF)
    got = z_exchange(pair)
    return jnp.sum(got.reshape((nz, -1) + got.shape[1:]).astype(F32), axis=0)


def gather_dp(rows, n):
    return dp_exchange(tile_rows(rows, n))


def scatter_dp(part, n):
    got = dp_exchange(part)
    return jnp.sum(got.reshape((n, -1) + got.shape[1:]).astype(F32), axis=0)


def rotate(values, cosine, sine):
    half = values.shape[-1] // 2
    first = values[..., :half]
    second = values[..., half:]
    return jnp.concatenate(
        [first * cosine - second * sine, second * cosine + first * sine], axis=-1
    )


def split_pair(column):
    high = column.astype(BF)
    low = (column - high.astype(F32)).astype(BF)
    wide = jnp.zeros((column.shape[0], 126), BF)
    return jnp.concatenate([high[:, None], low[:, None], wide], axis=1)


def attention(q_raw, kv_raw, total, width, cosine, sine, visible):
    scale = lax.rsqrt(total / width + EPS)[:, None]
    tokens = q_raw.shape[0]
    heads = q_raw.shape[1] // HEAD_SIZE
    q = (q_raw * scale).reshape(tokens, heads, HEAD_SIZE)
    queries = rotate(q, cosine[:, None], sine[:, None]).astype(BF)
    kv = (kv_raw * scale).astype(BF)
    keys = rotate(kv[:, :HEAD_SIZE].astype(F32), cosine, sine).astype(BF)
    values = kv[:, HEAD_SIZE:]
    scores = jnp.einsum("qgh,kh->gqk", queries, keys, preferred_element_type=F32) / math.sqrt(
        HEAD_SIZE
    )
    scores = jnp.where(visible[None], scores, -1e30)
    weights = jnp.exp(scores)
    probs = weights / jnp.sum(weights, axis=-1, keepdims=True)
    low = probs.astype(BF)
    mixed = jnp.einsum("gqk,kh->qgh", low, values, preferred_element_type=F32)
    mixed = mixed.reshape(tokens, -1).astype(BF)
    return mixed, (q_raw, kv_raw, scale, queries, keys, values, probs, low)


def attention_back(saved, d_mixed, width, cosine, sine):
    q_raw, kv_raw, scale, queries, keys, values, probs, low = saved
    tokens = q_raw.shape[0]
    dm = d_mixed.astype(BF).reshape(queries.shape)
    d_probs = jnp.einsum("qgh,kh->gqk", dm, values, preferred_element_type=F32)
    d_values = jnp.einsum("gqk,qgh->kh", low, dm, preferred_element_type=F32)
    d_scores = probs * (d_probs - jnp.sum(probs * d_probs, axis=-1, keepdims=True))
    d_scores = (d_scores / math.sqrt(HEAD_SIZE)).astype(BF)
    d_queries = jnp.einsum("gqk,kh->qgh", d_scores, keys, preferred_element_type=F32)
    d_keys = jnp.einsum("gqk,qgh->kh", d_scores, queries, preferred_element_type=F32)
    dq = rotate(d_queries, cosine[:, None], -sine[:, None]).reshape(tokens, -1)
    dkv = jnp.concatenate([rotate(d_keys, cosine, -sine), d_values], axis=1)
    dq = (dq * scale).astype(BF)
    dkv = (dkv * scale).astype(BF)
    dot = jnp.sum(dq.astype(F32) * q_raw, axis=1) + jnp.sum(dkv.astype(F32) * kv_raw, axis=1)
    coef = dot * scale[:, 0] * scale[:, 0] / width
    return dq, dkv, coef


def shards(
    inputs,
    positions,
    out_grads,
    query_weight,
    key_value_weight,
    out_weight,
    query_stale,
    key_value_previous_gradient,
    out_stale,
):
    n_dp = lax.axis_size("dp")
    ranks = lax.axis_size("tensor")
    nz = ranks // 2
    pipe = lax.axis_index("pipe")
    rank = lax.axis_index("tensor")
    core = rank % 2
    first = pipe == 0
    micro, own, width = inputs.shape
    feats = width // n_dp
    block = own * ranks
    tokens = block * n_dp
    half = tokens // 2

    query_new = (query_weight.astype(F32) - LR * query_stale).astype(BF)
    kv_new = (key_value_weight.astype(F32) - LR * key_value_previous_gradient).astype(BF)
    out_new = (out_weight.astype(F32) - LR * out_stale).astype(BF)

    def both(own_part):
        other = swap(own_part, "pipe", 1)
        return jnp.where(first, own_part, other), jnp.where(first, other, own_part)

    wq0, wq1 = both(query_new[0])
    wo0, wo1 = both(out_new[0])
    kv_own = kv_new[0].T
    kv_side = swap(kv_own, "tensor", 1)
    kv_pair = jnp.where(
        core == 0,
        jnp.concatenate([kv_own, kv_side], axis=0),
        jnp.concatenate([kv_side, kv_own], axis=0),
    )
    kv_far = swap(kv_pair, "tensor", 2)
    even = (rank // 2) % 2 == 0
    kv_full = jnp.where(
        even,
        jnp.concatenate([kv_pair, kv_far], axis=0),
        jnp.concatenate([kv_far, kv_pair], axis=0),
    )
    wkv0, wkv1 = both(kv_full)

    b_row = lax.broadcasted_iota(jnp.int32, (tokens, tokens), 0)
    c_row = lax.broadcasted_iota(jnp.int32, (tokens, tokens), 1)

    def block_major(rel_core, chip, rest):
        return (rest // own) * block + (chip * 2 + rel_core) * own + rest % own

    rel = (c_row // half) ^ core
    inside = c_row % half
    order_c = (b_row == block_major(rel, inside // (n_dp * own), inside % (n_dp * own))).astype(BF)
    rk = c_row // (n_dp * own)
    order_r = (b_row == block_major(rk % 2, rk // 2, c_row % (n_dp * own))).astype(BF)

    spots = lax.dynamic_index_in_dim(positions, pipe, 0, keepdims=False)
    freqs = THETA ** (-2.0 * jnp.arange(HEAD_SIZE // 2, dtype=F32) / HEAD_SIZE)
    angles = spots.astype(F32)[:, None] * freqs[None, :]
    cosine = jnp.cos(angles)
    sine = jnp.sin(angles)
    index = jnp.arange(block, dtype=jnp.int32)
    visible = (index[None, :] <= index[:, None]) & (index[None, :] >= (index - spots)[:, None])

    start = jnp.stack(
        [
            lax.dynamic_index_in_dim(inputs, pipe, 0, keepdims=False),
            lax.dynamic_index_in_dim(out_grads, pipe, 0, keepdims=False),
        ]
    )
    start = start.reshape(2, own, n_dp, feats).transpose(2, 0, 1, 3).reshape(n_dp * 2 * own, feats)
    start = dp_exchange(start).reshape(n_dp, 2, own, feats)
    h0 = start[:, 0].reshape(n_dp * own, feats)
    g1 = start[:, 1].reshape(n_dp * own, feats)

    big_g1 = lax.all_gather(g1, "tensor", axis=0, tiled=True)

    def project(rows, wq, wkv):
        wide = rows.astype(F32)
        q = mm(rows, wq)
        kv = mm(rows, wkv, 1, 1)
        return jnp.concatenate(
            [q.astype(BF), kv.astype(BF), split_pair(jnp.sum(wide * wide, axis=1))], axis=1
        )

    def to_blocks(part):
        return mm(order_c, part).astype(BF)

    nq = query_new.shape[2]
    nkv = 2 * HEAD_SIZE

    def unpack(total):
        return (
            total[:, :nq],
            total[:, nq : nq + nkv],
            total[:, nq + nkv] + total[:, nq + nkv + 1],
        )

    h0_mine, h0_other = gather_z(h0, nz)
    part = jnp.concatenate([project(h0_mine, wq0, wkv0), project(h0_other, wq0, wkv0)], axis=0)
    total = scatter_dp(to_blocks(part), n_dp)
    mixed0, saved0 = attention(*unpack(total), width, cosine, sine, visible)
    all_m0 = mm(order_c, gather_dp(mixed0, n_dp), 0, 0).astype(BF)
    reduced = scatter_z(mm(all_m0[:half], wo0), mm(all_m0[half:], wo0), nz)
    h1 = (h0.astype(F32) + reduced).astype(BF)

    dm1 = mm(order_r, mm(big_g1, wo1, 1, 1).astype(BF)).astype(BF)
    h1_mine, h1_other = gather_z(h1, nz)
    part = jnp.concatenate([project(h1_mine, wq1, wkv1), project(h1_other, wq1, wkv1)], axis=0)
    total = scatter_dp(jnp.concatenate([to_blocks(part), dm1], axis=1), n_dp)
    packed = nq + nkv + 128
    mixed1, saved1 = attention(*unpack(total[:, :packed]), width, cosine, sine, visible)
    dq1, dkv1, coef1 = attention_back(saved1, total[:, packed:], width, cosine, sine)

    def back(dq, dkv, coef, extra, mine, other, wq, wkv, grad_rows):
        sent = jnp.concatenate([dq, dkv, split_pair(coef)] + extra, axis=1)
        got = gather_dp(sent, n_dp)
        rows = mm(order_c, got[:, : nq + nkv + 128], 0, 0).astype(BF)
        all_q = rows[:, :nq]
        all_kv = rows[:, nq : nq + nkv]
        c = rows[:, nq + nkv].astype(F32) + rows[:, nq + nkv + 1].astype(F32)

        def term(lo, hi, held):
            value = mm(all_q[lo:hi], wq, 1, 1) + mm(all_kv[lo:hi], wkv)
            return value - held.astype(F32) * c[lo:hi, None]

        reduced = scatter_z(term(0, half, mine), term(half, tokens, other), nz)
        grad = (grad_rows.astype(F32) + reduced).astype(BF)
        grad_q = mm(mine, all_q[:half], 0, 0) + mm(other, all_q[half:], 0, 0)
        grad_kv = mm(all_kv[:half], mine, 0, 0) + mm(all_kv[half:], other, 0, 0)
        return grad, grad_q, grad_kv, got[:, nq + nkv + 128 :]

    g0, gq1, gkv1, got_m1 = back(dq1, dkv1, coef1, [mixed1], h1_mine, h1_other, wq1, wkv1, g1)
    all_m1 = mm(order_r, got_m1, 0, 0).astype(BF)
    go1 = mm(all_m1, big_g1, 0, 0)
    out1 = lax.psum_scatter(
        mm(all_m1, wo1).astype(BF), "tensor", scatter_dimension=0, tiled=True
    )
    h2 = (h1.astype(F32) + out1.astype(F32)).astype(BF)

    g0_mine, g0_other = gather_z(g0, nz)
    dm0 = jnp.concatenate([mm(g0_mine, wo0, 1, 1), mm(g0_other, wo0, 1, 1)], axis=0).astype(BF)
    d_mixed0 = scatter_dp(mm(order_c, dm0).astype(BF), n_dp)
    dq0, dkv0, coef0 = attention_back(saved0, d_mixed0, width, cosine, sine)
    go0 = mm(all_m0[:half], g0_mine, 0, 0) + mm(all_m0[half:], g0_other, 0, 0)
    gi, gq0, gkv0, _ = back(dq0, dkv0, coef0, [], h0_mine, h0_other, wq0, wkv0, g0)

    def kv_columns(grad):
        cols = grad.shape[0] // 4
        quarters = grad.astype(BF).reshape(2, 2, cols, feats)
        keep = lax.dynamic_index_in_dim(quarters, core, 1, keepdims=False)
        send = lax.dynamic_index_in_dim(quarters, 1 - core, 1, keepdims=False)
        pair = keep.astype(F32) + swap(send, "tensor", 1).astype(F32)
        pair = pair.astype(BF)
        zz = (rank // 2) % 2
        keep = lax.dynamic_index_in_dim(pair, zz, 0, keepdims=False)
        send = lax.dynamic_index_in_dim(pair, 1 - zz, 0, keepdims=False)
        return keep.astype(F32) + swap(send, "tensor", 2).astype(F32)

    def home(grad0, grad1):
        to1 = lax.ppermute(grad1.astype(BF), "pipe", [(0, 1)])
        to0 = lax.ppermute(grad0.astype(BF), "pipe", [(1, 0)])
        return jnp.where(first, grad0 + to0.astype(F32), grad1 + to1.astype(F32))

    query_grad = home(gq0, gq1)
    kv_grad = home(kv_columns(gkv0), kv_columns(gkv1)).T
    out_grad = home(go0, go1)

    ends = jnp.stack([h1, gi, h2, g0]).reshape(4, n_dp, own, feats).transpose(1, 0, 2, 3)
    ends = dp_exchange(ends.reshape(n_dp * 4 * own, feats)).reshape(n_dp, 2, 2, own, feats)
    ends = ends.transpose(1, 2, 3, 0, 4).reshape(2, 2, own, width)
    keep = lax.dynamic_index_in_dim(ends, pipe, 0, keepdims=False)
    send = lax.dynamic_index_in_dim(ends, 1 - pipe, 0, keepdims=False)
    came = swap(send, "pipe", 1)
    rows = jnp.where(first, jnp.stack([keep, came], 1), jnp.stack([came, keep], 1))
    return (
        rows[0][None],
        rows[1][None],
        query_new,
        kv_new,
        out_new,
        query_grad[None],
        kv_grad[None],
        out_grad[None],
    )


def solution(mesh):
    placed = (
        P(None, ("dp", "tensor"), None),
        P(None, "dp"),
        P(None, ("dp", "tensor"), None),
        P("pipe", "dp", "tensor"),
        P("pipe", "dp", "tensor"),
        P("pipe", "tensor", "dp"),
        P("pipe", "dp", "tensor"),
        P("pipe", "dp", "tensor"),
        P("pipe", "tensor", "dp"),
    )
    return jax.shard_map(
        shards,
        mesh=mesh,
        in_specs=placed,
        out_specs=(
            P("pipe", None, ("dp", "tensor"), None),
            P("pipe", None, ("dp", "tensor"), None),
            P("pipe", "dp", "tensor"),
            P("pipe", "dp", "tensor"),
            P("pipe", "tensor", "dp"),
            P("pipe", "dp", "tensor"),
            P("pipe", "dp", "tensor"),
            P("pipe", "tensor", "dp"),
        ),
        check_vma=False,
    )
```

time: 1480 us -> 405 us (0.27)
  waiting for transfers between devices: 1180 us -> 116 us
  starting transfers between devices: 3.54 us -> 80.4 us
  blocking collectives: 82.5 us -> 43.8 us
  matrix products: 92.6 us -> 63.7 us
    unnamed x23 -> x2, waiting for transfers between devices: 425 us -> 0.03 us
    reduce_scatter x6 -> x1, waiting for transfers between devices: 405 us -> 0.01 us  [shards(): lax.psum_scatter(mm(all_m1, wo1).astype(BF), 'tensor', scatter_dimension=...]
    all_gather x9 -> x1, waiting for transfers between devices: 344 us -> 6.74 us  [shards(): big_g1 = lax.all_gather(g1, 'tensor', axis=0, tiled=True)]
    all_to_all x0 -> x12, waiting for transfers between devices: none -> 85.5 us  [the longest x7 53.2 us: dp_exchange(): return lax.all_to_all(value, 'dp', 0, 0, tiled=True)]
    all_gather x5 -> x0, blocking collectives: 82.5 us -> none  [gather_rows(): return lax.all_gather(stacked, 'tensor', axis=1, tiled=True)]
    all_to_all x0 -> x12, starting transfers between devices: none -> 56.1 us  [the longest x7 31.7 us: dp_exchange(): return lax.all_to_all(value, 'dp', 0, 0, tiled=True)]
    all_to_all x0 -> x2, blocking collectives: none -> 43.8 us  [the longest x1 24.6 us: z_exchange(): lax.all_to_all(value, 'tensor', 0, 0, axis_index_groups=same_core(size),...]
    dot_general x49 -> x50, matrix products: 92.6 us -> 61.8 us  [the longest x40 47.1 us: mm(): lax.dot_general(a, b, (((ca,), (cb,)), ((), ())), preferred_element_type=...]
  transfers between devices with their start and end apart: 23 -> 36, of which waited for: 22 -> 17; matrix products, arithmetic and copies ran while one was open for 7% -> 24% of each run, Pallas kernels for 0% -> 0%
where the time goes in v1:
time: 405 us; the launch traced here: 401 us
  waiting for transfers between devices  116 us (29%)
  starting transfers between devices  80.4 us (20%)
  matrix products  63.7 us (16%)
  blocking collectives  43.8 us (11%)
  other arithmetic  40.9 us (10%)
  local copies, waits for them, and re-layouts  40.4 us (10%)
  between operations  15.7 us (4%)
    all_to_all x7, waiting for transfers between devices, dp_exchange(): return lax.all_to_all(value, 'dp', 0, 0, tiled=True)  53.2 us
    dot_general x40, matrix products, mm(): lax.dot_general(a, b, (((ca,), (cb,)), ((), ())), preferred_element_type=...  47.1 us
    all_to_all x5, waiting for transfers between devices, z_exchange(): lax.all_to_all(value, 'tensor', 0, 0, axis_index_groups=same_core(size),...  32.3 us
    all_to_all x7, starting transfers between devices, dp_exchange(): return lax.all_to_all(value, 'dp', 0, 0, tiled=True)  31.7 us
    all_to_all x1, blocking collectives, z_exchange(): lax.all_to_all(value, 'tensor', 0, 0, axis_index_groups=same_core(size),...  24.6 us
    all_to_all x5, starting transfers between devices, z_exchange(): lax.all_to_all(value, 'tensor', 0, 0, axis_index_groups=same_core(size),...  24.4 us
    ppermute x16, waiting for transfers between devices, swap(): return lax.ppermute(value, axis, pairs)  23.6 us
    all_to_all x1, blocking collectives, dp_exchange(): return lax.all_to_all(value, 'dp', 0, 0, tiled=True)  19.2 us
  transfers between devices with their start and end apart: 36, of which 17 were waited for; matrix products, arithmetic and copies ran while one was open for 24% of the time, Pallas kernels for 0%

profile of v1, /device:TPU:8, one launch (start us, length us, event | category | flops | bytes accessed | tf_op | source)
XLA Modules:
  0.0 400.9 jit_solution(15321856016375586172)
XLA Ops:
  10.2 6.0 %all-to-all-start = ((bf16[8,8,1024]{2,1,0:T(8,128)(2,1)}), bf16[8,8,1024]{2,1,0:T(8,128)(2,1)S(1)}, u32[]{:S(2)}, u32[]{:S(2)}) async-start(bf16[8,8,1024]{2,1,0:T(8,128)(2,1)} %all_to_all.84), calls=%async_computation | async-start | bytes 262144 | tf_op jit(solution)/shard_map/all_to_all | solution.py:37
  16.3 2.0 collective-permute-start.2
  19.9 4.5 %all-to-all-done = bf16[8,8,1024]{2,1,0:T(8,128)(2,1)S(1)} async-done(((bf16[8,8,1024]{2,1,0:T(8,128)(2,1)}), bf16[8,8,1024]{2,1,0:T(8,128)(2,1)S(1)}, u32[]{:S(2)}, u32[]{:S(2)}) %all-to-all-start) | async-done | bytes 131104 | tf_op jit(solution)/shard_map/all_to_all | solution.py:37
  26.1 8.5 %all-to-all-start.1 = ((bf16[8,32,1024]{2,1,0:T(8,128)(2,1)}), bf16[8,32,1024]{2,1,0:T(8,128)(2,1)S(1)}, u32[]{:S(2)}, u32[]{:S(2)}) async-start(bf16[8,32,1024]{2,1,0:T(8,128)(2,1)} %broadcast_in_dim.37), calls=%async_computation.1 | async-start | bytes 1048576 | tf_op jit(solution)/shard_map/all_to_all | solution.py:31
  37.1 10.1 %collective-permute-done.3 = bf16[256,1024]{1,0:T(8,128)(2,1)S(1)} collective-permute-done((bf16[256,1024]{1,0:T(8,128)(2,1)S(1)}, bf16[256,1024]{1,0:T(8,128)(2,1)S(1)}, u32[]{:S(2)}, u32[]{:S(2)}) %collective-permute-start.3) | collective-permute-done | bytes 524320 | tf_op jit(solution)/shard_map/ppermute | solution.py:22
  48.1 3.0 all-to-all-done.1
  55.8 4.3 %all-to-all-start.2 = ((bf16[8,64,640]{2,1,0:T(8,128)(2,1)}), bf16[8,64,640]{2,1,0:T(8,128)(2,1)}, u32[]{:S(2)}, u32[]{:S(2)}) async-start(bf16[8,64,640]{2,1,0:T(8,128)(2,1)} %bitcast.9), calls=%async_computation.2 | async-start | bytes 1310720 | tf_op jit(solution)/shard_map/all_to_all | solution.py:37
  63.1 10.7 %all-to-all-done.2 = bf16[8,64,640]{2,1,0:T(8,128)(2,1)} async-done(((bf16[8,64,640]{2,1,0:T(8,128)(2,1)}), bf16[8,64,640]{2,1,0:T(8,128)(2,1)}, u32[]{:S(2)}, u32[]{:S(2)}) %all-to-all-start.2) | async-done | bytes 655392 | tf_op jit(solution)/shard_map/all_to_all | solution.py:37
  78.5 4.1 %all-to-all-start.3 = ((bf16[8,64,256]{2,1,0:T(8,128)(2,1)}), bf16[8,64,256]{2,1,0:T(8,128)(2,1)}, u32[]{:S(2)}, u32[]{:S(2)}) async-start(bf16[8,64,256]{2,1,0:T(8,128)(2,1)} %broadcast_in_dim.40), calls=%async_computation.3 | async-start | bytes 524288 | tf_op jit(solution)/shard_map/all_to_all | solution.py:37
  83.8 7.7 %all-to-all-done.3 = bf16[8,64,256]{2,1,0:T(8,128)(2,1)} async-done(((bf16[8,64,256]{2,1,0:T(8,128)(2,1)}), bf16[8,64,256]{2,1,0:T(8,128)(2,1)}, u32[]{:S(2)}, u32[]{:S(2)}) %all-to-all-start.3) | async-done | bytes 262176 | tf_op jit(solution)/shard_map/all_to_all | solution.py:37
  97.7 24.6 %all_to_all.126 = bf16[8,32,1024]{2,1,0:T(8,128)(2,1)S(1)} all-to-all(bf16[8,32,1024]{2,1,0:T(8,128)(2,1)S(1)} %bitcast.287), channel_id=1, replica_groups={{0,2,4,6,8,10,12,14},{1,3,5,7,9,11,13,15},{16,18,20,22,24,26,28,30},{17..., dimensions={0} | all-to-all | bytes 1048576 | tf_op jit(solution)/shard_map/all_to_all | solution.py:31
  123.3 3.5 all-to-all-start.5
  126.9 6.7 %all-gather.2.cloned.1.call-done = bf16[512,1024]{1,0:T(8,128)(2,1)} async-done(((bf16[32,1024]{1,0:T(8,128)(2,1)}), bf16[512,1024]{1,0:T(8,128)(2,1)}) %all-gather.2.cloned.1.call-update) | async-done | bytes 1048592 | tf_op jit(solution)/shard_map/all_gather | solution.py:204
  133.7 2.8 convolution_convert_fusion.8
  136.6 8.1 %all-to-all-done.5 = bf16[8,32,1024]{2,1,0:T(8,128)(2,1)S(1)} async-done(((bf16[8,32,1024]{2,1,0:T(8,128)(2,1)}), bf16[8,32,1024]{2,1,0:T(8,128)(2,1)S(1)}, u32[]{:S(2)}, u32[]{:S(2)}) %all-to-all-start.5) | async-done | bytes 524320 | tf_op jit(solution)/shard_map/all_to_all | solution.py:31
  147.4 4.3 %concatenate.81 = bf16[256,640]{0,1:T(8,128)(2,1)} concatenate(bf16[256,256]{0,1:T(8,128)(2,1)S(1)} %convolution_convert_fusion.16, bf16[256,256]{0,1:T(8,128)(2,1)} %convolution_convert_fusion.15, bf16[256,1]{0,1:T(2,128)(2,1)S(1)} %get-tuple-element.71, bf16[256,1]{0,1:T(2,128)(2,1)S(1)} %get-tuple-element.70, bf16[256,126]{0,1:T(8,128)(2,1)S(1)} %broadcast.240), dimensions={1} | concatenate | bytes 655360 | tf_op jit(solution)/shard_map/concatenate | solution.py:210
  154.3 4.2 %concatenate.82 = bf16[256,640]{0,1:T(8,128)(2,1)} concatenate(bf16[256,256]{0,1:T(8,128)(2,1)S(1)} %convolution_convert_fusion.14, bf16[256,256]{0,1:T(8,128)(2,1)} %convolution_convert_fusion.13, bf16[256,1]{0,1:T(2,128)(2,1)S(1)} %convert_element_type.644, bf16[256,1]{0,1:T(2,128)(2,1)S(1)} %subtract_convert_fusion.5, bf16[256,126]{0,1:T(8,128)(2,1)S(1)} %broadcast.240), dimensions={1} | concatenate | bytes 655360 | tf_op jit(solution)/shard_map/concatenate | solution.py:210
  160.5 19.2 %all_to_all.127 = bf16[8,64,896]{2,1,0:T(8,128)(2,1)S(1)} all-to-all(bf16[8,64,896]{2,1,0:T(8,128)(2,1)S(1)} %bitcast.281), channel_id=1, replica_groups=mesh['dp'=8,'pipe'=2,'tensor'=16] {'dp'}, dimensions={0} | all-to-all | bytes 1835008 | tf_op jit(solution)/shard_map/all_to_all | solution.py:37
  205.7 4.2 %all-to-all-start.7 = ((bf16[8,64,896]{2,1,0:T(8,128)(2,1)}), bf16[8,64,896]{2,1,0:T(8,128)(2,1)}, u32[]{:S(2)}, u32[]{:S(2)}) async-start(bf16[8,64,896]{2,1,0:T(8,128)(2,1)} %broadcast_in_dim.42), calls=%async_computation.7 | async-start | bytes 1835008 | tf_op jit(solution)/shard_map/all_to_all | solution.py:37
  210.7 14.9 %all-to-all-done.7 = bf16[8,64,896]{2,1,0:T(8,128)(2,1)} async-done(((bf16[8,64,896]{2,1,0:T(8,128)(2,1)}), bf16[8,64,896]{2,1,0:T(8,128)(2,1)}, u32[]{:S(2)}, u32[]{:S(2)}) %all-to-all-start.7) | async-done | bytes 917536 | tf_op jit(solution)/shard_map/all_to_all | solution.py:37
  232.5 4.1 %all-to-all-start.8 = ((bf16[8,32,1024]{2,1,0:T(8,128)(2,1)}), bf16[8,32,1024]{2,1,0:T(8,128)(2,1)}, u32[]{:S(2)}, u32[]{:S(2)}) async-start(bf16[8,32,1024]{2,1,0:T(8,128)(2,1)} %bitcast.288), calls=%async_computation.8 | async-start | bytes 1048576 | tf_op jit(solution)/shard_map/all_to_all | solution.py:31
  236.7 2.5 convolution_convert_fusion
  240.5 2.4 fusion.239
  244.2 2.3 fusion.106
  246.5 8.5 %all-to-all-done.8 = bf16[8,32,1024]{2,1,0:T(8,128)(2,1)} async-done(((bf16[8,32,1024]{2,1,0:T(8,128)(2,1)}), bf16[8,32,1024]{2,1,0:T(8,128)(2,1)}, u32[]{:S(2)}, u32[]{:S(2)}) %all-to-all-start.8) | async-done | bytes 524320 | tf_op jit(solution)/shard_map/all_to_all | solution.py:31
  257.8 4.2 %all-to-all-start.9 = ((bf16[8,32,1024]{2,1,0:T(8,128)(2,1)}), bf16[8,32,1024]{2,1,0:T(8,128)(2,1)}, u32[]{:S(2)}, u32[]{:S(2)}) async-start(bf16[8,32,1024]{2,1,0:T(8,128)(2,1)} %broadcast_in_dim.43), calls=%async_computation.9 | async-start | bytes 1048576 | tf_op jit(solution)/shard_map/all_to_all | solution.py:31
  267.0 12.6 %all-to-all-done.9 = bf16[8,32,1024]{2,1,0:T(8,128)(2,1)} async-done(((bf16[8,32,1024]{2,1,0:T(8,128)(2,1)}), bf16[8,32,1024]{2,1,0:T(8,128)(2,1)}, u32[]{:S(2)}, u32[]{:S(2)}) %all-to-all-start.9) | async-done | bytes 524320 | tf_op jit(solution)/shard_map/all_to_all | solution.py:31
  280.3 2.1 collective-permute-start.18
  283.9 2.4 fusion.115
  287.7 4.1 %all-to-all-start.10 = ((bf16[8,64,256]{2,1,0:T(8,128)(2,1)}), bf16[8,64,256]{2,1,0:T(8,128)(2,1)}, u32[]{:S(2)}, u32[]{:S(2)}) async-start(bf16[8,64,256]{2,1,0:T(8,128)(2,1)} %bitcast.36), calls=%async_computation.10 | async-start | bytes 524288 | tf_op jit(solution)/shard_map/all_to_all | solution.py:37
  291.8 2.6 fusion.242
  294.3 3.2 collective-permute-start.20
  297.5 3.8 all-to-all-done.10
  307.9 1.8 convolution_bitcast_fusion
  319.0 1.8 broadcast_in_dim.44
  320.8 4.2 %all-to-all-start.11 = ((bf16[8,64,640]{2,1,0:T(8,128)(2,1)}), bf16[8,64,640]{2,1,0:T(8,128)(2,1)}, u32[]{:S(2)}, u32[]{:S(2)}) async-start(bf16[8,64,640]{2,1,0:T(8,128)(2,1)} %broadcast_in_dim.44), calls=%async_computation.11 | async-start | bytes 1310720 | tf_op jit(solution)/shard_map/all_to_all | solution.py:37
  330.3 2.8 select_bitcast_fusion
  333.0 5.1 %all-to-all-done.11 = bf16[8,64,640]{2,1,0:T(8,128)(2,1)} async-done(((bf16[8,64,640]{2,1,0:T(8,128)(2,1)}), bf16[8,64,640]{2,1,0:T(8,128)(2,1)}, u32[]{:S(2)}, u32[]{:S(2)}) %all-to-all-start.11) | async-done | bytes 655392 | tf_op jit(solution)/shard_map/all_to_all | solution.py:37
  344.4 4.2 %all-to-all-start.12 = ((bf16[8,32,1024]{2,1,0:T(8,128)(2,1)}), bf16[8,32,1024]{2,1,0:T(8,128)(2,1)}, u32[]{:S(2)}, u32[]{:S(2)}) async-start(bf16[8,32,1024]{2,1,0:T(8,128)(2,1)} %bitcast.43), calls=%async_computation.12 | async-start | bytes 1048576 | tf_op jit(solution)/shard_map/all_to_all | solution.py:31
  350.0 2.0 collective-permute-start.15
  353.1 2.6 collective-permute-start.12
  355.7 9.7 %collective-permute-done.15 = bf16[64,1024]{1,0:T(8,128)(2,1)S(1)} collective-permute-done((bf16[64,1024]{1,0:T(8,128)(2,1)S(1)}, bf16[64,1024]{1,0:T(8,128)(2,1)S(1)}, u32[]{:S(2)}, u32[]{:S(2)}) %collective-permute-start.15) | collective-permute-done | bytes 131104 | tf_op jit(solution)/shard_map/ppermute | solution.py:22
  366.1 3.1 collective-permute-start.16
  374.0 4.8 %all-to-all-start.13 = ((bf16[8,16,1024]{2,1,0:T(8,128)(2,1)}), bf16[8,16,1024]{2,1,0:T(8,128)(2,1)S(1)}, u32[]{:S(2)}, u32[]{:S(2)}) async-start(bf16[8,16,1024]{2,1,0:T(8,128)(2,1)} %copy.269), calls=%async_computation.14 | async-start | bytes 524288 | tf_op jit(solution)/shard_map/all_to_all | solution.py:37
  378.8 2.2 select_bitcast_fusion.1
  381.0 6.6 %all-to-all-done.13 = bf16[8,16,1024]{2,1,0:T(8,128)(2,1)S(1)} async-done(((bf16[8,16,1024]{2,1,0:T(8,128)(2,1)}), bf16[8,16,1024]{2,1,0:T(8,128)(2,1)S(1)}, u32[]{:S(2)}, u32[]{:S(2)}) %all-to-all-start.13) | async-done | bytes 262176 | tf_op jit(solution)/shard_map/all_to_all | solution.py:37
  388.1 1.8 select_bitcast_fusion.2
  390.0 3.1 collective-permute-done.11
  (384 shorter events, 121.2 us)
Async XLA Ops:
  8.2 8.0 %collective-permute-start.1 = (bf16[64,1024]{1,0:T(8,128)(2,1)S(1)}, bf16[64,1024]{1,0:T(8,128)(2,1)S(1)}, u32[]{:S(2)}, u32[]{:S(2)}) collective-permute-start(bf16[64,1024]{1,0:T(8,128)(2,1)S(1)} %bitcast.293), channel_id=1, source_target_pairs={{0,1},{1,0},{2,3},{3,2},{4,5},{5,4},{6,7},{7,6},{8,9},{9,8},{10,11... | collective-permute-start | bytes 393224 | tf_op jit(solution)/shard_map/ppermute | solution.py:22
  10.2 14.2 %all-to-all-start = ((bf16[8,8,1024]{2,1,0:T(8,128)(2,1)}), bf16[8,8,1024]{2,1,0:T(8,128)(2,1)S(1)}, u32[]{:S(2)}, u32[]{:S(2)}) async-start(bf16[8,8,1024]{2,1,0:T(8,128)(2,1)} %all_to_all.84), calls=%async_computation | async-start | bytes 262144 | tf_op jit(solution)/shard_map/all_to_all | solution.py:37
  16.3 18.2 %collective-permute-start.2 = (bf16[128,1024]{1,0:T(8,128)(2,1)S(1)}, bf16[128,1024]{1,0:T(8,128)(2,1)S(1)}, u32[]{:S(2)}, u32[]{:S(2)}) collective-permute-start(bf16[128,1024]{1,0:T(8,128)(2,1)S(1)} %maximum_select_fusion.1), channel_id=1, source_target_pairs={{0,2},{1,3},{2,0},{3,1},{4,6},{5,7},{6,4},{7,5},{8,10},{9,11},{10,... | collective-permute-start | bytes 786440 | tf_op jit(solution)/shard_map/ppermute | solution.py:22
  18.5 17.7 %collective-permute-start = (bf16[1024,256]{1,0:T(8,128)(2,1)S(1)}, bf16[1024,256]{1,0:T(8,128)(2,1)S(1)}, u32[]{:S(2)}, u32[]{:S(2)}) collective-permute-start(bf16[1024,256]{1,0:T(8,128)(2,1)S(1)} %bitcast.286), channel_id=1, source_target_pairs={{0,16},{16,0},{1,17},{17,1},{2,18},{18,2},{3,19},{19,3},{4,20},{20... | collective-permute-start | bytes 1572872 | tf_op jit(solution)/shard_map/ppermute | solution.py:22
  26.1 25.0 %all-to-all-start.1 = ((bf16[8,32,1024]{2,1,0:T(8,128)(2,1)}), bf16[8,32,1024]{2,1,0:T(8,128)(2,1)S(1)}, u32[]{:S(2)}, u32[]{:S(2)}) async-start(bf16[8,32,1024]{2,1,0:T(8,128)(2,1)} %broadcast_in_dim.37), calls=%async_computation.1 | async-start | bytes 1048576 | tf_op jit(solution)/shard_map/all_to_all | solution.py:31
  34.7 12.6 %collective-permute-start.3 = (bf16[256,1024]{1,0:T(8,128)(2,1)S(1)}, bf16[256,1024]{1,0:T(8,128)(2,1)S(1)}, u32[]{:S(2)}, u32[]{:S(2)}) collective-permute-start(bf16[256,1024]{1,0:T(8,128)(2,1)S(1)} %maximum_select_fusion), channel_id=1, source_target_pairs={{0,16},{16,0},{1,17},{17,1},{2,18},{18,2},{3,19},{19,3},{4,20},{20... | collective-permute-start | bytes 1572872 | tf_op jit(solution)/shard_map/ppermute | solution.py:22
  36.2 122.4 %copy-start.48 = (s32[512]{0:T(512)}, s32[512]{0:T(512)S(1)}, u32[]{:S(2)}) copy-start(s32[512]{0:T(512)S(1)} %get-tuple-element.88) | copy-start | bytes 6148
  36.2 122.4 %copy-start.52 = (s32[512]{0:T(512)}, s32[512]{0:T(512)S(1)}, u32[]{:S(2)}) copy-start(s32[512]{0:T(512)S(1)} %get-tuple-element.89) | copy-start | bytes 6148
  36.2 122.4 %copy-start.56 = (s32[512]{0:T(512)}, s32[512]{0:T(512)S(1)}, u32[]{:S(2)}) copy-start(s32[512]{0:T(512)S(1)} %get-tuple-element.90) | copy-start | bytes 6148
  36.2 122.4 %copy-start.60 = (s32[512]{0:T(512)}, s32[512]{0:T(512)S(1)}, u32[]{:S(2)}) copy-start(s32[512]{0:T(512)S(1)} %get-tuple-element.91) | copy-start | bytes 6148
  51.1 1.9 collective-permute-start.4
  55.8 18.0 %all-to-all-start.2 = ((bf16[8,64,640]{2,1,0:T(8,128)(2,1)}), bf16[8,64,640]{2,1,0:T(8,128)(2,1)}, u32[]{:S(2)}, u32[]{:S(2)}) async-start(bf16[8,64,640]{2,1,0:T(8,128)(2,1)} %bitcast.9), calls=%async_computation.2 | async-start | bytes 1310720 | tf_op jit(solution)/shard_map/all_to_all | solution.py:37
  61.5 72.2 %copy-start.6 = (bf16[1,256,1024]{2,1,0:T(8,128)(2,1)}, bf16[1,256,1024]{2,1,0:T(8,128)(2,1)S(1)}, u32[]{:S(2)}) copy-start(bf16[1,256,1024]{2,1,0:T(8,128)(2,1)S(1)} %subtract_convert_fusion) | copy-start | bytes 1572868
  61.5 21.1 %collective-permute-start.5 = (bf16[256,1024]{1,0:T(8,128)(2,1)S(1)}, bf16[256,1024]{1,0:T(8,128)(2,1)}, u32[]{:S(2)}, u32[]{:S(2)}) collective-permute-start(bf16[256,1024]{1,0:T(8,128)(2,1)S(1)} %bitcast.280), channel_id=1, source_target_pairs={{0,16},{16,0},{1,17},{17,1},{2,18},{18,2},{3,19},{19,3},{4,20},{20... | collective-permute-start | bytes 1572872 | tf_op jit(solution)/shard_map/ppermute | solution.py:22
  76.6 122.9 %copy-start.20 = (f32[64,64]{1,0:T(8,128)}, f32[64,64]{1,0:T(8,128)S(1)}, u32[]{:S(2)}) copy-start(f32[64,64]{1,0:T(8,128)S(1)} %get-tuple-element.69) | copy-start | bytes 49156
  78.5 13.0 %all-to-all-start.3 = ((bf16[8,64,256]{2,1,0:T(8,128)(2,1)}), bf16[8,64,256]{2,1,0:T(8,128)(2,1)}, u32[]{:S(2)}, u32[]{:S(2)}) async-start(bf16[8,64,256]{2,1,0:T(8,128)(2,1)} %broadcast_in_dim.40), calls=%async_computation.3 | async-start | bytes 524288 | tf_op jit(solution)/shard_map/all_to_all | solution.py:37
  82.6 51.1 %all-gather.2.cloned.1.call-start = ((), (), s32[]{:S(2)}) async-start(), calls=%async_computation.15 | async-start | bytes 1114112 | tf_op jit(solution)/shard_map/all_gather | solution.py:204
  94.1 2.3 collective-permute-start.6
  97.7 24.7 %copy-start.23 = (bf16[32,1024]{1,0:T(8,128)(2,1)S(1)}, bf16[32,1024]{1,0:T(8,128)(2,1)}, u32[]{:S(2)}) copy-start(bf16[32,1024]{1,0:T(8,128)(2,1)} %copy-done.22) | copy-start | bytes 196612
  123.3 21.4 %all-to-all-start.5 = ((bf16[8,32,1024]{2,1,0:T(8,128)(2,1)}), bf16[8,32,1024]{2,1,0:T(8,128)(2,1)S(1)}, u32[]{:S(2)}, u32[]{:S(2)}) async-start(bf16[8,32,1024]{2,1,0:T(8,128)(2,1)} %broadcast_in_dim.41), calls=%async_computation.5 | async-start | bytes 1048576 | tf_op jit(solution)/shard_map/all_to_all | solution.py:31
  144.7 7.0 %collective-permute-start.7 = (bf16[256,1024]{1,0:T(8,128)(2,1)S(1)}, bf16[256,1024]{1,0:T(8,128)(2,1)S(1)}, u32[]{:S(2)}, u32[]{:S(2)}) collective-permute-start(bf16[256,1024]{1,0:T(8,128)(2,1)S(1)} %bitcast.274), channel_id=1, source_target_pairs={{0,1},{1,0},{2,3},{3,2},{4,5},{5,4},{6,7},{7,6},{8,9},{9,8},{10,11... | collective-permute-start | bytes 1572872 | tf_op jit(solution)/shard_map/ppermute | solution.py:22
  205.7 19.9 %copy-start.53 = (s32[512]{0:T(512)S(1)}, s32[512]{0:T(512)}, u32[]{:S(2)}) copy-start(s32[512]{0:T(512)} %copy-done.52) | copy-start | bytes 6148
  205.7 19.9 %copy-start.57 = (s32[512]{0:T(512)S(1)}, s32[512]{0:T(512)}, u32[]{:S(2)}) copy-start(s32[512]{0:T(512)} %copy-done.56) | copy-start | bytes 6148
  205.7 19.9 %copy-start.61 = (s32[512]{0:T(512)S(1)}, s32[512]{0:T(512)}, u32[]{:S(2)}) copy-start(s32[512]{0:T(512)} %copy-done.60) | copy-start | bytes 6148
  205.7 19.9 %copy-start.76 = (pred[512]{0:T(512)(128)(4,1)S(1)}, pred[512]{0:T(512)(128)(4,1)}, u32[]{:S(2)}) copy-start(pred[512]{0:T(512)(128)(4,1)} %copy-done.73) | copy-start | bytes 1540
  205.7 19.9 %copy-start.82 = (pred[512]{0:T(512)(128)(4,1)S(1)}, pred[512]{0:T(512)(128)(4,1)}, u32[]{:S(2)}) copy-start(pred[512]{0:T(512)(128)(4,1)} %copy-done.79) | copy-start | bytes 1540
  205.7 19.9 %all-to-all-start.7 = ((bf16[8,64,896]{2,1,0:T(8,128)(2,1)}), bf16[8,64,896]{2,1,0:T(8,128)(2,1)}, u32[]{:S(2)}, u32[]{:S(2)}) async-start(bf16[8,64,896]{2,1,0:T(8,128)(2,1)} %broadcast_in_dim.42), calls=%async_computation.7 | async-start | bytes 1835008 | tf_op jit(solution)/shard_map/all_to_all | solution.py:37
  229.2 2.1 collective-permute-start.8
  232.5 22.4 %all-to-all-start.8 = ((bf16[8,32,1024]{2,1,0:T(8,128)(2,1)}), bf16[8,32,1024]{2,1,0:T(8,128)(2,1)}, u32[]{:S(2)}, u32[]{:S(2)}) async-start(bf16[8,32,1024]{2,1,0:T(8,128)(2,1)} %bitcast.288), calls=%async_computation.8 | async-start | bytes 1048576 | tf_op jit(solution)/shard_map/all_to_all | solution.py:31
  236.7 91.9 %reduce-scatter.2.cloned.1.call-start = ((), (), s32[]{:S(2)}) async-start(), calls=%async_computation.16 | async-start | bytes 1114112 | tf_op jit(solution)/shard_map/reduce_scatter | solution.py:264
  242.9 135.8 %collective-permute-start.13 = (bf16[1024,256]{1,0:T(8,128)(2,1)}, bf16[1024,256]{1,0:T(8,128)(2,1)}, u32[]{:S(2)}, u32[]{:S(2)}) collective-permute-start(bf16[1024,256]{1,0:T(8,128)(2,1)} %get-tuple-element.74), channel_id=1, source_target_pairs={{0,16},{1,17},{2,18},{3,19},{4,20},{5,21},{6,22},{7,23},{8,24},{9,... | collective-permute-start | bytes 1572872 | tf_op jit(solution)/shard_map/ppermute | solution.py:289
  257.8 21.8 %all-to-all-start.9 = ((bf16[8,32,1024]{2,1,0:T(8,128)(2,1)}), bf16[8,32,1024]{2,1,0:T(8,128)(2,1)}, u32[]{:S(2)}, u32[]{:S(2)}) async-start(bf16[8,32,1024]{2,1,0:T(8,128)(2,1)} %broadcast_in_dim.43), calls=%async_computation.9 | async-start | bytes 1048576 | tf_op jit(solution)/shard_map/all_to_all | solution.py:31
  263.7 3.2 collective-permute-start.17
  265.5 64.7 %collective-permute-start.21 = (bf16[256,1024]{1,0:T(8,128)(2,1)}, bf16[256,1024]{1,0:T(8,128)(2,1)}, u32[]{:S(2)}, u32[]{:S(2)}) collective-permute-start(bf16[256,1024]{1,0:T(8,128)(2,1)} %get-tuple-element.78), channel_id=1, source_target_pairs={{0,16},{1,17},{2,18},{3,19},{4,20},{5,21},{6,22},{7,23},{8,24},{9,... | collective-permute-start | bytes 1572872 | tf_op jit(solution)/shard_map/ppermute | solution.py:289
  279.7 6.6 %collective-permute-start.9 = (bf16[256,1024]{1,0:T(8,128)(2,1)}, bf16[256,1024]{1,0:T(8,128)(2,1)S(1)}, u32[]{:S(2)}, u32[]{:S(2)}) collective-permute-start(bf16[256,1024]{1,0:T(8,128)(2,1)} %bitcast.35), channel_id=1, source_target_pairs={{0,1},{1,0},{2,3},{3,2},{4,5},{5,4},{6,7},{7,6},{8,9},{9,8},{10,11... | collective-permute-start | bytes 1572872 | tf_op jit(solution)/shard_map/ppermute | solution.py:22
  280.3 44.7 %collective-permute-start.18 = (bf16[64,1024]{1,0:T(8,128)(2,1)}, bf16[64,1024]{1,0:T(8,128)(2,1)}, u32[]{:S(2)}, u32[]{:S(2)}) collective-permute-start(bf16[64,1024]{1,0:T(8,128)(2,1)} %dynamic-slice_bitcast_fusion.2), channel_id=1, source_target_pairs={{0,2},{1,3},{2,0},{3,1},{4,6},{5,7},{6,4},{7,5},{8,10},{9,11},{10,... | collective-permute-start | bytes 393224 | tf_op jit(solution)/shard_map/ppermute | solution.py:22
  287.7 13.6 %all-to-all-start.10 = ((bf16[8,64,256]{2,1,0:T(8,128)(2,1)}), bf16[8,64,256]{2,1,0:T(8,128)(2,1)}, u32[]{:S(2)}, u32[]{:S(2)}) async-start(bf16[8,64,256]{2,1,0:T(8,128)(2,1)} %bitcast.36), calls=%async_computation.10 | async-start | bytes 524288 | tf_op jit(solution)/shard_map/all_to_all | solution.py:37
  294.3 35.9 %collective-permute-start.20 = (bf16[256,1024]{1,0:T(8,128)(2,1)}, bf16[256,1024]{1,0:T(8,128)(2,1)}, u32[]{:S(2)}, u32[]{:S(2)}) collective-permute-start(bf16[256,1024]{1,0:T(8,128)(2,1)} %get-tuple-element.80), channel_id=1, source_target_pairs={{16,0},{17,1},{18,2},{19,3},{20,4},{21,5},{22,6},{23,7},{24,8},{25... | collective-permute-start | bytes 1572872 | tf_op jit(solution)/shard_map/ppermute | solution.py:290
  320.8 17.3 %all-to-all-start.11 = ((bf16[8,64,640]{2,1,0:T(8,128)(2,1)}), bf16[8,64,640]{2,1,0:T(8,128)(2,1)}, u32[]{:S(2)}, u32[]{:S(2)}) async-start(bf16[8,64,640]{2,1,0:T(8,128)(2,1)} %broadcast_in_dim.44), calls=%async_computation.11 | async-start | bytes 1310720 | tf_op jit(solution)/shard_map/all_to_all | solution.py:37
  326.6 61.4 %collective-permute-start.19 = (bf16[64,1024]{1,0:T(8,128)(2,1)}, bf16[64,1024]{1,0:T(8,128)(2,1)}, u32[]{:S(2)}, u32[]{:S(2)}) collective-permute-start(bf16[64,1024]{1,0:T(8,128)(2,1)} %fusion.77), channel_id=1, source_target_pairs={{0,16},{1,17},{2,18},{3,19},{4,20},{5,21},{6,22},{7,23},{8,24},{9,... | collective-permute-start | bytes 393224 | tf_op jit(solution)/shard_map/ppermute | solution.py:289
  341.2 2.0 collective-permute-start.10
  342.3 6.6 %collective-permute-start.14 = (bf16[2,64,1024]{2,1,0:T(8,128)(2,1)}, bf16[2,64,1024]{2,1,0:T(8,128)(2,1)}, u32[]{:S(2)}, u32[]{:S(2)}) collective-permute-start(bf16[2,64,1024]{2,1,0:T(8,128)(2,1)} %dynamic-slice_bitcast_fusion.1), channel_id=1, source_target_pairs={{0,1},{1,0},{2,3},{3,2},{4,5},{5,4},{6,7},{7,6},{8,9},{9,8},{10,11... | collective-permute-start | bytes 786440 | tf_op jit(solution)/shard_map/ppermute | solution.py:22
  344.4 24.8 %all-to-all-start.12 = ((bf16[8,32,1024]{2,1,0:T(8,128)(2,1)}), bf16[8,32,1024]{2,1,0:T(8,128)(2,1)}, u32[]{:S(2)}, u32[]{:S(2)}) async-start(bf16[8,32,1024]{2,1,0:T(8,128)(2,1)} %bitcast.43), calls=%async_computation.12 | async-start | bytes 1048576 | tf_op jit(solution)/shard_map/all_to_all | solution.py:31
  350.0 15.4 %collective-permute-start.15 = (bf16[64,1024]{1,0:T(8,128)(2,1)S(1)}, bf16[64,1024]{1,0:T(8,128)(2,1)S(1)}, u32[]{:S(2)}, u32[]{:S(2)}) collective-permute-start(bf16[64,1024]{1,0:T(8,128)(2,1)S(1)} %dynamic-slice_bitcast_fusion.3), channel_id=1, source_target_pairs={{0,2},{1,3},{2,0},{3,1},{4,6},{5,7},{6,4},{7,5},{8,10},{9,11},{10,... | collective-permute-start | bytes 393224 | tf_op jit(solution)/shard_map/ppermute | solution.py:22
  353.1 25.6 %collective-permute-start.12 = (bf16[1024,256]{1,0:T(8,128)(2,1)}, bf16[1024,256]{1,0:T(8,128)(2,1)S(1)}, u32[]{:S(2)}, u32[]{:S(2)}) collective-permute-start(bf16[1024,256]{1,0:T(8,128)(2,1)} %get-tuple-element.76), channel_id=1, source_target_pairs={{16,0},{17,1},{18,2},{19,3},{20,4},{21,5},{22,6},{23,7},{24,8},{25... | collective-permute-start | bytes 1572872 | tf_op jit(solution)/shard_map/ppermute | solution.py:290
  366.1 22.0 %collective-permute-start.16 = (bf16[64,1024]{1,0:T(8,128)(2,1)}, bf16[64,1024]{1,0:T(8,128)(2,1)}, u32[]{:S(2)}, u32[]{:S(2)}) collective-permute-start(bf16[64,1024]{1,0:T(8,128)(2,1)} %fusion.76), channel_id=1, source_target_pairs={{16,0},{17,1},{18,2},{19,3},{20,4},{21,5},{22,6},{23,7},{24,8},{25... | collective-permute-start | bytes 393224 | tf_op jit(solution)/shard_map/ppermute | solution.py:290
  374.0 13.6 %all-to-all-start.13 = ((bf16[8,16,1024]{2,1,0:T(8,128)(2,1)}), bf16[8,16,1024]{2,1,0:T(8,128)(2,1)S(1)}, u32[]{:S(2)}, u32[]{:S(2)}) async-start(bf16[8,16,1024]{2,1,0:T(8,128)(2,1)} %copy.269), calls=%async_computation.14 | async-start | bytes 524288 | tf_op jit(solution)/shard_map/all_to_all | solution.py:37
  388.0 5.1 %collective-permute-start.11 = (bf16[2,4,8192]{2,1,0:T(4,128)(2,1)S(1)}, bf16[2,4,8192]{2,1,0:T(4,128)(2,1)S(1)}, u32[]{:S(2)}, u32[]{:S(2)}) collective-permute-start(bf16[2,4,8192]{2,1,0:T(4,128)(2,1)S(1)} %get-tuple-element.33), channel_id=1, source_target_pairs={{0,16},{16,0},{1,17},{17,1},{2,18},{18,2},{3,19},{19,3},{4,20},{20... | collective-permute-start | bytes 393224 | tf_op jit(solution)/shard_map/ppermute | solution.py:22
  (77 other events, 528.6 us)
Sparse Core Ops, SparseCore 0:
  96.4 37.2 all-gather.1
  240.6 59.0 reduce-scatter.1

commit v2 on v1

v2 whole, which is shorter than its diff:
```python
import functools
import math

import jax
import jax.numpy as jnp
from jax import lax
from jax.experimental import pallas as pl
from jax.experimental.pallas import tpu as pltpu
from jax.sharding import PartitionSpec as P

HEAD_SIZE = 128
EPS = 1e-05
THETA = 500000.0
LR = 0.5
BF = jnp.bfloat16
F32 = jnp.float32


def mm(a, b, ca=1, cb=0):
    return lax.dot_general(a, b, (((ca,), (cb,)), ((), ())), preferred_element_type=F32)


def swap(value, axis, mask):
    pairs = [(source, source ^ mask) for source in range(lax.axis_size(axis))]
    return lax.ppermute(value, axis, pairs)


def same_core(size):
    return [list(range(c, size, 2)) for c in range(2)]


def z_exchange(value):
    size = lax.axis_size("tensor")
    return lax.all_to_all(
        value, "tensor", 0, 0, axis_index_groups=same_core(size), tiled=True
    )


def dp_exchange(value):
    return lax.all_to_all(value, "dp", 0, 0, tiled=True)


def tile_rows(value, copies):
    return jnp.broadcast_to(value[None], (copies,) + value.shape).reshape(
        (copies * value.shape[0],) + value.shape[1:]
    )


def call(body, shapes, *operands, flops=0):
    outs = [jax.ShapeDtypeStruct(shape, kind) for shape, kind in shapes]
    moved = sum(x.size * x.dtype.itemsize for x in list(operands) + outs)
    return pl.pallas_call(
        body,
        out_shape=outs,
        in_specs=[pl.BlockSpec(memory_space=pltpu.VMEM)] * len(operands),
        out_specs=[pl.BlockSpec(memory_space=pltpu.VMEM)] * len(outs),
        compiler_params=pltpu.CompilerParams(vmem_limit_bytes=48 * 2**20),
        cost_estimate=pl.CostEstimate(flops=flops, bytes_accessed=moved, transcendentals=0),
    )(*operands)


def one_hot(target):
    size = target.shape[1]
    row = lax.broadcasted_iota(jnp.int32, (size, size), 0)
    return jnp.where(row == target, 1.0, 0.0).astype(BF)


def pair_columns(column):
    high = column.astype(BF).astype(F32)
    lane = lax.broadcasted_iota(jnp.int32, (column.shape[0], 128), 1)
    return jnp.where(lane == 0, high, jnp.where(lane == 1, column - high, 0.0)).astype(BF)


def project_body(target, mine, other, wq, wkv, *rest):
    half = mine.shape[0]
    parts = []
    for rows in (mine[...], other[...]):
        wide = rows.astype(F32)
        squares = jnp.sum(wide * wide, axis=1, keepdims=True)
        parts.append(
            jnp.concatenate(
                [mm(rows, wq[...]).astype(BF), mm(rows, wkv[...], 1, 1).astype(BF), pair_columns(squares)],
                axis=1,
            )
        )
    order = one_hot(target[...])
    value = (mm(order[:, :half], parts[0]) + mm(order[:, half:], parts[1])).astype(BF)
    out = rest[-1]
    out[:, : value.shape[1]] = value
    if len(rest) > 1:
        out[:, value.shape[1] :] = rest[0][...]


def project(target, mine, other, wq, wkv, *extra):
    rows = 2 * mine.shape[0]
    cols = wq.shape[1] + wkv.shape[0] + 128
    flops = 2 * rows * cols * (mine.shape[1] + rows)
    cols = cols + sum(x.shape[1] for x in extra)
    return call(
        project_body, [((rows, cols), BF)], target, mine, other, wq, wkv, *extra, flops=flops
    )[0]


def mixed_grad_body(target, *refs):
    wo, out = refs[-2:]
    order = one_hot(target[...])
    total = None
    at = 0
    for part in refs[:-2]:
        count = part.shape[0]
        low = mm(part[...], wo[...], 1, 1).astype(BF)
        value = mm(order[:, at : at + count], low)
        total = value if total is None else total + value
        at = at + count
    out[...] = total.astype(BF)


def mixed_grad(target, parts, wo):
    rows = target.shape[1]
    cols = wo.shape[0]
    flops = 2 * rows * cols * (wo.shape[1] + rows)
    return call(mixed_grad_body, [((rows, cols), BF)], target, *parts, wo, flops=flops)[0]


def whole_body(target, got, wo, rows_out, out):
    rows = mm(one_hot(target[...]), got[...], 0, 0).astype(BF)
    rows_out[...] = rows
    out[...] = mm(rows, wo[...]).astype(BF)


def whole_project(target, got, wo):
    rows, cols = got.shape
    feats = wo.shape[1]
    return call(
        whole_body,
        [((rows, cols), BF), ((rows, feats), BF)],
        target,
        got,
        wo,
        flops=2 * rows * cols * (rows + feats),
    )


def out_body(target, got, wo, rows_out, other_out, mine_out):
    half = mine_out.shape[0]
    rows = mm(one_hot(target[...]), got[...], 0, 0).astype(BF)
    rows_out[...] = rows
    other_out[...] = mm(rows[half:], wo[...]).astype(BF)
    mine_out[...] = mm(rows[:half], wo[...])


def out_project(target, got, wo):
    rows, cols = got.shape
    feats = wo.shape[1]
    return call(
        out_body,
        [((rows, cols), BF), ((rows // 2, feats), BF), ((rows // 2, feats), F32)],
        target,
        got,
        wo,
        flops=2 * rows * cols * (rows + feats),
    )


def back_body(target, got, mine, other, wq, wkv, rows_out, other_out, mine_out):
    half = mine.shape[0]
    nq = wq.shape[1]
    end = nq + wkv.shape[0]
    rows = mm(one_hot(target[...]), got[:, : end + 128], 0, 0)
    coef = jnp.sum(rows[:, end:], axis=1, keepdims=True)
    low = rows[:, :end].astype(BF)
    rows_out[...] = low

    def term(part, c, held):
        value = mm(part[:, :nq], wq[...], 1, 1) + mm(part[:, nq:], wkv[...])
        return value - held[...].astype(F32) * c

    other_out[...] = term(low[half:], coef[half:], other).astype(BF)
    mine_out[...] = term(low[:half], coef[:half], mine)


def back_project(target, got, mine, other, wq, wkv):
    rows = got.shape[0]
    cols = wq.shape[1] + wkv.shape[0]
    feats = mine.shape[1]
    return call(
        back_body,
        [((rows, cols), BF), ((rows // 2, feats), BF), ((rows // 2, feats), F32)],
        target,
        got,
        mine,
        other,
        wq,
        wkv,
        flops=2 * rows * (cols + 128) * (rows + feats),
    )


def settle_body(count, got, held, out, wide_out):
    rows = held.shape[0]
    total = held[...].astype(F32)
    for i in range(count):
        total = total + got[i * rows : (i + 1) * rows].astype(F32)
    low = total.astype(BF)
    out[...] = low
    for i in range(count):
        wide_out[i * rows : (i + 1) * rows] = low


def settle(got, held):
    count = got.shape[0] // held.shape[0]
    return call(
        functools.partial(settle_body, count),
        [(held.shape, BF), (got.shape, BF)],
        got,
        held,
    )


def turn(value, cosine, sine):
    return value * cosine + pltpu.roll(value, HEAD_SIZE // 2, 1) * sine


def heads_down(value):
    count = value.shape[1] // HEAD_SIZE
    return jnp.concatenate(
        [value[:, i * HEAD_SIZE : (i + 1) * HEAD_SIZE] for i in range(count)], axis=0
    )


def heads_across(value, tokens):
    count = value.shape[0] // tokens
    return jnp.concatenate([value[i * tokens : (i + 1) * tokens] for i in range(count)], axis=1)


def add_parts(ref, tokens):
    total = ref[:tokens].astype(F32)
    for i in range(1, ref.shape[0] // tokens):
        total = total + ref[i * tokens : (i + 1) * tokens].astype(F32)
    return total


def look(total, nq, width, cosine, sine, mask):
    tokens = total.shape[0]
    heads = nq // HEAD_SIZE
    end = nq + 2 * HEAD_SIZE
    squares = jnp.sum(total[:, end:], axis=1, keepdims=True)
    scale = lax.rsqrt(squares / width + EPS)
    wide_cos = jnp.concatenate([cosine] * heads, axis=0)
    wide_sin = jnp.concatenate([sine] * heads, axis=0)
    queries = turn(heads_down(total[:, :nq] * scale), wide_cos, wide_sin).astype(BF)
    kv = (total[:, nq:end] * scale).astype(BF)
    keys = turn(kv[:, :HEAD_SIZE].astype(F32), cosine, sine).astype(BF)
    values = kv[:, HEAD_SIZE:]
    scores = mm(queries, keys, 1, 1) * (1.0 / math.sqrt(HEAD_SIZE))
    weights = jnp.exp(jnp.where(mask > 0.0, scores, -1e30))
    probs = weights / jnp.sum(weights, axis=1, keepdims=True)
    low = probs.astype(BF)
    return scale, queries, keys, values, probs, low, wide_cos, wide_sin


def look_back(total, d_mixed, nq, width, cosine, sine, seen):
    scale, queries, keys, values, probs, low, wide_cos, wide_sin = seen
    tokens = total.shape[0]
    end = nq + 2 * HEAD_SIZE
    dm = heads_down(d_mixed).astype(BF)
    d_probs = mm(dm, values, 1, 1)
    d_values = mm(low, dm, 0, 0)
    d_scores = probs * (d_probs - jnp.sum(probs * d_probs, axis=1, keepdims=True))
    d_scores = (d_scores * (1.0 / math.sqrt(HEAD_SIZE))).astype(BF)
    dq = turn(mm(d_scores, keys), wide_cos, -wide_sin)
    dk = turn(mm(d_scores, queries, 0, 0), cosine, -sine)
    dq = (heads_across(dq, tokens) * scale).astype(BF)
    dkv = (jnp.concatenate([dk, d_values], axis=1) * scale).astype(BF)
    both = jnp.concatenate([dq, dkv], axis=1)
    dot = jnp.sum(both.astype(F32) * total[:, :end], axis=1, keepdims=True)
    return jnp.concatenate([both, pair_columns(dot * scale * scale / width)], axis=1)


def spread(out, value):
    rows = value.shape[0]
    for i in range(out.shape[0] // rows):
        out[i * rows : (i + 1) * rows] = value


def forward_body(nq, width, got, cosine, sine, mask, mixed_out, total_out):
    tokens = cosine.shape[0]
    total = add_parts(got, tokens)
    total_out[...] = total
    seen = look(total, nq, width, cosine[...], sine[...], mask[...])
    spread(mixed_out, heads_across(mm(seen[5], seen[3]), tokens).astype(BF))


def both_body(nq, width, got, cosine, sine, mask, sent_out):
    tokens = cosine.shape[0]
    total = add_parts(got, tokens)
    d_mixed = total[:, total.shape[1] - nq :]
    total = total[:, : total.shape[1] - nq]
    seen = look(total, nq, width, cosine[...], sine[...], mask[...])
    mixed = heads_across(mm(seen[5], seen[3]), tokens).astype(BF)
    sent = look_back(total, d_mixed, nq, width, cosine[...], sine[...], seen)
    spread(sent_out, jnp.concatenate([sent, mixed], axis=1))


def backward_body(nq, width, total, grads, cosine, sine, mask, sent_out):
    tokens = cosine.shape[0]
    d_mixed = add_parts(grads, tokens)
    seen = look(total[...], nq, width, cosine[...], sine[...], mask[...])
    spread(sent_out, look_back(total[...], d_mixed, nq, width, cosine[...], sine[...], seen))


def shards(
    inputs,
    positions,
    out_grads,
    query_weight,
    key_value_weight,
    out_weight,
    query_stale,
    key_value_previous_gradient,
    out_stale,
):
    n_dp = lax.axis_size("dp")
    ranks = lax.axis_size("tensor")
    nz = ranks // 2
    pipe = lax.axis_index("pipe")
    rank = lax.axis_index("tensor")
    core = rank % 2
    first = pipe == 0
    micro, own, width = inputs.shape
    feats = width // n_dp
    block = own * ranks
    tokens = block * n_dp
    half = tokens // 2

    query_new = (query_weight.astype(F32) - LR * query_stale).astype(BF)
    kv_new = (key_value_weight.astype(F32) - LR * key_value_previous_gradient).astype(BF)
    out_new = (out_weight.astype(F32) - LR * out_stale).astype(BF)

    def arrange(own_part, other):
        return jnp.where(first, own_part, other), jnp.where(first, other, own_part)

    wq0, wq1 = arrange(query_new[0], swap(query_new[0], "pipe", 1))
    kv_own = kv_new[0].T
    kv_here, kv_next = arrange(kv_own, swap(kv_own, "pipe", 1))
    even = (rank // 2) % 2 == 0

    def whole_head(own_part):
        side = swap(own_part, "tensor", 1)
        pair = jnp.where(
            core == 0,
            jnp.concatenate([own_part, side], axis=0),
            jnp.concatenate([side, own_part], axis=0),
        )
        far = swap(pair, "tensor", 2)
        return jnp.where(
            even,
            jnp.concatenate([pair, far], axis=0),
            jnp.concatenate([far, pair], axis=0),
        )

    wkv0 = whole_head(kv_here)

    at = lax.broadcasted_iota(jnp.int32, (1, tokens), 1)
    inside = at % half
    chip = inside // (n_dp * own)
    rest = inside % (n_dp * own)
    target = (rest // own) * block + (chip * 2 + ((at // half) ^ core)) * own + rest % own
    rest = at % (n_dp * own)
    by_rank = (rest // own) * block + (at // (n_dp * own)) * own + rest % own

    spots = lax.dynamic_index_in_dim(positions, pipe, 0, keepdims=False)
    freqs = THETA ** (-2.0 * jnp.arange(HEAD_SIZE // 2, dtype=F32) / HEAD_SIZE)
    angles = spots.astype(F32)[:, None] * freqs[None, :]
    cosine = jnp.concatenate([jnp.cos(angles)] * 2, axis=1)
    sine = jnp.concatenate([-jnp.sin(angles), jnp.sin(angles)], axis=1)
    index = jnp.arange(block, dtype=jnp.int32)
    visible = (index[None, :] <= index[:, None]) & (index[None, :] >= (index - spots)[:, None])
    nq = query_new.shape[2]
    mask = jnp.concatenate([visible.astype(F32)] * (nq // HEAD_SIZE), axis=0)

    start = jnp.stack(
        [
            lax.dynamic_index_in_dim(inputs, pipe, 0, keepdims=False),
            lax.dynamic_index_in_dim(out_grads, pipe, 0, keepdims=False),
        ]
    )
    start = start.reshape(2, own, n_dp, feats).transpose(2, 0, 1, 3).reshape(n_dp * 2 * own, feats)
    start = dp_exchange(start).reshape(n_dp, 2, own, feats)
    h0 = start[:, 0].reshape(n_dp * own, feats)
    g1 = start[:, 1].reshape(n_dp * own, feats)

    def gather_z(tiled):
        mine = z_exchange(tiled)
        return mine, swap(mine, "tensor", 1)

    def scatter_z(part_mine, part_other):
        moved = swap(part_other, "tensor", 1)
        return z_exchange((part_mine + moved.astype(F32)).astype(BF))

    def head_rows(columns):
        return [((n_dp * block, columns), BF)]

    sent_columns = nq + 2 * HEAD_SIZE + 128

    h0_mine, h0_other = gather_z(tile_rows(h0, nz))
    part = project(target, h0_mine, h0_other, wq0, wkv0)
    part, g1_sent, own_out, kv_next = lax.optimization_barrier((part, g1, out_new[0], kv_next))
    got = dp_exchange(part)
    all_g1 = lax.all_gather(g1_sent, "tensor", axis=0, tiled=True)
    wo0, wo1 = arrange(own_out, swap(own_out, "pipe", 1))
    wkv1 = whole_head(kv_next)
    mixed0, total0 = call(
        functools.partial(forward_body, nq, width),
        head_rows(nq) + [((block, sent_columns), F32)],
        got,
        cosine,
        sine,
        mask,
    )
    got_m0, all_g1 = lax.optimization_barrier((dp_exchange(mixed0), all_g1))
    all_m0, far0, near0 = out_project(target, got_m0, wo0)
    h1, h1_tiled = settle(scatter_z(near0, far0), h0)

    dm1 = mixed_grad(by_rank, [all_g1], wo1)
    h1_mine, h1_other = gather_z(h1_tiled)
    got = dp_exchange(project(target, h1_mine, h1_other, wq1, wkv1, dm1))
    sent1 = call(
        functools.partial(both_body, nq, width),
        head_rows(sent_columns + nq),
        got,
        cosine,
        sine,
        mask,
    )[0]
    got1 = dp_exchange(sent1)
    rows1, far1, near1 = back_project(target, got1, h1_mine, h1_other, wq1, wkv1)
    g0, g0_tiled = settle(scatter_z(near1, far1), g1)

    def section_grads(rows, mine, other):
        grad_q = mm(mine, rows[:half, :nq], 0, 0) + mm(other, rows[half:, :nq], 0, 0)
        grad_kv = mm(rows[:half, nq:], mine, 0, 0) + mm(rows[half:, nq:], other, 0, 0)
        return grad_q, grad_kv

    g0_mine, g0_other = gather_z(g0_tiled)
    gq1, gkv1 = section_grads(rows1, h1_mine, h1_other)
    all_m1, term1 = whole_project(by_rank, got1[:, sent_columns:], wo1)
    go1 = mm(all_m1, all_g1, 0, 0)
    out1 = lax.psum_scatter(term1, "tensor", scatter_dimension=0, tiled=True)
    h2 = (h1.astype(F32) + out1.astype(F32)).astype(BF)
    got_dm0 = dp_exchange(mixed_grad(target, [g0_mine, g0_other], wo0))
    sent0 = call(
        functools.partial(backward_body, nq, width),
        head_rows(sent_columns),
        total0,
        got_dm0,
        cosine,
        sine,
        mask,
    )[0]
    go0 = mm(all_m0[:half], g0_mine, 0, 0) + mm(all_m0[half:], g0_other, 0, 0)
    rows0, far, near = back_project(target, dp_exchange(sent0), h0_mine, h0_other, wq0, wkv0)
    gi, _ = settle(scatter_z(near, far), g0)
    gq0, gkv0 = section_grads(rows0, h0_mine, h0_other)

    def kv_columns(grad):
        cols = grad.shape[0] // 4
        quarters = grad.astype(BF).reshape(2, 2, cols, feats)
        keep = lax.dynamic_index_in_dim(quarters, core, 1, keepdims=False)
        send = lax.dynamic_index_in_dim(quarters, 1 - core, 1, keepdims=False)
        pair = keep.astype(F32) + swap(send, "tensor", 1).astype(F32)
        pair = pair.astype(BF)
        zz = (rank // 2) % 2
        keep = lax.dynamic_index_in_dim(pair, zz, 0, keepdims=False)
        send = lax.dynamic_index_in_dim(pair, 1 - zz, 0, keepdims=False)
        return keep.astype(F32) + swap(send, "tensor", 2).astype(F32)

    def home(grad0, grad1):
        to1 = lax.ppermute(grad1.astype(BF), "pipe", [(0, 1)])
        to0 = lax.ppermute(grad0.astype(BF), "pipe", [(1, 0)])
        return jnp.where(first, grad0 + to0.astype(F32), grad1 + to1.astype(F32))

    query_grad = home(gq0, gq1)
    kv_grad = home(kv_columns(gkv0), kv_columns(gkv1)).T
    out_grad = home(go0, go1)

    ends = jnp.stack([h1, gi, h2, g0]).reshape(2, 2, n_dp, own, feats).transpose(2, 0, 1, 3, 4)
    ends = lax.all_to_all(
        ends.reshape(n_dp * 4 * own, feats), ("dp", "pipe"), 0, 0, tiled=True
    ).reshape(n_dp, micro, 2, own, feats)
    rows = ends.transpose(2, 1, 3, 0, 4).reshape(2, micro, own, width)
    return (
        rows[0][None],
        rows[1][None],
        query_new,
        kv_new,
        out_new,
        query_grad[None],
        kv_grad[None],
        out_grad[None],
    )


def solution(mesh):
    placed = (
        P(None, ("dp", "tensor"), None),
        P(None, "dp"),
        P(None, ("dp", "tensor"), None),
        P("pipe", "dp", "tensor"),
        P("pipe", "dp", "tensor"),
        P("pipe", "tensor", "dp"),
        P("pipe", "dp", "tensor"),
        P("pipe", "dp", "tensor"),
        P("pipe", "tensor", "dp"),
    )
    return jax.shard_map(
        shards,
        mesh=mesh,
        in_specs=placed,
        out_specs=(
            P("pipe", None, ("dp", "tensor"), None),
            P("pipe", None, ("dp", "tensor"), None),
            P("pipe", "dp", "tensor"),
            P("pipe", "dp", "tensor"),
            P("pipe", "tensor", "dp"),
            P("pipe", "dp", "tensor"),
            P("pipe", "dp", "tensor"),
            P("pipe", "tensor", "dp"),
        ),
        check_vma=False,
    )
```

time: 405 us -> 339 us (0.84)
  matrix products: 63.7 us -> 13.5 us
  blocking collectives: 43.8 us -> 74.4 us
  local copies, waits for them, and re-layouts: 40.4 us -> 15 us
  other arithmetic: 40.9 us -> 20.9 us
  Pallas kernels: 0 us -> 15.8 us
  waiting for transfers between devices: 116 us -> 107 us
  starting transfers between devices: 80.4 us -> 75.8 us
    dot_general x40 -> x11, matrix products: 47.1 us -> 13.5 us  [mm(): lax.dot_general(a, b, (((ca,), (cb,)), ((), ())), preferred_element_type=...]
    all_to_all x1 -> x3, blocking collectives: 19.2 us -> 52.4 us  [dp_exchange(): return lax.all_to_all(value, 'dp', 0, 0, tiled=True)]
    all_to_all x7 -> x4, waiting for transfers between devices: 53.2 us -> 21.1 us  [dp_exchange(): return lax.all_to_all(value, 'dp', 0, 0, tiled=True)]
    all_to_all x5, waiting for transfers between devices: 32.3 us -> 48.4 us  [z_exchange(): lax.all_to_all(value, 'tensor', 0, 0, axis_index_groups=same_core(size),...]
    pallas_call x0 -> x14, Pallas kernels: none -> 15.8 us  [call(): pl.pallas_call(body, out_shape=outs, in_specs=[pl.BlockSpec(memory_space=...]
    all_to_all x7 -> x4, starting transfers between devices: 31.7 us -> 16.8 us  [dp_exchange(): return lax.all_to_all(value, 'dp', 0, 0, tiled=True)]
    dot_general x10 -> x0, matrix products: 14.7 us -> none  [the longest x2 3.61 us: attention_back(): jnp.einsum('gqk,kh->qgh', d_scores, keys, preferred_element_type=F32)]
    concatenate x6 -> x0, local copies, waits for them, and re-layouts: 11.5 us -> none  [the longest x4 9.16 us: project(): jnp.concatenate([q.astype(BF), kv.astype(BF), split_pair(jnp.sum(wide * w...]
  transfers between devices with their start and end apart: 36 -> 35, of which waited for: 17 -> 17; matrix products, arithmetic and copies ran while one was open for 24% -> 11% of each run, Pallas kernels for 0% -> 3%
where the time goes in v2:
time: 339 us; the launch traced here: 337 us
  waiting for transfers between devices  107 us (32%)
  starting transfers between devices  75.8 us (22%)
  blocking collectives  74.4 us (22%)
  other arithmetic  20.9 us (6%)
  Pallas kernels  15.8 us (5%)
  local copies, waits for them, and re-layouts  15 us (4%)
  between operations  15 us (4%)
  matrix products  13.5 us (4%)
    all_to_all x3, blocking collectives, dp_exchange(): return lax.all_to_all(value, 'dp', 0, 0, tiled=True)  52.4 us
    all_to_all x5, waiting for transfers between devices, z_exchange(): lax.all_to_all(value, 'tensor', 0, 0, axis_index_groups=same_core(size),...  48.4 us
    all_to_all x5, starting transfers between devices, z_exchange(): lax.all_to_all(value, 'tensor', 0, 0, axis_index_groups=same_core(size),...  27 us
    ppermute x17, waiting for transfers between devices, swap(): return lax.ppermute(value, axis, pairs)  22.7 us
    all_to_all x1, blocking collectives, z_exchange(): lax.all_to_all(value, 'tensor', 0, 0, axis_index_groups=same_core(size),...  22 us
    all_to_all x4, waiting for transfers between devices, dp_exchange(): return lax.all_to_all(value, 'dp', 0, 0, tiled=True)  21.1 us
    all_to_all x4, starting transfers between devices, dp_exchange(): return lax.all_to_all(value, 'dp', 0, 0, tiled=True)  16.8 us
    pallas_call x14, Pallas kernels, call(): pl.pallas_call(body, out_shape=outs, in_specs=[pl.BlockSpec(memory_space=...  15.8 us
  transfers between devices with their start and end apart: 35, of which 17 were waited for; matrix products, arithmetic and copies ran while one was open for 11% of the time, Pallas kernels for 3%

profile of v2, /device:TPU:8, one launch (start us, length us, event | category | flops | bytes accessed | tf_op | source)
XLA Modules:
  0.0 337.1 jit_solution(7905561374957131172)
XLA Ops:
  8.3 13.9 %all_to_all.148 = bf16[8,8,1024]{2,1,0:T(8,128)(2,1)S(1)} all-to-all(bf16[8,8,1024]{2,1,0:T(8,128)(2,1)S(1)} %all_to_all.95), channel_id=1, replica_groups=mesh['dp'=8,'pipe'=2,'tensor'=16] {'dp'}, dimensions={0} | all-to-all | bytes 262144 | tf_op jit(solution)/shard_map/all_to_all | solution.py:40
  23.3 8.6 %all-to-all-start.1 = ((bf16[8,32,1024]{2,1,0:T(8,128)(2,1)}), bf16[8,32,1024]{2,1,0:T(8,128)(2,1)S(1)}, u32[]{:S(2)}, u32[]{:S(2)}) async-start(bf16[8,32,1024]{2,1,0:T(8,128)(2,1)} %broadcast_in_dim.11), calls=%async_computation.1 | async-start | bytes 1048576 | tf_op jit(solution)/shard_map/all_to_all | solution.py:34
  33.4 3.6 %collective-permute-done.2 = bf16[64,1024]{1,0:T(8,128)(2,1)S(1)} collective-permute-done((bf16[64,1024]{1,0:T(8,128)(2,1)S(1)}, bf16[64,1024]{1,0:T(8,128)(2,1)S(1)}, u32[]{:S(2)}, u32[]{:S(2)}) %collective-permute-start.2) | collective-permute-done | bytes 131104 | tf_op jit(solution)/shard_map/ppermute | solution.py:25
  39.4 2.1 collective-permute-start.4
  41.4 7.0 %all-to-all-done.1 = bf16[8,32,1024]{2,1,0:T(8,128)(2,1)S(1)} async-done(((bf16[8,32,1024]{2,1,0:T(8,128)(2,1)}), bf16[8,32,1024]{2,1,0:T(8,128)(2,1)S(1)}, u32[]{:S(2)}, u32[]{:S(2)}) %all-to-all-start.1) | async-done | bytes 524320 | tf_op jit(solution)/shard_map/all_to_all | solution.py:34
  48.5 1.5 subtract_convert_fusion
  53.2 2.1 shard_map.152
  56.1 3.6 %all-to-all-start.2 = ((bf16[8,64,640]{2,1,0:T(8,128)(2,1)}), bf16[8,64,640]{2,1,0:T(8,128)(2,1)S(1)}, u32[]{:S(2)}, u32[]{:S(2)}) async-start(bf16[8,64,640]{2,1,0:T(8,128)(2,1)} %bitcast.8), calls=%async_computation.2 | async-start | bytes 1310720 | tf_op jit(solution)/shard_map/all_to_all | solution.py:40
  59.6 1.5 collective-permute-start.5
  61.5 11.9 %all-to-all-done.2 = bf16[8,64,640]{2,1,0:T(8,128)(2,1)S(1)} async-done(((bf16[8,64,640]{2,1,0:T(8,128)(2,1)}), bf16[8,64,640]{2,1,0:T(8,128)(2,1)S(1)}, u32[]{:S(2)}, u32[]{:S(2)}) %all-to-all-start.2) | async-done | bytes 655392 | tf_op jit(solution)/shard_map/all_to_all | solution.py:40
  75.3 3.4 %all-to-all-start.3 = ((bf16[8,64,256]{2,1,0:T(8,128)(2,1)}), bf16[8,64,256]{2,1,0:T(8,128)(2,1)S(1)}, u32[]{:S(2)}, u32[]{:S(2)}) async-start(bf16[8,64,256]{2,1,0:T(8,128)(2,1)} %bitcast.11), calls=%async_computation.3 | async-start | bytes 524288 | tf_op jit(solution)/shard_map/all_to_all | solution.py:40
  78.7 2.3 collective-permute-done.5
  82.1 5.4 %all-to-all-done.3 = bf16[8,64,256]{2,1,0:T(8,128)(2,1)S(1)} async-done(((bf16[8,64,256]{2,1,0:T(8,128)(2,1)}), bf16[8,64,256]{2,1,0:T(8,128)(2,1)S(1)}, u32[]{:S(2)}, u32[]{:S(2)}) %all-to-all-start.3) | async-done | bytes 262176 | tf_op jit(solution)/shard_map/all_to_all | solution.py:40
  87.5 4.8 %all-gather.2.cloned.1.call-done.refs_0_ = bf16[512,1024]{1,0:T(8,128)(2,1)} async-done(((bf16[32,1024]{1,0:T(8,128)(2,1)}), bf16[512,1024]{1,0:T(8,128)(2,1)}) %all-gather.2.cloned.1.call-update) | async-done | bytes 1048592 | tf_op jit(solution)/shard_map/all_gather | solution.py:410
  93.6 1.7 collective-permute-done.6
  95.4 22.0 %all_to_all.149 = bf16[8,32,1024]{2,1,0:T(8,128)(2,1)S(1)} all-to-all(bf16[8,32,1024]{2,1,0:T(8,128)(2,1)S(1)} %bitcast.148), channel_id=1, replica_groups={{0,2,4,6,8,10,12,14},{1,3,5,7,9,11,13,15},{16,18,20,22,24,26,28,30},{17..., dimensions={0} | all-to-all | bytes 1048576 | tf_op jit(solution)/shard_map/all_to_all | solution.py:34
  118.3 3.6 %all-to-all-start.5 = ((bf16[8,32,1024]{2,1,0:T(8,128)(2,1)}), bf16[8,32,1024]{2,1,0:T(8,128)(2,1)S(1)}, u32[]{:S(2)}, u32[]{:S(2)}) async-start(bf16[8,32,1024]{2,1,0:T(8,128)(2,1)} %bitcast.135), calls=%async_computation.5 | async-start | bytes 1048576 | tf_op jit(solution)/shard_map/all_to_all | solution.py:34
  122.0 17.2 %all-to-all-done.5 = bf16[8,32,1024]{2,1,0:T(8,128)(2,1)S(1)} async-done(((bf16[8,32,1024]{2,1,0:T(8,128)(2,1)}), bf16[8,32,1024]{2,1,0:T(8,128)(2,1)S(1)}, u32[]{:S(2)}, u32[]{:S(2)}) %all-to-all-start.5) | async-done | bytes 524320 | tf_op jit(solution)/shard_map/all_to_all | solution.py:34
  141.2 8.1 %collective-permute-done.9 = bf16[128,1024]{1,0:T(8,128)(2,1)S(1)} collective-permute-done((bf16[128,1024]{1,0:T(8,128)(2,1)S(1)}, bf16[128,1024]{1,0:T(8,128)(2,1)S(1)}, u32[]{:S(2)}, u32[]{:S(2)}) %collective-permute-start.9) | collective-permute-done | bytes 262176 | tf_op jit(solution)/shard_map/ppermute | solution.py:25
  151.7 21.3 %all_to_all.150 = bf16[8,64,896]{2,1,0:T(8,128)(2,1)S(1)} all-to-all(bf16[8,64,896]{2,1,0:T(8,128)(2,1)S(1)} %bitcast.132), channel_id=1, replica_groups=mesh['dp'=8,'pipe'=2,'tensor'=16] {'dp'}, dimensions={0} | all-to-all | bytes 1835008 | tf_op jit(solution)/shard_map/all_to_all | solution.py:40
  174.1 17.2 %all_to_all.151 = bf16[8,64,896]{2,1,0:T(8,128)(2,1)S(1)} all-to-all(bf16[8,64,896]{2,1,0:T(8,128)(2,1)S(1)} %bitcast.125), channel_id=1, replica_groups=mesh['dp'=8,'pipe'=2,'tensor'=16] {'dp'}, dimensions={0} | all-to-all | bytes 1835008 | tf_op jit(solution)/shard_map/all_to_all | solution.py:40
  192.5 1.9 collective-permute-done.10
  195.4 4.1 %all-to-all-start.8 = ((bf16[8,32,1024]{2,1,0:T(8,128)(2,1)}), bf16[8,32,1024]{2,1,0:T(8,128)(2,1)}, u32[]{:S(2)}, u32[]{:S(2)}) async-start(bf16[8,32,1024]{2,1,0:T(8,128)(2,1)} %bitcast.147), calls=%async_computation.8 | async-start | bytes 1048576 | tf_op jit(solution)/shard_map/all_to_all | solution.py:34
  204.1 2.2 fusion.9
  206.4 11.3 %all-to-all-done.8 = bf16[8,32,1024]{2,1,0:T(8,128)(2,1)} async-done(((bf16[8,32,1024]{2,1,0:T(8,128)(2,1)}), bf16[8,32,1024]{2,1,0:T(8,128)(2,1)}, u32[]{:S(2)}, u32[]{:S(2)}) %all-to-all-start.8) | async-done | bytes 524320 | tf_op jit(solution)/shard_map/all_to_all | solution.py:34
  220.2 3.5 %all-to-all-start.9 = ((bf16[8,32,1024]{2,1,0:T(8,128)(2,1)}), bf16[8,32,1024]{2,1,0:T(8,128)(2,1)S(1)}, u32[]{:S(2)}, u32[]{:S(2)}) async-start(bf16[8,32,1024]{2,1,0:T(8,128)(2,1)} %bitcast.134), calls=%async_computation.9 | async-start | bytes 1048576 | tf_op jit(solution)/shard_map/all_to_all | solution.py:34
  223.7 1.7 fusion.1
  227.1 1.5 fusion.34
  229.9 12.9 %all-to-all-done.9 = bf16[8,32,1024]{2,1,0:T(8,128)(2,1)S(1)} async-done(((bf16[8,32,1024]{2,1,0:T(8,128)(2,1)}), bf16[8,32,1024]{2,1,0:T(8,128)(2,1)S(1)}, u32[]{:S(2)}, u32[]{:S(2)}) %all-to-all-start.9) | async-done | bytes 524320 | tf_op jit(solution)/shard_map/all_to_all | solution.py:34
  245.1 1.6 fusion.36
  249.5 3.5 %all-to-all-start.10 = ((bf16[8,64,256]{2,1,0:T(8,128)(2,1)}), bf16[8,64,256]{2,1,0:T(8,128)(2,1)S(1)}, u32[]{:S(2)}, u32[]{:S(2)}) async-start(bf16[8,64,256]{2,1,0:T(8,128)(2,1)} %bitcast.26), calls=%async_computation.10 | async-start | bytes 524288 | tf_op jit(solution)/shard_map/all_to_all | solution.py:40
  255.2 6.7 %reduce-scatter.2.cloned.1.call-done = bf16[32,1024]{1,0:T(8,128)(2,1)} async-done(((bf16[512,1024]{1,0:T(8,128)(2,1)}), bf16[32,1024]{1,0:T(8,128)(2,1)}) %reduce-scatter.2.cloned.1.call-update) | async-done | bytes 65552 | tf_op jit(solution)/shard_map/reduce_scatter | solution.py:449
  261.9 1.5 fusion.21
  263.4 1.7 shard_map.162
  265.0 6.3 %all-to-all-start.11 = ((bf16[8,64,640]{2,1,0:T(8,128)(2,1)}), bf16[8,64,640]{2,1,0:T(8,128)(2,1)S(1)}, u32[]{:S(2)}, u32[]{:S(2)}) async-start(bf16[8,64,640]{2,1,0:T(8,128)(2,1)} %bitcast.28), calls=%async_computation.11 | async-start | bytes 1310720 | tf_op jit(solution)/shard_map/all_to_all | solution.py:40
  273.1 5.4 %collective-permute-start.21 = (bf16[256,1024]{1,0:T(8,128)(2,1)}, bf16[256,1024]{1,0:T(8,128)(2,1)}, u32[]{:S(2)}, u32[]{:S(2)}) collective-permute-start(bf16[256,1024]{1,0:T(8,128)(2,1)} %get-tuple-element.75), channel_id=1, source_target_pairs={{16,0},{17,1},{18,2},{19,3},{20,4},{21,5},{22,6},{23,7},{24,8},{25... | collective-permute-start | bytes 1572872 | tf_op jit(solution)/shard_map/ppermute | solution.py:480
  278.5 3.8 %all-to-all-done.11 = bf16[8,64,640]{2,1,0:T(8,128)(2,1)S(1)} async-done(((bf16[8,64,640]{2,1,0:T(8,128)(2,1)}), bf16[8,64,640]{2,1,0:T(8,128)(2,1)S(1)}, u32[]{:S(2)}, u32[]{:S(2)}) %all-to-all-start.11) | async-done | bytes 655392 | tf_op jit(solution)/shard_map/all_to_all | solution.py:40
  287.0 7.2 %all-to-all-start.12 = ((bf16[8,32,1024]{2,1,0:T(8,128)(2,1)}), bf16[8,32,1024]{2,1,0:T(8,128)(2,1)S(1)}, u32[]{:S(2)}, u32[]{:S(2)}) async-start(bf16[8,32,1024]{2,1,0:T(8,128)(2,1)} %bitcast.30), calls=%async_computation.12 | async-start | bytes 1048576 | tf_op jit(solution)/shard_map/all_to_all | solution.py:34
  294.2 2.5 fusion.35
  296.7 3.7 %collective-permute-start.13 = (bf16[1024,256]{1,0:T(8,128)(2,1)}, bf16[1024,256]{1,0:T(8,128)(2,1)S(1)}, u32[]{:S(2)}, u32[]{:S(2)}) collective-permute-start(bf16[1024,256]{1,0:T(8,128)(2,1)} %get-tuple-element.71), channel_id=1, source_target_pairs={{16,0},{17,1},{18,2},{19,3},{20,4},{21,5},{22,6},{23,7},{24,8},{25... | collective-permute-start | bytes 1572872 | tf_op jit(solution)/shard_map/ppermute | solution.py:480
  301.4 2.1 collective-permute-start.16
  303.5 2.5 select_bitcast_fusion
  306.0 4.8 %collective-permute-done.16 = bf16[64,1024]{1,0:T(8,128)(2,1)S(1)} collective-permute-done((bf16[64,1024]{1,0:T(8,128)(2,1)S(1)}, bf16[64,1024]{1,0:T(8,128)(2,1)S(1)}, u32[]{:S(2)}, u32[]{:S(2)}) %collective-permute-start.16) | collective-permute-done | bytes 131104 | tf_op jit(solution)/shard_map/ppermute | solution.py:25
  311.5 4.1 %collective-permute-start.17 = (bf16[64,1024]{1,0:T(8,128)(2,1)}, bf16[64,1024]{1,0:T(8,128)(2,1)}, u32[]{:S(2)}, u32[]{:S(2)}) collective-permute-start(bf16[64,1024]{1,0:T(8,128)(2,1)} %fusion.4), channel_id=1, source_target_pairs={{16,0},{17,1},{18,2},{19,3},{20,4},{21,5},{22,6},{23,7},{24,8},{25... | collective-permute-start | bytes 393224 | tf_op jit(solution)/shard_map/ppermute | solution.py:480
  317.6 3.7 %all-to-all-start.13 = ((bf16[16,8,1024]{2,1,0:T(8,128)(2,1)}), bf16[16,8,1024]{2,1,0:T(8,128)(2,1)S(1)}, u32[]{:S(2)}, u32[]{:S(2)}) async-start(bf16[16,8,1024]{2,1,0:T(8,128)(2,1)} %all_to_all.132), calls=%async_computation.14 | async-start | bytes 524288 | tf_op jit(solution)/shard_map/all_to_all | solution.py:488
  321.3 2.3 select_bitcast_fusion.1
  323.6 1.8 select_bitcast_fusion.2
  325.4 3.0 all-to-all-done.13
  (211 shorter events, 52.3 us)
Async XLA Ops:
  22.4 9.5 %copy-start.47 = (f32[1,1024,64]{1,2,0:T(8,128)S(1)}, f32[1,1024,64]{1,2,0:T(8,128)}, u32[]{:S(2)}) copy-start(f32[1,1024,64]{1,2,0:T(8,128)} %param.16) | copy-start | bytes 786436
  23.3 14.5 %copy-start.39 = (f32[1,1024,256]{2,1,0:T(8,128)S(1)}, f32[1,1024,256]{2,1,0:T(8,128)}, u32[]{:S(2)}) copy-start(f32[1,1024,256]{2,1,0:T(8,128)} %param.15) | copy-start | bytes 3145732
  23.3 25.2 %all-to-all-start.1 = ((bf16[8,32,1024]{2,1,0:T(8,128)(2,1)}), bf16[8,32,1024]{2,1,0:T(8,128)(2,1)S(1)}, u32[]{:S(2)}, u32[]{:S(2)}) async-start(bf16[8,32,1024]{2,1,0:T(8,128)(2,1)} %broadcast_in_dim.11), calls=%async_computation.1 | async-start | bytes 1048576 | tf_op jit(solution)/shard_map/all_to_all | solution.py:34
  31.9 60.4 %all-gather.2.cloned.1.call-start = ((), (), s32[]{:S(2)}) async-start(), calls=%async_computation.15 | async-start | bytes 1114112 | tf_op jit(solution)/shard_map/all_gather | solution.py:410
  32.0 5.1 %collective-permute-start.2 = (bf16[64,1024]{1,0:T(8,128)(2,1)S(1)}, bf16[64,1024]{1,0:T(8,128)(2,1)S(1)}, u32[]{:S(2)}, u32[]{:S(2)}) collective-permute-start(bf16[64,1024]{1,0:T(8,128)(2,1)S(1)} %bitcast.151), channel_id=1, source_target_pairs={{0,16},{16,0},{1,17},{17,1},{2,18},{18,2},{3,19},{19,3},{4,20},{20... | collective-permute-start | bytes 393224 | tf_op jit(solution)/shard_map/ppermute | solution.py:25
  37.7 1.6 collective-permute-start.3
  37.9 14.4 %copy-start.34 = (bf16[1,1024,256]{2,1,0:T(8,128)(2,1)}, bf16[1,1024,256]{2,1,0:T(8,128)(2,1)S(1)}, u32[]{:S(2)}) copy-start(bf16[1,1024,256]{2,1,0:T(8,128)(2,1)S(1)} %subtract_convert_fusion.1) | copy-start | bytes 1572868
  37.9 14.4 %collective-permute-start.1 = (bf16[1024,256]{1,0:T(8,128)(2,1)S(1)}, bf16[1024,256]{1,0:T(8,128)(2,1)S(1)}, u32[]{:S(2)}, u32[]{:S(2)}) collective-permute-start(bf16[1024,256]{1,0:T(8,128)(2,1)S(1)} %bitcast.144), channel_id=1, source_target_pairs={{0,16},{16,0},{1,17},{17,1},{2,18},{18,2},{3,19},{19,3},{4,20},{20... | collective-permute-start | bytes 1572872 | tf_op jit(solution)/shard_map/ppermute | solution.py:25
  39.4 11.4 %collective-permute-start.4 = (bf16[128,1024]{1,0:T(8,128)(2,1)S(1)}, bf16[128,1024]{1,0:T(8,128)(2,1)}, u32[]{:S(2)}, u32[]{:S(2)}) collective-permute-start(bf16[128,1024]{1,0:T(8,128)(2,1)S(1)} %maximum_select_fusion.2), channel_id=1, source_target_pairs={{0,2},{1,3},{2,0},{3,1},{4,6},{5,7},{6,4},{7,5},{8,10},{9,11},{10,... | collective-permute-start | bytes 786440 | tf_op jit(solution)/shard_map/ppermute | solution.py:25
  48.5 4.7 %collective-permute-start = (bf16[256,1024]{1,0:T(8,128)(2,1)S(1)}, bf16[256,1024]{1,0:T(8,128)(2,1)S(1)}, u32[]{:S(2)}, u32[]{:S(2)}) collective-permute-start(bf16[256,1024]{1,0:T(8,128)(2,1)S(1)} %bitcast.111), channel_id=1, source_target_pairs={{0,1},{1,0},{2,3},{3,2},{4,5},{5,4},{6,7},{7,6},{8,9},{9,8},{10,11... | collective-permute-start | bytes 1572872 | tf_op jit(solution)/shard_map/ppermute | solution.py:25
  50.0 31.0 %copy-start.35 = (bf16[1,256,1024]{2,1,0:T(8,128)(2,1)}, bf16[1,256,1024]{2,1,0:T(8,128)(2,1)S(1)}, u32[]{:S(2)}) copy-start(bf16[1,256,1024]{2,1,0:T(8,128)(2,1)S(1)} %subtract_convert_fusion) | copy-start | bytes 1572868
  56.1 17.3 %all-to-all-start.2 = ((bf16[8,64,640]{2,1,0:T(8,128)(2,1)}), bf16[8,64,640]{2,1,0:T(8,128)(2,1)S(1)}, u32[]{:S(2)}, u32[]{:S(2)}) async-start(bf16[8,64,640]{2,1,0:T(8,128)(2,1)} %bitcast.8), calls=%async_computation.2 | async-start | bytes 1310720 | tf_op jit(solution)/shard_map/all_to_all | solution.py:40
  59.6 21.4 %collective-permute-start.5 = (bf16[256,1024]{1,0:T(8,128)(2,1)S(1)}, bf16[256,1024]{1,0:T(8,128)(2,1)}, u32[]{:S(2)}, u32[]{:S(2)}) collective-permute-start(bf16[256,1024]{1,0:T(8,128)(2,1)S(1)} %bitcast.145), channel_id=1, source_target_pairs={{0,16},{16,0},{1,17},{17,1},{2,18},{18,2},{3,19},{19,3},{4,20},{20... | collective-permute-start | bytes 1572872 | tf_op jit(solution)/shard_map/ppermute | solution.py:25
  75.3 12.2 %all-to-all-start.3 = ((bf16[8,64,256]{2,1,0:T(8,128)(2,1)}), bf16[8,64,256]{2,1,0:T(8,128)(2,1)S(1)}, u32[]{:S(2)}, u32[]{:S(2)}) async-start(bf16[8,64,256]{2,1,0:T(8,128)(2,1)} %bitcast.11), calls=%async_computation.3 | async-start | bytes 524288 | tf_op jit(solution)/shard_map/all_to_all | solution.py:40
  82.1 11.1 %copy-start.1 = (bf16[256,1024]{1,0:T(8,128)(2,1)}, bf16[256,1024]{1,0:T(8,128)(2,1)S(1)}, u32[]{:S(2)}) copy-start(bf16[256,1024]{1,0:T(8,128)(2,1)S(1)} %get-tuple-element.57.wo.refs_2_) | copy-start | bytes 1572868
  93.2 2.0 collective-permute-start.6
  118.3 143.6 %copy-start.22 = (bf16[32,1024]{1,0:T(8,128)(2,1)}, bf16[32,1024]{1,0:T(8,128)(2,1)S(1)}, u32[]{:S(2)}) copy-start(bf16[32,1024]{1,0:T(8,128)(2,1)S(1)} %get-tuple-element.39) | copy-start | bytes 196612
  118.3 21.0 %all-to-all-start.5 = ((bf16[8,32,1024]{2,1,0:T(8,128)(2,1)}), bf16[8,32,1024]{2,1,0:T(8,128)(2,1)S(1)}, u32[]{:S(2)}, u32[]{:S(2)}) async-start(bf16[8,32,1024]{2,1,0:T(8,128)(2,1)} %bitcast.135), calls=%async_computation.5 | async-start | bytes 1048576 | tf_op jit(solution)/shard_map/all_to_all | solution.py:34
  121.9 27.5 %copy-start = (bf16[512,1024]{1,0:T(8,128)(2,1)S(1)}, bf16[512,1024]{1,0:T(8,128)(2,1)}, u32[]{:S(2)}) copy-start(bf16[512,1024]{1,0:T(8,128)(2,1)} %all-gather.2.cloned.1.call-done.refs_0_) | copy-start | bytes 3145732
  121.9 17.3 %collective-permute-start.8 = (bf16[64,1024]{1,0:T(8,128)(2,1)S(1)}, bf16[64,1024]{1,0:T(8,128)(2,1)}, u32[]{:S(2)}, u32[]{:S(2)}) collective-permute-start(bf16[64,1024]{1,0:T(8,128)(2,1)S(1)} %copy-done.40), channel_id=1, source_target_pairs={{0,1},{1,0},{2,3},{3,2},{4,5},{5,4},{6,7},{7,6},{8,9},{9,8},{10,11... | collective-permute-start | bytes 393224 | tf_op jit(solution)/shard_map/ppermute | solution.py:25
  139.2 11.1 %collective-permute-start.7 = (bf16[256,1024]{1,0:T(8,128)(2,1)S(1)}, bf16[256,1024]{1,0:T(8,128)(2,1)S(1)}, u32[]{:S(2)}, u32[]{:S(2)}) collective-permute-start(bf16[256,1024]{1,0:T(8,128)(2,1)S(1)} %bitcast.116), channel_id=1, source_target_pairs={{0,1},{1,0},{2,3},{3,2},{4,5},{5,4},{6,7},{7,6},{8,9},{9,8},{10,11... | collective-permute-start | bytes 1572872 | tf_op jit(solution)/shard_map/ppermute | solution.py:25
  140.3 9.0 %collective-permute-start.9 = (bf16[128,1024]{1,0:T(8,128)(2,1)S(1)}, bf16[128,1024]{1,0:T(8,128)(2,1)S(1)}, u32[]{:S(2)}, u32[]{:S(2)}) collective-permute-start(bf16[128,1024]{1,0:T(8,128)(2,1)S(1)} %maximum_select_fusion.3), channel_id=1, source_target_pairs={{0,2},{1,3},{2,0},{3,1},{4,6},{5,7},{6,4},{7,5},{8,10},{9,11},{10,... | collective-permute-start | bytes 786440 | tf_op jit(solution)/shard_map/ppermute | solution.py:25
  150.4 40.9 %copy-start.3 = (bf16[256,1024]{1,0:T(8,128)(2,1)}, bf16[256,1024]{1,0:T(8,128)(2,1)S(1)}, u32[]{:S(2)}) copy-start(bf16[256,1024]{1,0:T(8,128)(2,1)S(1)} %collective-permute-done.7.other) | copy-start | bytes 1572868
  192.4 2.0 collective-permute-start.10
  195.4 22.3 %all-to-all-start.8 = ((bf16[8,32,1024]{2,1,0:T(8,128)(2,1)}), bf16[8,32,1024]{2,1,0:T(8,128)(2,1)}, u32[]{:S(2)}, u32[]{:S(2)}) async-start(bf16[8,32,1024]{2,1,0:T(8,128)(2,1)} %bitcast.147), calls=%async_computation.8 | async-start | bytes 1048576 | tf_op jit(solution)/shard_map/all_to_all | solution.py:34
  199.5 62.4 %reduce-scatter.2.cloned.1.call-start = ((), (), s32[]{:S(2)}) async-start(), calls=%async_computation.16 | async-start | bytes 1114112 | tf_op jit(solution)/shard_map/reduce_scatter | solution.py:449
  204.1 13.5 %copy-start.10 = (bf16[32,1024]{1,0:T(8,128)(2,1)S(1)}, bf16[32,1024]{1,0:T(8,128)(2,1)}, u32[]{:S(2)}) copy-start(bf16[32,1024]{1,0:T(8,128)(2,1)} %reshape_squeeze.4.held) | copy-start | bytes 196612
  220.2 22.6 %all-to-all-start.9 = ((bf16[8,32,1024]{2,1,0:T(8,128)(2,1)}), bf16[8,32,1024]{2,1,0:T(8,128)(2,1)S(1)}, u32[]{:S(2)}, u32[]{:S(2)}) async-start(bf16[8,32,1024]{2,1,0:T(8,128)(2,1)} %bitcast.134), calls=%async_computation.9 | async-start | bytes 1048576 | tf_op jit(solution)/shard_map/all_to_all | solution.py:34
  226.3 16.5 %collective-permute-start.18 = (bf16[2,64,1024]{2,1,0:T(8,128)(2,1)}, bf16[2,64,1024]{2,1,0:T(8,128)(2,1)}, u32[]{:S(2)}, u32[]{:S(2)}) collective-permute-start(bf16[2,64,1024]{2,1,0:T(8,128)(2,1)} %dynamic-slice_bitcast_fusion), channel_id=1, source_target_pairs={{0,1},{1,0},{2,3},{3,2},{4,5},{5,4},{6,7},{7,6},{8,9},{9,8},{10,11... | collective-permute-start | bytes 786440 | tf_op jit(solution)/shard_map/ppermute | solution.py:25
  228.6 92.7 %collective-permute-start.14 = (bf16[1024,256]{1,0:T(8,128)(2,1)}, bf16[1024,256]{1,0:T(8,128)(2,1)}, u32[]{:S(2)}, u32[]{:S(2)}) collective-permute-start(bf16[1024,256]{1,0:T(8,128)(2,1)} %get-tuple-element.69), channel_id=1, source_target_pairs={{0,16},{1,17},{2,18},{3,19},{4,20},{5,21},{6,22},{7,23},{8,24},{9,... | collective-permute-start | bytes 1572872 | tf_op jit(solution)/shard_map/ppermute | solution.py:479
  242.8 5.2 %collective-permute-start.11 = (bf16[256,1024]{1,0:T(8,128)(2,1)S(1)}, bf16[256,1024]{1,0:T(8,128)(2,1)S(1)}, u32[]{:S(2)}, u32[]{:S(2)}) collective-permute-start(bf16[256,1024]{1,0:T(8,128)(2,1)S(1)} %bitcast.121), channel_id=1, source_target_pairs={{0,1},{1,0},{2,3},{3,2},{4,5},{5,4},{6,7},{7,6},{8,9},{9,8},{10,11... | collective-permute-start | bytes 1572872 | tf_op jit(solution)/shard_map/ppermute | solution.py:25
  244.6 8.4 %collective-permute-start.19 = (bf16[64,1024]{1,0:T(8,128)(2,1)}, bf16[64,1024]{1,0:T(8,128)(2,1)S(1)}, u32[]{:S(2)}, u32[]{:S(2)}) collective-permute-start(bf16[64,1024]{1,0:T(8,128)(2,1)} %dynamic-slice_bitcast_fusion.2), channel_id=1, source_target_pairs={{0,2},{1,3},{2,0},{3,1},{4,6},{5,7},{6,4},{7,5},{8,10},{9,11},{10,... | collective-permute-start | bytes 393224 | tf_op jit(solution)/shard_map/ppermute | solution.py:25
  246.7 54.7 %collective-permute-start.22 = (bf16[256,1024]{1,0:T(8,128)(2,1)}, bf16[256,1024]{1,0:T(8,128)(2,1)}, u32[]{:S(2)}, u32[]{:S(2)}) collective-permute-start(bf16[256,1024]{1,0:T(8,128)(2,1)} %get-tuple-element.73), channel_id=1, source_target_pairs={{0,16},{1,17},{2,18},{3,19},{4,20},{5,21},{6,22},{7,23},{8,24},{9,... | collective-permute-start | bytes 1572872 | tf_op jit(solution)/shard_map/ppermute | solution.py:479
  249.5 13.9 %all-to-all-start.10 = ((bf16[8,64,256]{2,1,0:T(8,128)(2,1)}), bf16[8,64,256]{2,1,0:T(8,128)(2,1)S(1)}, u32[]{:S(2)}, u32[]{:S(2)}) async-start(bf16[8,64,256]{2,1,0:T(8,128)(2,1)} %bitcast.26), calls=%async_computation.10 | async-start | bytes 524288 | tf_op jit(solution)/shard_map/all_to_all | solution.py:40
  253.8 9.6 %copy-start.29 = (f32[64,640]{1,0:T(8,128)S(1)}, f32[64,640]{1,0:T(8,128)}, u32[]{:S(2)}) copy-start(f32[64,640]{1,0:T(8,128)} %copy-done.28) | copy-start | bytes 491524
  253.8 69.8 %collective-permute-start.20 = (bf16[64,1024]{1,0:T(8,128)(2,1)}, bf16[64,1024]{1,0:T(8,128)(2,1)}, u32[]{:S(2)}, u32[]{:S(2)}) collective-permute-start(bf16[64,1024]{1,0:T(8,128)(2,1)} %fusion.5), channel_id=1, source_target_pairs={{0,16},{1,17},{2,18},{3,19},{4,20},{5,21},{6,22},{7,23},{8,24},{9,... | collective-permute-start | bytes 393224 | tf_op jit(solution)/shard_map/ppermute | solution.py:479
  265.0 17.2 %all-to-all-start.11 = ((bf16[8,64,640]{2,1,0:T(8,128)(2,1)}), bf16[8,64,640]{2,1,0:T(8,128)(2,1)S(1)}, u32[]{:S(2)}, u32[]{:S(2)}) async-start(bf16[8,64,640]{2,1,0:T(8,128)(2,1)} %bitcast.28), calls=%async_computation.11 | async-start | bytes 1310720 | tf_op jit(solution)/shard_map/all_to_all | solution.py:40
  271.7 10.6 %copy-start.12 = (bf16[1024,256]{1,0:T(8,128)(2,1)S(1)}, bf16[1024,256]{1,0:T(8,128)(2,1)}, u32[]{:S(2)}) copy-start(bf16[1024,256]{1,0:T(8,128)(2,1)} %copy-done.11) | copy-start | bytes 1572868
  271.7 10.6 %copy-start.17 = (bf16[256,1024]{1,0:T(8,128)(2,1)S(1)}, bf16[256,1024]{1,0:T(8,128)(2,1)}, u32[]{:S(2)}) copy-start(bf16[256,1024]{1,0:T(8,128)(2,1)} %copy-done.16) | copy-start | bytes 1572868
  273.1 30.4 %collective-permute-start.21 = (bf16[256,1024]{1,0:T(8,128)(2,1)}, bf16[256,1024]{1,0:T(8,128)(2,1)}, u32[]{:S(2)}, u32[]{:S(2)}) collective-permute-start(bf16[256,1024]{1,0:T(8,128)(2,1)} %get-tuple-element.75), channel_id=1, source_target_pairs={{16,0},{17,1},{18,2},{19,3},{20,4},{21,5},{22,6},{23,7},{24,8},{25... | collective-permute-start | bytes 1572872 | tf_op jit(solution)/shard_map/ppermute | solution.py:480
  283.5 2.1 collective-permute-start.12
  285.6 11.1 %collective-permute-start.15 = (bf16[2,64,1024]{2,1,0:T(8,128)(2,1)S(1)}, bf16[2,64,1024]{2,1,0:T(8,128)(2,1)}, u32[]{:S(2)}, u32[]{:S(2)}) collective-permute-start(bf16[2,64,1024]{2,1,0:T(8,128)(2,1)S(1)} %dynamic-slice_bitcast_fusion.1), channel_id=1, source_target_pairs={{0,1},{1,0},{2,3},{3,2},{4,5},{5,4},{6,7},{7,6},{8,9},{9,8},{10,11... | collective-permute-start | bytes 786440 | tf_op jit(solution)/shard_map/ppermute | solution.py:25
  287.0 28.6 %all-to-all-start.12 = ((bf16[8,32,1024]{2,1,0:T(8,128)(2,1)}), bf16[8,32,1024]{2,1,0:T(8,128)(2,1)S(1)}, u32[]{:S(2)}, u32[]{:S(2)}) async-start(bf16[8,32,1024]{2,1,0:T(8,128)(2,1)} %bitcast.30), calls=%async_computation.12 | async-start | bytes 1048576 | tf_op jit(solution)/shard_map/all_to_all | solution.py:34
  296.7 24.6 %collective-permute-start.13 = (bf16[1024,256]{1,0:T(8,128)(2,1)}, bf16[1024,256]{1,0:T(8,128)(2,1)S(1)}, u32[]{:S(2)}, u32[]{:S(2)}) collective-permute-start(bf16[1024,256]{1,0:T(8,128)(2,1)} %get-tuple-element.71), channel_id=1, source_target_pairs={{16,0},{17,1},{18,2},{19,3},{20,4},{21,5},{22,6},{23,7},{24,8},{25... | collective-permute-start | bytes 1572872 | tf_op jit(solution)/shard_map/ppermute | solution.py:480
  301.4 9.4 %collective-permute-start.16 = (bf16[64,1024]{1,0:T(8,128)(2,1)S(1)}, bf16[64,1024]{1,0:T(8,128)(2,1)S(1)}, u32[]{:S(2)}, u32[]{:S(2)}) collective-permute-start(bf16[64,1024]{1,0:T(8,128)(2,1)S(1)} %dynamic-slice_bitcast_fusion.3), channel_id=1, source_target_pairs={{0,2},{1,3},{2,0},{3,1},{4,6},{5,7},{6,4},{7,5},{8,10},{9,11},{10,... | collective-permute-start | bytes 393224 | tf_op jit(solution)/shard_map/ppermute | solution.py:25
  306.0 9.6 %copy-start.25 = (bf16[32,1024]{1,0:T(8,128)(2,1)S(1)}, bf16[32,1024]{1,0:T(8,128)(2,1)}, u32[]{:S(2)}) copy-start(bf16[32,1024]{1,0:T(8,128)(2,1)} %copy-done.24) | copy-start | bytes 196612
  311.5 12.1 %collective-permute-start.17 = (bf16[64,1024]{1,0:T(8,128)(2,1)}, bf16[64,1024]{1,0:T(8,128)(2,1)}, u32[]{:S(2)}, u32[]{:S(2)}) collective-permute-start(bf16[64,1024]{1,0:T(8,128)(2,1)} %fusion.4), channel_id=1, source_target_pairs={{16,0},{17,1},{18,2},{19,3},{20,4},{21,5},{22,6},{23,7},{24,8},{25... | collective-permute-start | bytes 393224 | tf_op jit(solution)/shard_map/ppermute | solution.py:480
  317.6 10.8 %all-to-all-start.13 = ((bf16[16,8,1024]{2,1,0:T(8,128)(2,1)}), bf16[16,8,1024]{2,1,0:T(8,128)(2,1)S(1)}, u32[]{:S(2)}, u32[]{:S(2)}) async-start(bf16[16,8,1024]{2,1,0:T(8,128)(2,1)} %all_to_all.132), calls=%async_computation.14 | async-start | bytes 524288 | tf_op jit(solution)/shard_map/all_to_all | solution.py:488
  (38 other events, 102.0 us)
Sparse Core Ops, SparseCore 0:
  55.4 36.8 all-gather.1
  203.5 58.3 reduce-scatter.1

commit v3 on v2

v3 whole, which is shorter than its diff:
```python
import functools
import math

import jax
import jax.numpy as jnp
from jax import lax
from jax.experimental import pallas as pl
from jax.experimental.pallas import tpu as pltpu
from jax.sharding import PartitionSpec as P

HEAD_SIZE = 128
EPS = 1e-05
THETA = 500000.0
LR = 0.5
BF = jnp.bfloat16
F32 = jnp.float32


def mm(a, b, ca=1, cb=0):
    return lax.dot_general(a, b, (((ca,), (cb,)), ((), ())), preferred_element_type=F32)


def swap(value, axis, mask):
    pairs = [(source, source ^ mask) for source in range(lax.axis_size(axis))]
    return lax.ppermute(value, axis, pairs)


def exchange(value, groups):
    return lax.all_to_all(value, "tensor", 0, 0, axis_index_groups=groups, tiled=True)


def dp_exchange(value):
    return lax.all_to_all(value, "dp", 0, 0, tiled=True)


def tile_rows(value, copies):
    return jnp.broadcast_to(value[None], (copies,) + value.shape).reshape(
        (copies * value.shape[0],) + value.shape[1:]
    )


def call(body, shapes, *operands, flops=0, deps=()):
    outs, specs, kept, sent = [], [], [], []
    for i, (shape, kind, copies) in enumerate(shapes):
        if copies:
            outs.append(jax.ShapeDtypeStruct((copies * shape[0], shape[1]), kind))
            specs.append(pl.BlockSpec(memory_space=pltpu.HBM))
            kept.append(pltpu.VMEM(shape, kind))
            sent.append((i, copies))
        else:
            outs.append(jax.ShapeDtypeStruct(shape, kind))
            specs.append(pl.BlockSpec(shape, lambda i: (0, 0)))
    count = sum(copies for _, copies in sent)
    first = len(operands)
    extra = len(deps)

    def plain(*refs):
        body(*refs[:first], *refs[first + extra :])

    def whole(*refs):
        refs = refs[:first] + refs[first + extra :]
        ends = list(refs[first : first + len(outs)])
        buffers = refs[first + len(outs) :]
        finals = []
        for (i, copies), buffer in zip(sent, buffers):
            finals.append((ends[i], copies, buffer))
            ends[i] = buffer
        body(*refs[:first], *ends)
        moves = []
        for final, copies, buffer in finals:
            rows = buffer.shape[0]
            for k in range(copies):
                where = final.at[pl.ds(k * rows, rows)]
                move = pltpu.make_async_copy(buffer, where, buffers[-1].at[len(moves)])
                move.start()
                moves.append(move)
        for move in moves:
            move.wait()

    moved = sum(x.size * x.dtype.itemsize for x in list(operands) + outs)
    return pl.pallas_call(
        whole if sent else plain,
        out_shape=outs,
        grid=(1,),
        in_specs=[pl.BlockSpec(memory_space=pltpu.VMEM)] * first
        + [pl.BlockSpec(memory_space=pl.ANY)] * extra,
        out_specs=specs,
        scratch_shapes=kept + ([pltpu.SemaphoreType.DMA((count,))] if sent else []),
        compiler_params=pltpu.CompilerParams(vmem_limit_bytes=20 * 2**20),
        cost_estimate=pl.CostEstimate(flops=flops, bytes_accessed=moved, transcendentals=0),
    )(*operands, *deps)


def nothing(*refs):
    pass


def tie(value, *others):
    return pl.pallas_call(
        nothing,
        out_shape=jax.ShapeDtypeStruct(value.shape, value.dtype),
        in_specs=[pl.BlockSpec(memory_space=pl.ANY)] * (1 + len(others)),
        out_specs=pl.BlockSpec(memory_space=pl.ANY),
        input_output_aliases={0: 0},
    )(value, *others)


def one_hot(target):
    size = target.shape[1]
    row = lax.broadcasted_iota(jnp.int32, (size, size), 0)
    return jnp.where(row == target, 1.0, 0.0).astype(BF)


def pair_columns(column):
    high = column.astype(BF).astype(F32)
    lane = lax.broadcasted_iota(jnp.int32, (column.shape[0], 128), 1)
    return jnp.where(lane == 0, high, jnp.where(lane == 1, column - high, 0.0)).astype(BF)


def project_body(tokens, target, mine, other, wq, wkv, *rest):
    half = mine.shape[0]
    nq = wq.shape[1]
    parts = []
    for rows in (mine[...], other[...]):
        wide = rows.astype(F32)
        squares = jnp.sum(wide * wide, axis=1, keepdims=True)
        parts.append(
            jnp.concatenate(
                [mm(rows, wq[...]).astype(BF), mm(rows, wkv[...], 1, 1).astype(BF), pair_columns(squares)],
                axis=1,
            )
        )
    order = one_hot(target[...])
    value = (mm(order[:, :half], parts[0]) + mm(order[:, half:], parts[1])).astype(BF)
    out = rest[-1]
    lot = nq // 2
    for k in range(out.shape[0] // tokens):
        rows = slice((k // 2) * tokens, (k // 2 + 1) * tokens)
        cols = slice((k % 2) * lot, (k % 2 + 1) * lot)
        pieces = [value[rows, cols], value[rows, nq:]]
        if len(rest) > 1:
            pieces.append(rest[0][rows, cols])
        out[k * tokens : (k + 1) * tokens] = jnp.concatenate(pieces, axis=1)


def project(tokens, target, mine, other, wq, wkv, *extra):
    rows = 2 * mine.shape[0]
    cols = wq.shape[1] + wkv.shape[0] + 128
    flops = 2 * rows * cols * (mine.shape[1] + rows)
    cols = cols - wq.shape[1] // 2 + sum(x.shape[1] // 2 for x in extra)
    return call(
        functools.partial(project_body, tokens),
        [((2 * rows, cols), BF, 1)],
        target,
        mine,
        other,
        wq,
        wkv,
        *extra,
        flops=flops,
    )[0]


def mixed_grad_body(tokens, target, mine, other, wo, out):
    half = mine.shape[0]
    parts = [mm(x[...], wo[...], 1, 1).astype(BF) for x in (mine, other)]
    order = one_hot(target[...])
    value = (mm(order[:, :half], parts[0]) + mm(order[:, half:], parts[1])).astype(BF)
    if tokens is None:
        out[...] = value
        return
    lot = value.shape[1] // 2
    for k in range(out.shape[0] // tokens):
        rows = slice((k // 2) * tokens, (k // 2 + 1) * tokens)
        out[k * tokens : (k + 1) * tokens] = value[rows, (k % 2) * lot : (k % 2 + 1) * lot]


def mixed_grad(tokens, target, mine, other, wo):
    rows = target.shape[1]
    cols = wo.shape[0]
    flops = 2 * rows * cols * (wo.shape[1] + rows)
    shape = (rows, cols) if tokens is None else (2 * rows, cols // 2)
    body = functools.partial(mixed_grad_body, tokens)
    copies = 0 if tokens is None else 1
    return call(body, [(shape, BF, copies)], target, mine, other, wo, flops=flops)[0]


def side_by_side(got, tokens, lo, hi):
    pairs = []
    for k in range(0, got.shape[0] // tokens, 2):
        left = got[k * tokens : (k + 1) * tokens, lo:hi]
        right = got[(k + 1) * tokens : (k + 2) * tokens, lo:hi]
        pairs.append(jnp.concatenate([left, right], axis=1))
    return jnp.concatenate(pairs, axis=0)


def summed(got, tokens, lo, hi):
    pairs = []
    for k in range(0, got.shape[0] // tokens, 2):
        left = got[k * tokens : (k + 1) * tokens, lo:hi].astype(F32)
        pairs.append(left + got[(k + 1) * tokens : (k + 2) * tokens, lo:hi].astype(F32))
    return jnp.concatenate(pairs, axis=0)


def out_body(tokens, target, got, wo, rows_out, other_out, mine_out):
    half = mine_out.shape[0]
    held = side_by_side(got, tokens, 0, got.shape[1])
    rows = mm(one_hot(target[...]), held, 0, 0).astype(BF)
    rows_out[...] = rows
    other_out[...] = mm(rows[half:], wo[...]).astype(BF)
    mine_out[...] = mm(rows[:half], wo[...])


def out_project(tokens, target, got, wo, *deps):
    rows, cols = got.shape[0] // 2, got.shape[1] * 2
    feats = wo.shape[1]
    return call(
        functools.partial(out_body, tokens),
        [((rows, cols), BF, 0), ((rows // 2, feats), BF, 0), ((rows // 2, feats), F32, 0)],
        target,
        got,
        wo,
        flops=2 * rows * cols * (rows + feats),
        deps=deps,
    )


def back_body(tokens, target, got, mine, other, wq, wkv, rows_out, other_out, mine_out):
    half = mine.shape[0]
    nq = wq.shape[1]
    lot = nq // 2
    end = lot + wkv.shape[0]
    coef = jnp.sum(summed(got, tokens, end, end + 128), axis=1, keepdims=True)
    held = jnp.concatenate(
        [
            side_by_side(got, tokens, 0, lot),
            summed(got, tokens, lot, end).astype(BF),
            pair_columns(coef),
        ],
        axis=1,
    )
    rows = mm(one_hot(target[...]), held, 0, 0)
    end = nq + wkv.shape[0]
    coef = jnp.sum(rows[:, end:], axis=1, keepdims=True)
    low = rows[:, :end].astype(BF)
    rows_out[...] = low

    def term(part, c, kept):
        value = mm(part[:, :nq], wq[...], 1, 1) + mm(part[:, nq:], wkv[...])
        return value - kept[...].astype(F32) * c

    other_out[...] = term(low[half:], coef[half:], other).astype(BF)
    mine_out[...] = term(low[:half], coef[:half], mine)


def back_project(tokens, target, got, mine, other, wq, wkv):
    rows = 2 * mine.shape[0]
    cols = wq.shape[1] + wkv.shape[0]
    feats = mine.shape[1]
    return call(
        functools.partial(back_body, tokens),
        [((rows, cols), BF, 0), ((rows // 2, feats), BF, 0), ((rows // 2, feats), F32, 0)],
        target,
        got,
        mine,
        other,
        wq,
        wkv,
        flops=2 * rows * (cols + 128) * (rows + feats),
    )


def settle_body(count, got, held, *outs):
    rows = held.shape[0]
    total = held[...].astype(F32)
    for i in range(count):
        total = total + got[i * rows : (i + 1) * rows].astype(F32)
    low = total.astype(BF)
    for out in outs:
        out[...] = low


def settle(got, held, *copies):
    count = got.shape[0] // held.shape[0]
    return call(
        functools.partial(settle_body, count),
        [(held.shape, BF, k) for k in copies],
        got,
        held,
    )


def copy_body(value, out):
    out[...] = value[...]


def turn(value, cosine, sine):
    return value * cosine + pltpu.roll(value, HEAD_SIZE // 2, 1) * sine


def heads_down(value):
    count = value.shape[1] // HEAD_SIZE
    return jnp.concatenate(
        [value[:, i * HEAD_SIZE : (i + 1) * HEAD_SIZE] for i in range(count)], axis=0
    )


def heads_across(value, tokens):
    count = value.shape[0] // tokens
    return jnp.concatenate([value[i * tokens : (i + 1) * tokens] for i in range(count)], axis=1)


def add_parts(ref, tokens):
    total = ref[:tokens].astype(F32)
    for i in range(1, ref.shape[0] // tokens):
        total = total + ref[i * tokens : (i + 1) * tokens].astype(F32)
    return total


def look(total, nq, width, cosine, sine, mask):
    tokens = total.shape[0]
    heads = nq // HEAD_SIZE
    end = nq + 2 * HEAD_SIZE
    squares = jnp.sum(total[:, end:], axis=1, keepdims=True)
    scale = lax.rsqrt(squares / width + EPS)
    wide_cos = jnp.concatenate([cosine] * heads, axis=0)
    wide_sin = jnp.concatenate([sine] * heads, axis=0)
    queries = turn(heads_down(total[:, :nq] * scale), wide_cos, wide_sin).astype(BF)
    kv = (total[:, nq:end] * scale).astype(BF)
    keys = turn(kv[:, :HEAD_SIZE].astype(F32), cosine, sine).astype(BF)
    values = kv[:, HEAD_SIZE:]
    scores = mm(queries, keys, 1, 1) * (1.0 / math.sqrt(HEAD_SIZE))
    weights = jnp.exp(jnp.where(mask > 0.0, scores, -1e30))
    probs = weights / jnp.sum(weights, axis=1, keepdims=True)
    low = probs.astype(BF)
    return scale, queries, keys, values, probs, low, wide_cos, wide_sin


def look_back(total, d_mixed, nq, width, cosine, sine, seen):
    scale, queries, keys, values, probs, low, wide_cos, wide_sin = seen
    tokens = total.shape[0]
    end = nq + 2 * HEAD_SIZE
    dm = heads_down(d_mixed).astype(BF)
    d_probs = mm(dm, values, 1, 1)
    d_values = mm(low, dm, 0, 0)
    d_scores = probs * (d_probs - jnp.sum(probs * d_probs, axis=1, keepdims=True))
    d_scores = (d_scores * (1.0 / math.sqrt(HEAD_SIZE))).astype(BF)
    dq = turn(mm(d_scores, keys), wide_cos, -wide_sin)
    dk = turn(mm(d_scores, queries, 0, 0), cosine, -sine)
    dq = (heads_across(dq, tokens) * scale).astype(BF)
    dkv = (jnp.concatenate([dk, d_values], axis=1) * scale).astype(BF)
    both = jnp.concatenate([dq, dkv], axis=1)
    dot = jnp.sum(both.astype(F32) * total[:, :end], axis=1, keepdims=True)
    return jnp.concatenate([both, pair_columns(dot * scale * scale / width)], axis=1)


def forward_body(nq, width, got, cosine, sine, mask, mixed_out, total_out):
    tokens = cosine.shape[0]
    total = add_parts(got, tokens)
    total_out[...] = total
    seen = look(total, nq, width, cosine[...], sine[...], mask[...])
    mixed_out[...] = heads_across(mm(seen[5], seen[3]), tokens).astype(BF)


def both_body(nq, width, got, cosine, sine, mask, sent_out):
    tokens = cosine.shape[0]
    total = add_parts(got, tokens)
    d_mixed = total[:, total.shape[1] - nq :]
    total = total[:, : total.shape[1] - nq]
    seen = look(total, nq, width, cosine[...], sine[...], mask[...])
    mixed = heads_across(mm(seen[5], seen[3]), tokens).astype(BF)
    sent = look_back(total, d_mixed, nq, width, cosine[...], sine[...], seen)
    sent_out[...] = jnp.concatenate([sent, mixed], axis=1)


def backward_body(nq, width, total, grads, cosine, sine, mask, sent_out):
    tokens = cosine.shape[0]
    d_mixed = add_parts(grads, tokens)
    seen = look(total[...], nq, width, cosine[...], sine[...], mask[...])
    sent_out[...] = look_back(total[...], d_mixed, nq, width, cosine[...], sine[...], seen)


def shards(
    inputs,
    positions,
    out_grads,
    query_weight,
    key_value_weight,
    out_weight,
    query_stale,
    key_value_previous_gradient,
    out_stale,
):
    n_dp = lax.axis_size("dp")
    ranks = lax.axis_size("tensor")
    pipe = lax.axis_index("pipe")
    rank = lax.axis_index("tensor")
    core = rank % 2
    odd = (rank // 2) % 2
    far_pair = rank // 4
    first = pipe == 0
    even = odd == 0
    micro, own, width = inputs.shape
    feats = width // n_dp
    block = own * ranks
    some = n_dp // 2
    tokens = some * block
    half = tokens // 2
    slab = n_dp * own
    chips = [list(range(c, ranks, 2)) for c in range(2)]
    alike = [list(range(c, ranks, 4)) for c in range(4)]

    query_new = (query_weight.astype(F32) - LR * query_stale).astype(BF)
    kv_new = (key_value_weight.astype(F32) - LR * key_value_previous_gradient).astype(BF)
    out_new = (out_weight.astype(F32) - LR * out_stale).astype(BF)

    def after(value, *others):
        return lax.optimization_barrier((value,) + others)[0]

    def arrange(own_part):
        other = swap(own_part, "pipe", 1)
        return jnp.where(first, own_part, other), jnp.where(first, other, own_part)

    def in_order(flag, own_part, other, axis):
        return jnp.where(
            flag,
            jnp.concatenate([own_part, other], axis=axis),
            jnp.concatenate([other, own_part], axis=axis),
        )

    def of_pair(own_part, other, axis):
        return in_order(even, own_part, other, axis)

    def head_half(own_part):
        return in_order(core == 0, own_part, swap(own_part, "tensor", 1), 0)

    def with_far(own_part, axis):
        return of_pair(own_part, swap(own_part, "tensor", 2), axis)

    far_q = swap(query_new[0], "tensor", 2)
    kv_here, kv_next = arrange(kv_new[0].T)
    pair0 = head_half(kv_here)

    at = lax.broadcasted_iota(jnp.int32, (1, tokens), 1)
    inside = at % half
    chip = inside // (some * own)
    rest = inside % (some * own)
    target = (rest // own) * block + (chip * 2 + ((at // half) ^ core)) * own + rest % own

    size = lax.axis_size("pipe")

    def source(d, p, r):
        b = some * ((r // 2) % 2) + d // 2
        return (b * size + p) * ranks + (2 * (r // 4) + d % 2) * 2 + r % 2

    spots = lax.ppermute(
        positions,
        ("dp", "pipe", "tensor"),
        [
            (source(d, p, r), (d * size + p) * ranks + r)
            for d in range(n_dp)
            for p in range(size)
            for r in range(ranks)
        ],
    )
    spots = lax.dynamic_index_in_dim(spots, pipe, 0, keepdims=False)
    freqs = THETA ** (-2.0 * jnp.arange(HEAD_SIZE // 2, dtype=F32) / HEAD_SIZE)
    angles = spots.astype(F32)[:, None] * freqs[None, :]
    cosine = jnp.concatenate([jnp.cos(angles)] * 2, axis=1)
    sine = jnp.concatenate([-jnp.sin(angles), jnp.sin(angles)], axis=1)
    index = jnp.arange(block, dtype=jnp.int32)
    visible = (index[None, :] <= index[:, None]) & (index[None, :] >= (index - spots)[:, None])
    nq = query_new.shape[2]
    mask = jnp.concatenate([visible.astype(F32)] * (nq // HEAD_SIZE), axis=0)

    start = jnp.stack(
        [
            lax.dynamic_index_in_dim(inputs, pipe, 0, keepdims=False),
            lax.dynamic_index_in_dim(out_grads, pipe, 0, keepdims=False),
        ]
    )
    start = start.reshape(2, own, n_dp, feats).transpose(2, 0, 1, 3).reshape(2 * slab, feats)
    start = dp_exchange(start)
    wkv0 = with_far(pair0, 0)
    start = start.reshape(2, some, 2, own, feats).transpose(0, 2, 1, 3, 4)
    start = start.reshape(2 * slab, feats)

    def gather_z(tiled):
        mine = exchange(tiled, alike)
        return mine, swap(mine, "tensor", 1)

    def add_pair(part_mine, part_other):
        moved = swap(part_other, "tensor", 1)
        return (part_mine + moved.astype(F32)).astype(BF)

    def head_rows(columns):
        return [((block, columns), BF, n_dp)]

    sent_columns = nq + 2 * HEAD_SIZE + 128
    near_chips = ranks // 4

    begin = call(copy_body, [(start.shape, BF, near_chips)], start, deps=[wkv0])[0]
    wq0, wq1 = arrange(of_pair(query_new[0], tie(far_q, begin), 1))
    begin = exchange(begin, chips)
    begin = begin.reshape(ranks // 2, 2, some * own, feats)
    h0_mine = after(begin[:, 0].reshape(half, feats), wq0, wkv0, wq1, out_new)
    g1_mine = begin[:, 1].reshape(half, feats)
    h0_other = swap(h0_mine, "tensor", 1)
    part = project(block, target, h0_mine, h0_other, wq0, wkv0)
    g1_sent = after(g1_mine, part)
    g1_other = swap(g1_sent, "tensor", 1)
    out_here, out_next = arrange(after(out_new[0], wq0))
    got = dp_exchange(part)
    wo0 = with_far(after(out_here, part), 0)
    wkv1 = with_far(after(head_half(kv_next), part), 0)
    h0 = lax.dynamic_slice_in_dim(h0_mine, far_pair * slab, slab, 0)
    g1 = lax.dynamic_slice_in_dim(g1_mine, far_pair * slab, slab, 0)
    mixed0, total0 = call(
        functools.partial(forward_body, nq, width),
        head_rows(nq) + [((block, sent_columns), F32, 1)],
        got,
        cosine,
        sine,
        mask,
    )
    all_m0, far0, near0 = out_project(block, target, dp_exchange(mixed0), wo0, wkv1)
    wo1 = of_pair(out_next, swap(tie(out_next, mixed0), "tensor", 2), 0)
    reduced = exchange(add_pair(near0, far0), alike)
    h1, h1_tiled = settle(after(reduced, g1_other), h0, 0, near_chips)

    dm1 = mixed_grad(None, target, g1_mine, g1_other, wo1)
    h1_mine = after(exchange(h1_tiled, alike), dm1)
    h1_other = swap(h1_mine, "tensor", 1)
    got = dp_exchange(project(block, target, h1_mine, h1_other, wq1, wkv1, dm1))
    sent1 = call(
        functools.partial(both_body, nq, width),
        head_rows(sent_columns + nq),
        got,
        cosine,
        sine,
        mask,
    )[0]
    got1 = dp_exchange(sent1)
    rows1, far1, near1 = back_project(block, target, got1, h1_mine, h1_other, wq1, wkv1)
    sent_back = add_pair(near1, far1)
    rows1 = tie(rows1, sent_back)
    g0, g0_tiled = settle(exchange(sent_back, alike), g1, 0, near_chips)

    def halves(rows):
        cut = [rows[:, :nq], rows[:, nq : 2 * nq]]
        return jnp.where(even, cut[0], cut[1]), jnp.where(even, cut[1], cut[0])

    def grads_q(rows, mine, other):
        return [
            mm(mine, x[:half], 0, 0) + mm(other, x[half:], 0, 0) for x in halves(rows[:, : 2 * nq])
        ]

    def grads_o(rows, mine, other):
        return [mm(x[:half], mine, 0, 0) + mm(x[half:], other, 0, 0) for x in halves(rows)]

    def grads_kv(rows, mine, other):
        low = rows[:, 2 * nq :]
        return mm(low[:half], mine, 0, 0) + mm(low[half:], other, 0, 0)

    def with_partner(own_grad, partner_grad, early, late):
        moved = swap(tie(partner_grad.astype(BF), early), "tensor", 2)
        return own_grad + tie(moved, late).astype(F32)

    gq1 = grads_q(rows1, h1_mine, h1_other)
    gkv1 = grads_kv(rows1, h1_mine, h1_other)
    all_m1, far_o, near_o = out_project(block, target, got1[:, sent_columns:], wo1, sent_back)
    pair1 = add_pair(near_o, far_o)
    go1 = grads_o(all_m1, g1_mine, g1_other)
    g0_mine = after(exchange(g0_tiled, alike), *gq1, *go1, gkv1, pair1)
    g0_other = swap(g0_mine, "tensor", 1)
    dm0 = mixed_grad(block, target, g0_mine, g0_other, wo0)
    gkv1 = after(gkv1, dm0)
    got_dm0 = dp_exchange(dm0)
    sent0 = call(
        functools.partial(backward_body, nq, width),
        head_rows(sent_columns),
        total0,
        got_dm0,
        cosine,
        sine,
        mask,
    )[0]
    go0 = grads_o(after(all_m0, dm0), g0_mine, g0_other)

    def at_home(rows):
        parts = rows.reshape(2, -1, feats)
        keep = lax.dynamic_index_in_dim(parts, odd, 0, keepdims=False)
        send = lax.dynamic_index_in_dim(parts, 1 - odd, 0, keepdims=False)
        return in_order(even, keep, swap(send, "tensor", 2), 0)

    h1_home, g0_home = at_home(after(h1, dm0)), at_home(after(g0, dm0))
    rows0, far, near = back_project(
        block, target, dp_exchange(sent0), h0_mine, h0_other, wq0, wkv0
    )
    both = [x.reshape(ranks // 2, -1, feats) for x in (add_pair(near, far), pair1)]
    both = jnp.concatenate(both, axis=1).reshape(2 * half, feats)
    rows0 = tie(rows0, both)
    gq0 = grads_q(rows0, h0_mine, h0_other)
    gkv0 = grads_kv(rows0, h0_mine, h0_other)
    last = exchange(both, chips)
    held = [x.reshape(2, -1, feats) for x in (g0_home, h1_home)]
    ends = settle(last, jnp.concatenate(held, axis=1).reshape(2 * slab, feats), 0)[0]
    ends = ends.reshape(2, 2, some * own, feats)
    gi, h2 = ends[:, 0].reshape(slab, feats), ends[:, 1].reshape(slab, feats)

    def home(grad0, grad1, *late):
        to1 = lax.ppermute(grad1.astype(BF), "pipe", [(0, 1)])
        to0 = lax.ppermute(grad0.astype(BF), "pipe", [(1, 0)])
        to0 = tie(to0, *late) if late else to0
        return jnp.where(first, grad0 + to0.astype(F32), grad1 + to1.astype(F32))

    def kv_sums(grad, early):
        quarters = grad.astype(BF).reshape(2, 2, grad.shape[0] // 4, feats)
        keep = lax.dynamic_index_in_dim(quarters, core, 1, keepdims=False)
        send = lax.dynamic_index_in_dim(quarters, 1 - core, 1, keepdims=False)
        return keep.astype(F32) + swap(after(send, early), "tensor", 1).astype(F32)

    sums = [
        with_partner(*gq1, dm0, sent0),
        with_partner(*go1, dm0, sent0),
        with_partner(*go0, sent0, both),
        with_partner(*gq0, both, last),
    ]
    query_grad = home(sums[3], sums[0])
    out_grad = home(sums[2], sums[1])
    kv_pair = home(kv_sums(gkv0, both), kv_sums(gkv1, got_dm0), sums[3]).astype(BF)
    keep = lax.dynamic_index_in_dim(kv_pair, odd, 0, keepdims=False)
    send = lax.dynamic_index_in_dim(kv_pair, 1 - odd, 0, keepdims=False)
    kv_grad = (keep.astype(F32) + swap(after(send, last), "tensor", 2).astype(F32)).T

    ends = jnp.stack([h1_home, gi, h2, g0_home])
    ends = ends.reshape(2, 2, n_dp, own, feats).transpose(2, 0, 1, 3, 4)
    ends = lax.all_to_all(
        ends.reshape(n_dp * 4 * own, feats), ("dp", "pipe"), 0, 0, tiled=True
    ).reshape(n_dp, micro, 2, own, feats)
    rows = ends.transpose(2, 1, 3, 0, 4).reshape(2, micro, own, width)
    return (
        rows[0][None],
        rows[1][None],
        query_new,
        kv_new,
        out_new,
        query_grad[None],
        kv_grad[None],
        out_grad[None],
    )


def solution(mesh):
    placed = (
        P(None, ("dp", "tensor"), None),
        P(None, "dp"),
        P(None, ("dp", "tensor"), None),
        P("pipe", "dp", "tensor"),
        P("pipe", "dp", "tensor"),
        P("pipe", "tensor", "dp"),
        P("pipe", "dp", "tensor"),
        P("pipe", "dp", "tensor"),
        P("pipe", "tensor", "dp"),
    )
    return jax.shard_map(
        shards,
        mesh=mesh,
        in_specs=placed,
        out_specs=(
            P("pipe", None, ("dp", "tensor"), None),
            P("pipe", None, ("dp", "tensor"), None),
            P("pipe", "dp", "tensor"),
            P("pipe", "dp", "tensor"),
            P("pipe", "tensor", "dp"),
            P("pipe", "dp", "tensor"),
            P("pipe", "dp", "tensor"),
            P("pipe", "tensor", "dp"),
        ),
        check_vma=False,
    )
```

time: 339 us -> 338 us (level)
  blocking collectives: 74.4 us -> 37 us
  waiting for transfers between devices: 107 us -> 71.1 us
  starting transfers between devices: 75.8 us -> 107 us
  other arithmetic: 20.9 us -> 43.7 us
  matrix products: 13.5 us -> 27.5 us
  between operations: 15 us -> 1.69 us
  local copies, waits for them, and re-layouts: 15 us -> 22.5 us
  Pallas kernels: 15.8 us -> 22.9 us
    all_to_all x5 -> x6, waiting for transfers between devices: 48.4 us -> 19.2 us  [exchange(): lax.all_to_all(value, 'tensor', 0, 0, axis_index_groups=groups, tiled=True)]
    all_to_all x1 -> x0, blocking collectives: 22 us -> none  [z_exchange(): lax.all_to_all(value, 'tensor', 0, 0, axis_index_groups=same_core(size),...]
    all_to_all x3 -> x2, blocking collectives: 52.4 us -> 37 us  [dp_exchange(): return lax.all_to_all(value, 'dp', 0, 0, tiled=True)]
    dot_general x11 -> x20, matrix products: 13.5 us -> 27.5 us  [mm(): lax.dot_general(a, b, (((ca,), (cb,)), ((), ())), preferred_element_type=...]
    select_n x4 -> x15, other arithmetic: 2.43 us -> 16.3 us  [the longest x11 14.3 us: in_order(): jnp.where(flag, jnp.concatenate([own_part, other], axis=axis), jnp.concat...]
    all_to_all x4 -> x5, starting transfers between devices: 16.8 us -> 25.3 us  [dp_exchange(): return lax.all_to_all(value, 'dp', 0, 0, tiled=True)]
    ppermute x17 -> x27, starting transfers between devices: 11.1 us -> 19.5 us  [swap(): return lax.ppermute(value, axis, pairs)]
    all_to_all x5 -> x6, starting transfers between devices: 27 us -> 34.5 us  [exchange(): lax.all_to_all(value, 'tensor', 0, 0, axis_index_groups=groups, tiled=True)]
  transfers between devices with their start and end apart: 35 -> 46, of which waited for: 17 -> 18; matrix products, arithmetic and copies ran while one was open for 11% -> 22% of each run, Pallas kernels for 3% -> 4%
where the time goes in v3:
time: 338 us; the launch traced here: 333 us
  starting transfers between devices  107 us (32%)
  waiting for transfers between devices  71.1 us (21%)
  other arithmetic  43.7 us (13%)
  blocking collectives  37 us (11%)
  matrix products  27.5 us (8%)
  Pallas kernels  22.9 us (7%)
  local copies, waits for them, and re-layouts  22.5 us (7%)
    all_to_all x2, blocking collectives, dp_exchange(): return lax.all_to_all(value, 'dp', 0, 0, tiled=True)  37 us
    all_to_all x6, starting transfers between devices, exchange(): lax.all_to_all(value, 'tensor', 0, 0, axis_index_groups=groups, tiled=True)  34.5 us
    dot_general x20, matrix products, mm(): lax.dot_general(a, b, (((ca,), (cb,)), ((), ())), preferred_element_type=...  27.5 us
    all_to_all x5, waiting for transfers between devices, dp_exchange(): return lax.all_to_all(value, 'dp', 0, 0, tiled=True)  26 us
    all_to_all x5, starting transfers between devices, dp_exchange(): return lax.all_to_all(value, 'dp', 0, 0, tiled=True)  25.3 us
    pallas_call x15, Pallas kernels, call(): pl.pallas_call(whole if sent else plain, out_shape=outs, grid=(1,), in_sp...  22.8 us
    ppermute x27, waiting for transfers between devices, swap(): return lax.ppermute(value, axis, pairs)  20.1 us
    ppermute x27, starting transfers between devices, swap(): return lax.ppermute(value, axis, pairs)  19.5 us
  transfers between devices with their start and end apart: 46, of which 18 were waited for; matrix products, arithmetic and copies ran while one was open for 22% of the time, Pallas kernels for 4%

profile of v3, /device:TPU:8, one launch (start us, length us, event | category | flops | bytes accessed | tf_op | source)
XLA Modules:
  0.0 333.4 jit_solution(9607278675702811069)
XLA Ops:
  1.7 2.3 collective-permute-start
  8.5 2.0 collective-permute-start.2
  11.4 6.0 %all-to-all-start = ((bf16[8,8,1024]{2,1,0:T(8,128)(2,1)}), bf16[8,8,1024]{2,1,0:T(8,128)(2,1)S(1)}, u32[]{:S(2)}, u32[]{:S(2)}) async-start(bf16[8,8,1024]{2,1,0:T(8,128)(2,1)} %copy.41), calls=%async_computation | async-start | bytes 262144 | tf_op jit(solution)/shard_map/all_to_all | solution.py:33
  17.5 8.1 %all-to-all-done = bf16[8,8,1024]{2,1,0:T(8,128)(2,1)S(1)} async-done(((bf16[8,8,1024]{2,1,0:T(8,128)(2,1)}), bf16[8,8,1024]{2,1,0:T(8,128)(2,1)S(1)}, u32[]{:S(2)}, u32[]{:S(2)}) %all-to-all-start) | async-done | bytes 131104 | tf_op jit(solution)/shard_map/all_to_all | solution.py:33
  31.3 9.7 %all-to-all-start.1 = ((bf16[8,32,1024]{2,1,0:T(8,128)(2,1)}), bf16[8,32,1024]{2,1,0:T(8,128)(2,1)S(1)}, u32[]{:S(2)}, u32[]{:S(2)}) async-start(bf16[8,32,1024]{2,1,0:T(8,128)(2,1)} %bitcast.6), calls=%async_computation.1 | async-start | bytes 1048576 | tf_op jit(solution)/shard_map/all_to_all | solution.py:29
  41.0 2.0 subtract_convert_fusion
  43.1 9.8 %collective-permute-done.4 = bf16[1024,512]{1,0:T(8,128)(2,1)} collective-permute-done((bf16[1024,512]{1,0:T(8,128)(2,1)S(1)}, bf16[1024,512]{1,0:T(8,128)(2,1)}, u32[]{:S(2)}, u32[]{:S(2)}) %collective-permute-start.4) | collective-permute-done | bytes 1048608 | tf_op jit(solution)/shard_map/ppermute | solution.py:25
  61.7 4.7 %all-to-all-start.2 = ((bf16[8,64,640]{2,1,0:T(8,128)(2,1)}), bf16[8,64,640]{2,1,0:T(8,128)(2,1)S(1)}, u32[]{:S(2)}, u32[]{:S(2)}) async-start(bf16[8,64,640]{2,1,0:T(8,128)(2,1)} %bitcast.142), calls=%async_computation.2 | async-start | bytes 1310720 | tf_op jit(solution)/shard_map/all_to_all | solution.py:33
  66.9 2.3 broadcast_select_fusion.2
  70.8 9.2 %all-to-all-done.2 = bf16[8,64,640]{2,1,0:T(8,128)(2,1)S(1)} async-done(((bf16[8,64,640]{2,1,0:T(8,128)(2,1)}), bf16[8,64,640]{2,1,0:T(8,128)(2,1)S(1)}, u32[]{:S(2)}, u32[]{:S(2)}) %all-to-all-start.2) | async-done | bytes 655392 | tf_op jit(solution)/shard_map/all_to_all | solution.py:33
  82.1 4.0 %all-to-all-start.3 = ((bf16[8,64,256]{2,1,0:T(8,128)(2,1)}), bf16[8,64,256]{2,1,0:T(8,128)(2,1)}, u32[]{:S(2)}, u32[]{:S(2)}) async-start(bf16[8,64,256]{2,1,0:T(8,128)(2,1)} %bitcast.13), calls=%async_computation.3 | async-start | bytes 524288 | tf_op jit(solution)/shard_map/all_to_all | solution.py:33
  86.1 2.2 maximum_select_fusion.4.refs_3_.refs_4_.refs_5_
  88.4 2.0 maximum_select_fusion.1.refs_2_.refs_3_
  90.3 4.8 %all-to-all-done.3 = bf16[8,64,256]{2,1,0:T(8,128)(2,1)} async-done(((bf16[8,64,256]{2,1,0:T(8,128)(2,1)}), bf16[8,64,256]{2,1,0:T(8,128)(2,1)}, u32[]{:S(2)}, u32[]{:S(2)}) %all-to-all-start.3) | async-done | bytes 262176 | tf_op jit(solution)/shard_map/all_to_all | solution.py:33
  100.1 6.8 %all-to-all-start.4 = ((bf16[4,32,1024]{2,1,0:T(8,128)(2,1)}), bf16[4,32,1024]{2,1,0:T(8,128)(2,1)}, u32[]{:S(2)}, u32[]{:S(2)}) async-start(bf16[4,32,1024]{2,1,0:T(8,128)(2,1)} %bitcast.162), calls=%async_computation.4 | async-start | bytes 524288 | tf_op jit(solution)/shard_map/all_to_all | solution.py:29
  111.8 7.3 %all-to-all-done.4 = bf16[4,32,1024]{2,1,0:T(8,128)(2,1)} async-done(((bf16[4,32,1024]{2,1,0:T(8,128)(2,1)}), bf16[4,32,1024]{2,1,0:T(8,128)(2,1)}, u32[]{:S(2)}, u32[]{:S(2)}) %all-to-all-start.4) | async-done | bytes 262176 | tf_op jit(solution)/shard_map/all_to_all | solution.py:29
  122.6 4.1 %all-to-all-start.5 = ((bf16[4,32,1024]{2,1,0:T(8,128)(2,1)}), bf16[4,32,1024]{2,1,0:T(8,128)(2,1)}, u32[]{:S(2)}, u32[]{:S(2)}) async-start(bf16[4,32,1024]{2,1,0:T(8,128)(2,1)} %bitcast.148), calls=%async_computation.5 | async-start | bytes 524288 | tf_op jit(solution)/shard_map/all_to_all | solution.py:29
  126.7 2.0 maximum_select_fusion.2.refs_3_.refs_2_
  128.8 2.0 shard_map.159.refs_5_
  132.5 3.9 %all-to-all-done.5 = bf16[4,32,1024]{2,1,0:T(8,128)(2,1)} async-done(((bf16[4,32,1024]{2,1,0:T(8,128)(2,1)}), bf16[4,32,1024]{2,1,0:T(8,128)(2,1)}, u32[]{:S(2)}, u32[]{:S(2)}) %all-to-all-start.5) | async-done | bytes 262176 | tf_op jit(solution)/shard_map/all_to_all | solution.py:29
  140.2 2.7 shard_map.160
  142.8 18.8 %all_to_all.148 = bf16[8,64,896]{2,1,0:T(8,128)(2,1)S(1)} all-to-all(bf16[8,64,896]{2,1,0:T(8,128)(2,1)S(1)} %bitcast.138), channel_id=1, replica_groups=mesh['dp'=8,'pipe'=2,'tensor'=16] {'dp'}, dimensions={0} | all-to-all | bytes 1835008 | tf_op jit(solution)/shard_map/all_to_all | solution.py:33
  161.6 2.2 shard_map.161
  163.9 18.2 %all_to_all.149 = bf16[8,64,896]{2,1,0:T(8,128)(2,1)S(1)} all-to-all(bf16[8,64,896]{2,1,0:T(8,128)(2,1)S(1)} %bitcast.140), channel_id=1, replica_groups=mesh['dp'=8,'pipe'=2,'tensor'=16] {'dp'}, dimensions={0} | all-to-all | bytes 1835008 | tf_op jit(solution)/shard_map/all_to_all | solution.py:33
  182.0 2.2 shard_map.162
  186.7 3.5 %all-to-all-start.8 = ((bf16[4,32,1024]{2,1,0:T(8,128)(2,1)}), bf16[4,32,1024]{2,1,0:T(8,128)(2,1)S(1)}, u32[]{:S(2)}, u32[]{:S(2)}) async-start(bf16[4,32,1024]{2,1,0:T(8,128)(2,1)} %bitcast.25), calls=%async_computation.8 | async-start | bytes 524288 | tf_op jit(solution)/shard_map/all_to_all | solution.py:29
  191.5 2.2 convolution_add_fusion.9
  194.1 2.2 convolution_add_fusion.8.refs_0_
  199.1 2.1 convolution_add_fusion.5
  202.9 2.2 convolution_add_fusion.7
  206.0 6.9 %all-to-all-start.9 = ((bf16[4,32,1024]{2,1,0:T(8,128)(2,1)}), bf16[4,32,1024]{2,1,0:T(8,128)(2,1)S(1)}, u32[]{:S(2)}, u32[]{:S(2)}) async-start(bf16[4,32,1024]{2,1,0:T(8,128)(2,1)} %bitcast.27), calls=%async_computation.9 | async-start | bytes 524288 | tf_op jit(solution)/shard_map/all_to_all | solution.py:29
  212.9 2.5 convolution_add_fusion.6.refs_0_
  217.1 7.4 %all-to-all-done.9 = bf16[4,32,1024]{2,1,0:T(8,128)(2,1)S(1)} async-done(((bf16[4,32,1024]{2,1,0:T(8,128)(2,1)}), bf16[4,32,1024]{2,1,0:T(8,128)(2,1)S(1)}, u32[]{:S(2)}, u32[]{:S(2)}) %all-to-all-start.9) | async-done | bytes 262176 | tf_op jit(solution)/shard_map/all_to_all | solution.py:29
  230.8 3.4 %all-to-all-start.10 = ((bf16[8,64,256]{2,1,0:T(8,128)(2,1)}), bf16[8,64,256]{2,1,0:T(8,128)(2,1)S(1)}, u32[]{:S(2)}, u32[]{:S(2)}) async-start(bf16[8,64,256]{2,1,0:T(8,128)(2,1)} %bitcast.32), calls=%async_computation.10 | async-start | bytes 524288 | tf_op jit(solution)/shard_map/all_to_all | solution.py:33
  246.3 7.1 %all-to-all-start.11 = ((bf16[8,64,640]{2,1,0:T(8,128)(2,1)}), bf16[8,64,640]{2,1,0:T(8,128)(2,1)S(1)}, u32[]{:S(2)}, u32[]{:S(2)}) async-start(bf16[8,64,640]{2,1,0:T(8,128)(2,1)} %bitcast.34), calls=%async_computation.11 | async-start | bytes 1310720 | tf_op jit(solution)/shard_map/all_to_all | solution.py:33
  259.4 2.3 fusion.5
  263.2 3.9 %all-to-all-done.11 = bf16[8,64,640]{2,1,0:T(8,128)(2,1)S(1)} async-done(((bf16[8,64,640]{2,1,0:T(8,128)(2,1)}), bf16[8,64,640]{2,1,0:T(8,128)(2,1)S(1)}, u32[]{:S(2)}, u32[]{:S(2)}) %all-to-all-start.11) | async-done | bytes 655392 | tf_op jit(solution)/shard_map/all_to_all | solution.py:33
  268.5 2.0 fusion.6
  272.9 3.5 %all-to-all-start.12 = ((bf16[8,32,1024]{2,1,0:T(8,128)(2,1)}), bf16[8,32,1024]{2,1,0:T(8,128)(2,1)S(1)}, u32[]{:S(2)}, u32[]{:S(2)}) async-start(bf16[8,32,1024]{2,1,0:T(8,128)(2,1)} %pad_maximum_fusion), calls=%async_computation.12 | async-start | bytes 1048576 | tf_op jit(solution)/shard_map/all_to_all | solution.py:29
  284.0 2.5 fusion.51
  287.8 6.3 %collective-permute-start.31 = (bf16[256,1024]{1,0:T(8,128)(2,1)}, bf16[256,1024]{1,0:T(8,128)(2,1)}, u32[]{:S(2)}, u32[]{:S(2)}) collective-permute-start(bf16[256,1024]{1,0:T(8,128)(2,1)} %get-tuple-element.103), channel_id=1, source_target_pairs={{16,0},{17,1},{18,2},{19,3},{20,4},{21,5},{22,6},{23,7},{24,8},{25... | collective-permute-start | bytes 1572872 | tf_op jit(solution)/shard_map/ppermute | solution.py:613
  296.6 8.9 %all-to-all-start.13 = ((bf16[16,8,1024]{2,1,0:T(8,128)(2,1)}), bf16[16,8,1024]{2,1,0:T(8,128)(2,1)S(1)}, u32[]{:S(2)}, u32[]{:S(2)}) async-start(bf16[16,8,1024]{2,1,0:T(8,128)(2,1)} %all_to_all.132), calls=%async_computation.13 | async-start | bytes 524288 | tf_op jit(solution)/shard_map/all_to_all | solution.py:638
  305.5 2.7 collective-permute-start.26
  308.2 2.5 fusion.50
  310.8 4.4 %collective-permute-done.26.refs_0_ = bf16[2,64,1024]{2,1,0:T(8,128)(2,1)} collective-permute-done((bf16[2,64,1024]{2,1,0:T(8,128)(2,1)}, bf16[2,64,1024]{2,1,0:T(8,128)(2,1)}, u32[]{:S(2)}, u32[]{:S(2)}) %collective-permute-start.26) | collective-permute-done | bytes 262176 | tf_op jit(solution)/shard_map/ppermute | solution.py:613
  315.2 5.2 %collective-permute-start.22 = (bf16[1024,256]{1,0:T(8,128)(2,1)}, bf16[1024,256]{1,0:T(8,128)(2,1)}, u32[]{:S(2)}, u32[]{:S(2)}) collective-permute-start(bf16[1024,256]{1,0:T(8,128)(2,1)} %get-tuple-element.101), channel_id=1, source_target_pairs={{16,0},{17,1},{18,2},{19,3},{20,4},{21,5},{22,6},{23,7},{24,8},{25... | collective-permute-start | bytes 1572872 | tf_op jit(solution)/shard_map/ppermute | solution.py:613
  322.5 2.7 select_bitcast_fusion
  330.8 2.6 select_bitcast_fusion.1
  (283 shorter events, 103.2 us)
Async XLA Ops:
  1.7 5.3 %collective-permute-start = (bf16[64,1024]{1,0:T(8,128)(2,1)S(1)}, bf16[64,1024]{1,0:T(8,128)(2,1)S(1)}, u32[]{:S(2)}, u32[]{:S(2)}) collective-permute-start(bf16[64,1024]{1,0:T(8,128)(2,1)S(1)} %bitcast.165), channel_id=1, source_target_pairs={{0,16},{16,0},{1,17},{17,1},{2,18},{18,2},{3,19},{19,3},{4,20},{20... | collective-permute-start | bytes 393224 | tf_op jit(solution)/shard_map/ppermute | solution.py:25
  5.5 21.4 %collective-permute-start.3 = (bf16[1024,256]{1,0:T(8,128)(2,1)S(1)}, bf16[1024,256]{1,0:T(8,128)(2,1)S(1)}, u32[]{:S(2)}, u32[]{:S(2)}) collective-permute-start(bf16[1024,256]{1,0:T(8,128)(2,1)S(1)} %bitcast.157), channel_id=1, source_target_pairs={{0,2},{1,3},{2,0},{3,1},{4,6},{5,7},{6,4},{7,5},{8,10},{9,11},{10,... | collective-permute-start | bytes 1572872 | tf_op jit(solution)/shard_map/ppermute | solution.py:25
  7.0 1.4 collective-permute-start.1
  8.5 17.2 %collective-permute-start.2 = (bf16[128,1024]{1,0:T(8,128)(2,1)S(1)}, bf16[128,1024]{1,0:T(8,128)(2,1)S(1)}, u32[]{:S(2)}, u32[]{:S(2)}) collective-permute-start(bf16[128,1024]{1,0:T(8,128)(2,1)S(1)} %maximum_select_fusion.5), channel_id=1, source_target_pairs={{0,2},{1,3},{2,0},{3,1},{4,6},{5,7},{6,4},{7,5},{8,10},{9,11},{10,... | collective-permute-start | bytes 786440 | tf_op jit(solution)/shard_map/ppermute | solution.py:25
  11.4 14.1 %all-to-all-start = ((bf16[8,8,1024]{2,1,0:T(8,128)(2,1)}), bf16[8,8,1024]{2,1,0:T(8,128)(2,1)S(1)}, u32[]{:S(2)}, u32[]{:S(2)}) async-start(bf16[8,8,1024]{2,1,0:T(8,128)(2,1)} %copy.41), calls=%async_computation | async-start | bytes 262144 | tf_op jit(solution)/shard_map/all_to_all | solution.py:33
  25.9 33.4 %copy-start.2 = (bf16[256,1024]{1,0:T(8,128)(2,1)}, bf16[256,1024]{1,0:T(8,128)(2,1)S(1)}, u32[]{:S(2)}) copy-start(bf16[256,1024]{1,0:T(8,128)(2,1)S(1)} %maximum_select_fusion.3.refs_1_.refs_4_.refs_5_) | copy-start | bytes 1572868
  29.2 23.7 %collective-permute-start.4 = (bf16[1024,512]{1,0:T(8,128)(2,1)S(1)}, bf16[1024,512]{1,0:T(8,128)(2,1)}, u32[]{:S(2)}, u32[]{:S(2)}) collective-permute-start(bf16[1024,512]{1,0:T(8,128)(2,1)S(1)} %maximum_select_fusion), channel_id=1, source_target_pairs={{0,16},{16,0},{1,17},{17,1},{2,18},{18,2},{3,19},{19,3},{4,20},{20... | collective-permute-start | bytes 3145736 | tf_op jit(solution)/shard_map/ppermute | solution.py:25
  30.6 12.4 %collective-permute-start.6 = (s32[2,64]{1,0:T(2,128)S(1)}, s32[2,64]{1,0:T(2,128)S(1)}, u32[]{:S(2)}, u32[]{:S(2)}) collective-permute-start(s32[2,64]{1,0:T(2,128)S(1)} %copy-done.58), channel_id=1, source_target_pairs={{0,0},{1,1},{128,2},{129,3},{4,4},{5,5},{132,6},{133,7},{8,8},{9,9... | collective-permute-start | bytes 1544 | tf_op jit(solution)/shard_map/ppermute | solution.py:456
  31.3 25.2 %all-to-all-start.1 = ((bf16[8,32,1024]{2,1,0:T(8,128)(2,1)}), bf16[8,32,1024]{2,1,0:T(8,128)(2,1)S(1)}, u32[]{:S(2)}, u32[]{:S(2)}) async-start(bf16[8,32,1024]{2,1,0:T(8,128)(2,1)} %bitcast.6), calls=%async_computation.1 | async-start | bytes 1048576 | tf_op jit(solution)/shard_map/all_to_all | solution.py:29
  43.0 14.4 %collective-permute-start.9 = (bf16[64,1024]{1,0:T(8,128)(2,1)S(1)}, bf16[64,1024]{1,0:T(8,128)(2,1)}, u32[]{:S(2)}, u32[]{:S(2)}) collective-permute-start(bf16[64,1024]{1,0:T(8,128)(2,1)S(1)} %get-tuple-element.90), channel_id=1, source_target_pairs={{0,1},{1,0},{2,3},{3,2},{4,5},{5,4},{6,7},{7,6},{8,9},{9,8},{10,11... | collective-permute-start | bytes 393224 | tf_op jit(solution)/shard_map/ppermute | solution.py:25
  54.6 12.4 %collective-permute-start.7 = (bf16[256,1024]{1,0:T(8,128)(2,1)}, bf16[256,1024]{1,0:T(8,128)(2,1)}, u32[]{:S(2)}, u32[]{:S(2)}) collective-permute-start(bf16[256,1024]{1,0:T(8,128)(2,1)} %bitcast.15), channel_id=1, source_target_pairs={{0,16},{16,0},{1,17},{17,1},{2,18},{18,2},{3,19},{19,3},{4,20},{20... | collective-permute-start | bytes 1572872 | tf_op jit(solution)/shard_map/ppermute | solution.py:25
  57.2 2.0 collective-permute-start.5
  61.7 18.3 %all-to-all-start.2 = ((bf16[8,64,640]{2,1,0:T(8,128)(2,1)}), bf16[8,64,640]{2,1,0:T(8,128)(2,1)S(1)}, u32[]{:S(2)}, u32[]{:S(2)}) async-start(bf16[8,64,640]{2,1,0:T(8,128)(2,1)} %bitcast.142), calls=%async_computation.2 | async-start | bytes 1310720 | tf_op jit(solution)/shard_map/all_to_all | solution.py:33
  66.4 19.7 %collective-permute-start.10 = (bf16[128,1024]{1,0:T(8,128)(2,1)}, bf16[128,1024]{1,0:T(8,128)(2,1)}, u32[]{:S(2)}, u32[]{:S(2)}) collective-permute-start(bf16[128,1024]{1,0:T(8,128)(2,1)} %maximum_select_fusion.6), channel_id=1, source_target_pairs={{0,2},{1,3},{2,0},{3,1},{4,6},{5,7},{6,4},{7,5},{8,10},{9,11},{10,... | collective-permute-start | bytes 786440 | tf_op jit(solution)/shard_map/ppermute | solution.py:25
  69.2 19.2 %collective-permute-start.8 = (bf16[256,1024]{1,0:T(8,128)(2,1)}, bf16[256,1024]{1,0:T(8,128)(2,1)}, u32[]{:S(2)}, u32[]{:S(2)}) collective-permute-start(bf16[256,1024]{1,0:T(8,128)(2,1)} %get-tuple-element.44), channel_id=1, source_target_pairs={{0,2},{1,3},{2,0},{3,1},{4,6},{5,7},{6,4},{7,5},{8,10},{9,11},{10,... | collective-permute-start | bytes 1572872 | tf_op jit(solution)/shard_map/ppermute | solution.py:25
  82.1 13.0 %all-to-all-start.3 = ((bf16[8,64,256]{2,1,0:T(8,128)(2,1)}), bf16[8,64,256]{2,1,0:T(8,128)(2,1)}, u32[]{:S(2)}, u32[]{:S(2)}) async-start(bf16[8,64,256]{2,1,0:T(8,128)(2,1)} %bitcast.13), calls=%async_computation.3 | async-start | bytes 524288 | tf_op jit(solution)/shard_map/all_to_all | solution.py:33
  97.8 1.6 collective-permute-start.11
  100.1 19.0 %all-to-all-start.4 = ((bf16[4,32,1024]{2,1,0:T(8,128)(2,1)}), bf16[4,32,1024]{2,1,0:T(8,128)(2,1)}, u32[]{:S(2)}, u32[]{:S(2)}) async-start(bf16[4,32,1024]{2,1,0:T(8,128)(2,1)} %bitcast.162), calls=%async_computation.4 | async-start | bytes 524288 | tf_op jit(solution)/shard_map/all_to_all | solution.py:29
  108.8 17.9 %collective-permute-start.13 = (bf16[256,1024]{1,0:T(8,128)(2,1)}, bf16[256,1024]{1,0:T(8,128)(2,1)}, u32[]{:S(2)}, u32[]{:S(2)}) collective-permute-start(bf16[256,1024]{1,0:T(8,128)(2,1)} %shard_map.158), channel_id=1, source_target_pairs={{0,2},{1,3},{2,0},{3,1},{4,6},{5,7},{6,4},{7,5},{8,10},{9,11},{10,... | collective-permute-start | bytes 1572872 | tf_op jit(solution)/shard_map/ppermute | solution.py:25
  109.9 1.9 collective-permute-start.12
  122.6 13.8 %all-to-all-start.5 = ((bf16[4,32,1024]{2,1,0:T(8,128)(2,1)}), bf16[4,32,1024]{2,1,0:T(8,128)(2,1)}, u32[]{:S(2)}, u32[]{:S(2)}) async-start(bf16[4,32,1024]{2,1,0:T(8,128)(2,1)} %bitcast.148), calls=%async_computation.5 | async-start | bytes 524288 | tf_op jit(solution)/shard_map/all_to_all | solution.py:29
  136.4 1.7 collective-permute-start.14
  140.1 41.9 %copy-start.9 = (bf16[128,1024]{1,0:T(8,128)(2,1)}, bf16[128,1024]{1,0:T(8,128)(2,1)S(1)}, u32[]{:S(2)}) copy-start(bf16[128,1024]{1,0:T(8,128)(2,1)S(1)} %collective-permute-done.14.refs_2_.refs_3_) | copy-start | bytes 786436
  184.2 1.6 collective-permute-start.15
  186.7 18.5 %all-to-all-start.8 = ((bf16[4,32,1024]{2,1,0:T(8,128)(2,1)}), bf16[4,32,1024]{2,1,0:T(8,128)(2,1)S(1)}, u32[]{:S(2)}, u32[]{:S(2)}) async-start(bf16[4,32,1024]{2,1,0:T(8,128)(2,1)} %bitcast.25), calls=%async_computation.8 | async-start | bytes 524288 | tf_op jit(solution)/shard_map/all_to_all | solution.py:29
  202.5 12.9 %collective-permute-start.16 = (bf16[128,1024]{1,0:T(8,128)(2,1)}, bf16[128,1024]{1,0:T(8,128)(2,1)}, u32[]{:S(2)}, u32[]{:S(2)}) collective-permute-start(bf16[128,1024]{1,0:T(8,128)(2,1)} %get-tuple-element.59), channel_id=1, source_target_pairs={{0,1},{1,0},{2,3},{3,2},{4,5},{5,4},{6,7},{7,6},{8,9},{9,8},{10,11... | collective-permute-start | bytes 786440 | tf_op jit(solution)/shard_map/ppermute | solution.py:25
  206.0 18.5 %all-to-all-start.9 = ((bf16[4,32,1024]{2,1,0:T(8,128)(2,1)}), bf16[4,32,1024]{2,1,0:T(8,128)(2,1)S(1)}, u32[]{:S(2)}, u32[]{:S(2)}) async-start(bf16[4,32,1024]{2,1,0:T(8,128)(2,1)} %bitcast.27), calls=%async_computation.9 | async-start | bytes 524288 | tf_op jit(solution)/shard_map/all_to_all | solution.py:29
  224.5 1.5 collective-permute-start.17
  229.3 11.9 %collective-permute-start.20 = (bf16[16,1024]{1,0:T(8,128)(2,1)}, bf16[16,1024]{1,0:T(8,128)(2,1)}, u32[]{:S(2)}, u32[]{:S(2)}) collective-permute-start(bf16[16,1024]{1,0:T(8,128)(2,1)} %get-tuple-element.97), channel_id=1, source_target_pairs={{0,2},{1,3},{2,0},{3,1},{4,6},{5,7},{6,4},{7,5},{8,10},{9,11},{10,... | collective-permute-start | bytes 98312 | tf_op jit(solution)/shard_map/ppermute | solution.py:25
  230.8 12.8 %all-to-all-start.10 = ((bf16[8,64,256]{2,1,0:T(8,128)(2,1)}), bf16[8,64,256]{2,1,0:T(8,128)(2,1)S(1)}, u32[]{:S(2)}, u32[]{:S(2)}) async-start(bf16[8,64,256]{2,1,0:T(8,128)(2,1)} %bitcast.32), calls=%async_computation.10 | async-start | bytes 524288 | tf_op jit(solution)/shard_map/all_to_all | solution.py:33
  234.8 8.9 %collective-permute-start.18 = (bf16[16,1024]{1,0:T(8,128)(2,1)}, bf16[16,1024]{1,0:T(8,128)(2,1)}, u32[]{:S(2)}, u32[]{:S(2)}) collective-permute-start(bf16[16,1024]{1,0:T(8,128)(2,1)} %get-tuple-element.95), channel_id=1, source_target_pairs={{0,2},{1,3},{2,0},{3,1},{4,6},{5,7},{6,4},{7,5},{8,10},{9,11},{10,... | collective-permute-start | bytes 98312 | tf_op jit(solution)/shard_map/ppermute | solution.py:25
  235.4 24.0 %collective-permute-start.23 = (bf16[1024,256]{1,0:T(8,128)(2,1)}, bf16[1024,256]{1,0:T(8,128)(2,1)}, u32[]{:S(2)}, u32[]{:S(2)}) collective-permute-start(bf16[1024,256]{1,0:T(8,128)(2,1)} %shard_map.173), channel_id=1, source_target_pairs={{0,2},{1,3},{2,0},{3,1},{4,6},{5,7},{6,4},{7,5},{8,10},{9,11},{10,... | collective-permute-start | bytes 1572872 | tf_op jit(solution)/shard_map/ppermute | solution.py:25
  236.9 26.3 %collective-permute-start.32 = (bf16[256,1024]{1,0:T(8,128)(2,1)}, bf16[256,1024]{1,0:T(8,128)(2,1)}, u32[]{:S(2)}, u32[]{:S(2)}) collective-permute-start(bf16[256,1024]{1,0:T(8,128)(2,1)} %shard_map.178), channel_id=1, source_target_pairs={{0,2},{1,3},{2,0},{3,1},{4,6},{5,7},{6,4},{7,5},{8,10},{9,11},{10,... | collective-permute-start | bytes 1572872 | tf_op jit(solution)/shard_map/ppermute | solution.py:25
  243.6 12.8 %collective-permute-start.27 = (bf16[2,64,1024]{2,1,0:T(8,128)(2,1)}, bf16[2,64,1024]{2,1,0:T(8,128)(2,1)}, u32[]{:S(2)}, u32[]{:S(2)}) collective-permute-start(bf16[2,64,1024]{2,1,0:T(8,128)(2,1)} %dynamic-slice_bitcast_fusion), channel_id=1, source_target_pairs={{0,1},{1,0},{2,3},{3,2},{4,5},{5,4},{6,7},{7,6},{8,9},{9,8},{10,11... | collective-permute-start | bytes 786440 | tf_op jit(solution)/shard_map/ppermute | solution.py:25
  246.3 20.8 %all-to-all-start.11 = ((bf16[8,64,640]{2,1,0:T(8,128)(2,1)}), bf16[8,64,640]{2,1,0:T(8,128)(2,1)S(1)}, u32[]{:S(2)}, u32[]{:S(2)}) async-start(bf16[8,64,640]{2,1,0:T(8,128)(2,1)} %bitcast.34), calls=%async_computation.11 | async-start | bytes 1310720 | tf_op jit(solution)/shard_map/all_to_all | solution.py:33
  255.0 28.9 %collective-permute-start.30 = (bf16[256,1024]{1,0:T(8,128)(2,1)}, bf16[256,1024]{1,0:T(8,128)(2,1)}, u32[]{:S(2)}, u32[]{:S(2)}) collective-permute-start(bf16[256,1024]{1,0:T(8,128)(2,1)} %shard_map.176), channel_id=1, source_target_pairs={{0,2},{1,3},{2,0},{3,1},{4,6},{5,7},{6,4},{7,5},{8,10},{9,11},{10,... | collective-permute-start | bytes 1572872 | tf_op jit(solution)/shard_map/ppermute | solution.py:25
  258.1 62.2 %collective-permute-start.28 = (bf16[2,64,1024]{2,1,0:T(8,128)(2,1)}, bf16[2,64,1024]{2,1,0:T(8,128)(2,1)}, u32[]{:S(2)}, u32[]{:S(2)}) collective-permute-start(bf16[2,64,1024]{2,1,0:T(8,128)(2,1)} %fusion.8), channel_id=1, source_target_pairs={{0,16},{1,17},{2,18},{3,19},{4,20},{5,21},{6,22},{7,23},{8,24},{9,... | collective-permute-start | bytes 786440 | tf_op jit(solution)/shard_map/ppermute | solution.py:612
  261.7 67.8 %collective-permute-start.24 = (bf16[1024,256]{1,0:T(8,128)(2,1)}, bf16[1024,256]{1,0:T(8,128)(2,1)}, u32[]{:S(2)}, u32[]{:S(2)}) collective-permute-start(bf16[1024,256]{1,0:T(8,128)(2,1)} %fusion.5), channel_id=1, source_target_pairs={{0,16},{1,17},{2,18},{3,19},{4,20},{5,21},{6,22},{7,23},{8,24},{9,... | collective-permute-start | bytes 1572872 | tf_op jit(solution)/shard_map/ppermute | solution.py:612
  268.4 3.6 %collective-permute-start.19 = (bf16[128,1024]{1,0:T(8,128)(2,1)S(1)}, bf16[128,1024]{1,0:T(8,128)(2,1)S(1)}, u32[]{:S(2)}, u32[]{:S(2)}) collective-permute-start(bf16[128,1024]{1,0:T(8,128)(2,1)S(1)} %get-tuple-element.64), channel_id=1, source_target_pairs={{0,1},{1,0},{2,3},{3,2},{4,5},{5,4},{6,7},{7,6},{8,9},{9,8},{10,11... | collective-permute-start | bytes 786440 | tf_op jit(solution)/shard_map/ppermute | solution.py:25
  270.5 51.9 %collective-permute-start.33 = (bf16[256,1024]{1,0:T(8,128)(2,1)}, bf16[256,1024]{1,0:T(8,128)(2,1)}, u32[]{:S(2)}, u32[]{:S(2)}) collective-permute-start(bf16[256,1024]{1,0:T(8,128)(2,1)} %fusion.6), channel_id=1, source_target_pairs={{0,16},{1,17},{2,18},{3,19},{4,20},{5,21},{6,22},{7,23},{8,24},{9,... | collective-permute-start | bytes 1572872 | tf_op jit(solution)/shard_map/ppermute | solution.py:612
  272.9 22.0 %all-to-all-start.12 = ((bf16[8,32,1024]{2,1,0:T(8,128)(2,1)}), bf16[8,32,1024]{2,1,0:T(8,128)(2,1)S(1)}, u32[]{:S(2)}, u32[]{:S(2)}) async-start(bf16[8,32,1024]{2,1,0:T(8,128)(2,1)} %pad_maximum_fusion), calls=%async_computation.12 | async-start | bytes 1048576 | tf_op jit(solution)/shard_map/all_to_all | solution.py:29
  278.9 26.6 %collective-permute-start.21 = (bf16[1024,256]{1,0:T(8,128)(2,1)}, bf16[1024,256]{1,0:T(8,128)(2,1)}, u32[]{:S(2)}, u32[]{:S(2)}) collective-permute-start(bf16[1024,256]{1,0:T(8,128)(2,1)} %shard_map.171), channel_id=1, source_target_pairs={{0,2},{1,3},{2,0},{3,1},{4,6},{5,7},{6,4},{7,5},{8,10},{9,11},{10,... | collective-permute-start | bytes 1572872 | tf_op jit(solution)/shard_map/ppermute | solution.py:25
  283.8 4.0 %collective-permute-start.25 = (bf16[2,64,1024]{2,1,0:T(8,128)(2,1)}, bf16[2,64,1024]{2,1,0:T(8,128)(2,1)S(1)}, u32[]{:S(2)}, u32[]{:S(2)}) collective-permute-start(bf16[2,64,1024]{2,1,0:T(8,128)(2,1)} %dynamic-slice_bitcast_fusion.1), channel_id=1, source_target_pairs={{0,1},{1,0},{2,3},{3,2},{4,5},{5,4},{6,7},{7,6},{8,9},{9,8},{10,11... | collective-permute-start | bytes 786440 | tf_op jit(solution)/shard_map/ppermute | solution.py:25
  287.8 34.6 %collective-permute-start.31 = (bf16[256,1024]{1,0:T(8,128)(2,1)}, bf16[256,1024]{1,0:T(8,128)(2,1)}, u32[]{:S(2)}, u32[]{:S(2)}) collective-permute-start(bf16[256,1024]{1,0:T(8,128)(2,1)} %get-tuple-element.103), channel_id=1, source_target_pairs={{16,0},{17,1},{18,2},{19,3},{20,4},{21,5},{22,6},{23,7},{24,8},{25... | collective-permute-start | bytes 1572872 | tf_op jit(solution)/shard_map/ppermute | solution.py:613
  296.6 31.1 %all-to-all-start.13 = ((bf16[16,8,1024]{2,1,0:T(8,128)(2,1)}), bf16[16,8,1024]{2,1,0:T(8,128)(2,1)S(1)}, u32[]{:S(2)}, u32[]{:S(2)}) async-start(bf16[16,8,1024]{2,1,0:T(8,128)(2,1)} %all_to_all.132), calls=%async_computation.13 | async-start | bytes 524288 | tf_op jit(solution)/shard_map/all_to_all | solution.py:638
  305.5 9.7 %collective-permute-start.26 = (bf16[2,64,1024]{2,1,0:T(8,128)(2,1)}, bf16[2,64,1024]{2,1,0:T(8,128)(2,1)}, u32[]{:S(2)}, u32[]{:S(2)}) collective-permute-start(bf16[2,64,1024]{2,1,0:T(8,128)(2,1)} %fusion.7), channel_id=1, source_target_pairs={{16,0},{17,1},{18,2},{19,3},{20,4},{21,5},{22,6},{23,7},{24,8},{25... | collective-permute-start | bytes 786440 | tf_op jit(solution)/shard_map/ppermute | solution.py:613
  315.2 15.6 %collective-permute-start.22 = (bf16[1024,256]{1,0:T(8,128)(2,1)}, bf16[1024,256]{1,0:T(8,128)(2,1)}, u32[]{:S(2)}, u32[]{:S(2)}) collective-permute-start(bf16[1024,256]{1,0:T(8,128)(2,1)} %get-tuple-element.101), channel_id=1, source_target_pairs={{16,0},{17,1},{18,2},{19,3},{20,4},{21,5},{22,6},{23,7},{24,8},{25... | collective-permute-start | bytes 1572872 | tf_op jit(solution)/shard_map/ppermute | solution.py:613
  321.9 5.1 %collective-permute-start.29 = (bf16[64,1024]{1,0:T(8,128)(2,1)S(1)}, bf16[64,1024]{1,0:T(8,128)(2,1)S(1)}, u32[]{:S(2)}, u32[]{:S(2)}) collective-permute-start(bf16[64,1024]{1,0:T(8,128)(2,1)S(1)} %dynamic-slice_bitcast_fusion.2), channel_id=1, source_target_pairs={{0,2},{1,3},{2,0},{3,1},{4,6},{5,7},{6,4},{7,5},{8,10},{9,11},{10,... | collective-permute-start | bytes 393224 | tf_op jit(solution)/shard_map/ppermute | solution.py:25
  (57 other events, 255.1 us)

commit v4 on v2

--- a/solution.py
+++ b/solution.py
@@ -46,17 +46,23 @@
     )
 
 
-def call(body, shapes, *operands, flops=0):
+def call(body, shapes, *operands, flops=0, deps=()):
+    first, extra = len(operands), len(deps)
+
+    def plain(*refs):
+        body(*refs[:first], *refs[first + extra :])
+
     outs = [jax.ShapeDtypeStruct(shape, kind) for shape, kind in shapes]
     moved = sum(x.size * x.dtype.itemsize for x in list(operands) + outs)
     return pl.pallas_call(
-        body,
+        plain,
         out_shape=outs,
-        in_specs=[pl.BlockSpec(memory_space=pltpu.VMEM)] * len(operands),
+        in_specs=[pl.BlockSpec(memory_space=pltpu.VMEM)] * first
+        + [pl.BlockSpec(memory_space=pl.ANY)] * extra,
         out_specs=[pl.BlockSpec(memory_space=pltpu.VMEM)] * len(outs),
         compiler_params=pltpu.CompilerParams(vmem_limit_bytes=48 * 2**20),
         cost_estimate=pl.CostEstimate(flops=flops, bytes_accessed=moved, transcendentals=0),
-    )(*operands)
+    )(*operands, *deps)
 
 
 def one_hot(target):
@@ -149,7 +155,7 @@
     mine_out[...] = mm(rows[:half], wo[...])
 
 
-def out_project(target, got, wo):
+def out_project(target, got, wo, *deps):
     rows, cols = got.shape
     feats = wo.shape[1]
     return call(
@@ -159,6 +165,7 @@
         got,
         wo,
         flops=2 * rows * cols * (rows + feats),
+        deps=deps,
     )
 
 
@@ -419,7 +426,7 @@
         mask,
     )
     got_m0, all_g1 = lax.optimization_barrier((dp_exchange(mixed0), all_g1))
-    all_m0, far0, near0 = out_project(target, got_m0, wo0)
+    all_m0, far0, near0 = out_project(target, got_m0, wo0, wkv1)
     h1, h1_tiled = settle(scatter_z(near0, far0), h0)
 
     dm1 = mixed_grad(by_rank, [all_g1], wo1)

time: 339 us -> 329 us (0.971)
  waiting for transfers between devices: 107 us -> 76 us
  blocking collectives: 74.4 us -> 95.8 us
    all_to_all x1 -> x2, blocking collectives: 22 us -> 41.6 us  [z_exchange(): lax.all_to_all(value, 'tensor', 0, 0, axis_index_groups=same_core(size),...]
    all_to_all x5 -> x4, waiting for transfers between devices: 48.4 us -> 32.3 us  [z_exchange(): lax.all_to_all(value, 'tensor', 0, 0, axis_index_groups=same_core(size),...]
    all_to_all x4, waiting for transfers between devices: 21.1 us -> 11.2 us  [dp_exchange(): return lax.all_to_all(value, 'dp', 0, 0, tiled=True)]
    all_to_all x5 -> x4, starting transfers between devices: 27 us -> 23.4 us  [z_exchange(): lax.all_to_all(value, 'tensor', 0, 0, axis_index_groups=same_core(size),...]
    all_gather x1, waiting for transfers between devices: 4.77 us -> 1.32 us  [shards(): all_g1 = lax.all_gather(g1_sent, 'tensor', axis=0, tiled=True)]
    unnamed x102 -> x98, local copies, waits for them, and re-layouts: 7.03 us -> 8.89 us
  transfers between devices with their start and end apart: 35 -> 34, of which waited for: 17 -> 16; matrix products, arithmetic and copies ran while one was open for 11% -> 11% of each run, Pallas kernels for 3% -> 3%
where the time goes in v4:
time: 329 us; the launch traced here: 327 us
  blocking collectives  95.8 us (29%)
  waiting for transfers between devices  76 us (23%)
  starting transfers between devices  73.6 us (22%)
  other arithmetic  20 us (6%)
  local copies, waits for them, and re-layouts  17.6 us (5%)
  Pallas kernels  15.9 us (5%)
  between operations  15 us (5%)
  matrix products  13.6 us (4%)
    all_to_all x3, blocking collectives, dp_exchange(): return lax.all_to_all(value, 'dp', 0, 0, tiled=True)  54.2 us
    all_to_all x2, blocking collectives, z_exchange(): lax.all_to_all(value, 'tensor', 0, 0, axis_index_groups=same_core(size),...  41.6 us
    all_to_all x4, waiting for transfers between devices, z_exchange(): lax.all_to_all(value, 'tensor', 0, 0, axis_index_groups=same_core(size),...  32.3 us
    all_to_all x4, starting transfers between devices, z_exchange(): lax.all_to_all(value, 'tensor', 0, 0, axis_index_groups=same_core(size),...  23.4 us
    ppermute x17, waiting for transfers between devices, swap(): return lax.ppermute(value, axis, pairs)  21.9 us
    all_to_all x4, starting transfers between devices, dp_exchange(): return lax.all_to_all(value, 'dp', 0, 0, tiled=True)  17.9 us
    pallas_call x14, Pallas kernels, call(): pl.pallas_call(plain, out_shape=outs, in_specs=[pl.BlockSpec(memory_space...  15.9 us
    dot_general x11, matrix products, mm(): lax.dot_general(a, b, (((ca,), (cb,)), ((), ())), preferred_element_type=...  13.6 us
  transfers between devices with their start and end apart: 34, of which 16 were waited for; matrix products, arithmetic and copies ran while one was open for 11% of the time, Pallas kernels for 3%

profile of v4, /device:TPU:8, one launch (start us, length us, event | category | flops | bytes accessed | tf_op | source)
XLA Modules:
  0.0 327.4 jit_solution(337928562232806738)
XLA Ops:
  8.3 13.9 %all_to_all.148 = bf16[8,8,1024]{2,1,0:T(8,128)(2,1)S(1)} all-to-all(bf16[8,8,1024]{2,1,0:T(8,128)(2,1)S(1)} %all_to_all.95), channel_id=1, replica_groups=mesh['dp'=8,'pipe'=2,'tensor'=16] {'dp'}, dimensions={0} | all-to-all | bytes 262144 | tf_op jit(solution)/shard_map/all_to_all | solution.py:40
  23.3 8.6 %all-to-all-start.1 = ((bf16[8,32,1024]{2,1,0:T(8,128)(2,1)}), bf16[8,32,1024]{2,1,0:T(8,128)(2,1)S(1)}, u32[]{:S(2)}, u32[]{:S(2)}) async-start(bf16[8,32,1024]{2,1,0:T(8,128)(2,1)} %broadcast_in_dim.11), calls=%async_computation.1 | async-start | bytes 1048576 | tf_op jit(solution)/shard_map/all_to_all | solution.py:34
  32.0 1.4 collective-permute-start.2
  33.4 3.6 %collective-permute-done.2 = bf16[64,1024]{1,0:T(8,128)(2,1)S(1)} collective-permute-done((bf16[64,1024]{1,0:T(8,128)(2,1)S(1)}, bf16[64,1024]{1,0:T(8,128)(2,1)S(1)}, u32[]{:S(2)}, u32[]{:S(2)}) %collective-permute-start.2) | collective-permute-done | bytes 131104 | tf_op jit(solution)/shard_map/ppermute | solution.py:25
  37.4 1.4 collective-permute-start.1
  38.9 2.1 collective-permute-start.4
  40.9 8.1 %all-to-all-done.1 = bf16[8,32,1024]{2,1,0:T(8,128)(2,1)S(1)} async-done(((bf16[8,32,1024]{2,1,0:T(8,128)(2,1)}), bf16[8,32,1024]{2,1,0:T(8,128)(2,1)S(1)}, u32[]{:S(2)}, u32[]{:S(2)}) %all-to-all-start.1) | async-done | bytes 524320 | tf_op jit(solution)/shard_map/all_to_all | solution.py:34
  49.0 1.5 subtract_convert_fusion
  53.5 2.1 shard_map.152
  57.1 3.6 %all-to-all-start.2 = ((bf16[8,64,640]{2,1,0:T(8,128)(2,1)}), bf16[8,64,640]{2,1,0:T(8,128)(2,1)S(1)}, u32[]{:S(2)}, u32[]{:S(2)}) async-start(bf16[8,64,640]{2,1,0:T(8,128)(2,1)} %bitcast.8), calls=%async_computation.2 | async-start | bytes 1310720 | tf_op jit(solution)/shard_map/all_to_all | solution.py:40
  60.6 1.7 collective-permute-start.5
  63.0 8.9 %collective-permute-done.7 = bf16[128,1024]{1,0:T(8,128)(2,1)S(1)} collective-permute-done((bf16[128,1024]{1,0:T(8,128)(2,1)S(1)}, bf16[128,1024]{1,0:T(8,128)(2,1)S(1)}, u32[]{:S(2)}, u32[]{:S(2)}) %collective-permute-start.7) | collective-permute-done | bytes 262176 | tf_op jit(solution)/shard_map/ppermute | solution.py:25
  76.0 4.9 %all-to-all-start.3 = ((bf16[8,64,256]{2,1,0:T(8,128)(2,1)}), bf16[8,64,256]{2,1,0:T(8,128)(2,1)S(1)}, u32[]{:S(2)}, u32[]{:S(2)}) async-start(bf16[8,64,256]{2,1,0:T(8,128)(2,1)} %bitcast.11), calls=%async_computation.3 | async-start | bytes 524288 | tf_op jit(solution)/shard_map/all_to_all | solution.py:40
  82.8 6.9 %all-to-all-done.3 = bf16[8,64,256]{2,1,0:T(8,128)(2,1)S(1)} async-done(((bf16[8,64,256]{2,1,0:T(8,128)(2,1)}), bf16[8,64,256]{2,1,0:T(8,128)(2,1)S(1)}, u32[]{:S(2)}, u32[]{:S(2)}) %all-to-all-start.3) | async-done | bytes 262176 | tf_op jit(solution)/shard_map/all_to_all | solution.py:40
  95.0 1.7 collective-permute-done.8
  96.8 22.4 %all_to_all.149 = bf16[8,32,1024]{2,1,0:T(8,128)(2,1)S(1)} all-to-all(bf16[8,32,1024]{2,1,0:T(8,128)(2,1)S(1)} %bitcast.148), channel_id=1, replica_groups={{0,2,4,6,8,10,12,14},{1,3,5,7,9,11,13,15},{16,18,20,22,24,26,28,30},{17..., dimensions={0} | all-to-all | bytes 1048576 | tf_op jit(solution)/shard_map/all_to_all | solution.py:34
  119.3 19.2 %all_to_all.150 = bf16[8,32,1024]{2,1,0:T(8,128)(2,1)S(1)} all-to-all(bf16[8,32,1024]{2,1,0:T(8,128)(2,1)S(1)} %bitcast.135), channel_id=1, replica_groups={{0,2,4,6,8,10,12,14},{1,3,5,7,9,11,13,15},{16,18,20,22,24,26,28,30},{17..., dimensions={0} | all-to-all | bytes 1048576 | tf_op jit(solution)/shard_map/all_to_all | solution.py:34
  141.7 22.3 %all_to_all.151 = bf16[8,64,896]{2,1,0:T(8,128)(2,1)S(1)} all-to-all(bf16[8,64,896]{2,1,0:T(8,128)(2,1)S(1)} %bitcast.132), channel_id=1, replica_groups=mesh['dp'=8,'pipe'=2,'tensor'=16] {'dp'}, dimensions={0} | all-to-all | bytes 1835008 | tf_op jit(solution)/shard_map/all_to_all | solution.py:40
  165.0 18.0 %all_to_all.152 = bf16[8,64,896]{2,1,0:T(8,128)(2,1)S(1)} all-to-all(bf16[8,64,896]{2,1,0:T(8,128)(2,1)S(1)} %bitcast.125), channel_id=1, replica_groups=mesh['dp'=8,'pipe'=2,'tensor'=16] {'dp'}, dimensions={0} | all-to-all | bytes 1835008 | tf_op jit(solution)/shard_map/all_to_all | solution.py:40
  184.3 1.9 collective-permute-done.10
  187.2 4.1 %all-to-all-start.8 = ((bf16[8,32,1024]{2,1,0:T(8,128)(2,1)}), bf16[8,32,1024]{2,1,0:T(8,128)(2,1)}, u32[]{:S(2)}, u32[]{:S(2)}) async-start(bf16[8,32,1024]{2,1,0:T(8,128)(2,1)} %bitcast.147), calls=%async_computation.8 | async-start | bytes 1048576 | tf_op jit(solution)/shard_map/all_to_all | solution.py:34
  195.9 2.2 fusion.9
  198.2 11.4 %all-to-all-done.8 = bf16[8,32,1024]{2,1,0:T(8,128)(2,1)} async-done(((bf16[8,32,1024]{2,1,0:T(8,128)(2,1)}), bf16[8,32,1024]{2,1,0:T(8,128)(2,1)}, u32[]{:S(2)}, u32[]{:S(2)}) %all-to-all-start.8) | async-done | bytes 524320 | tf_op jit(solution)/shard_map/all_to_all | solution.py:34
  211.5 3.5 %all-to-all-start.9 = ((bf16[8,32,1024]{2,1,0:T(8,128)(2,1)}), bf16[8,32,1024]{2,1,0:T(8,128)(2,1)S(1)}, u32[]{:S(2)}, u32[]{:S(2)}) async-start(bf16[8,32,1024]{2,1,0:T(8,128)(2,1)} %bitcast.134), calls=%async_computation.9 | async-start | bytes 1048576 | tf_op jit(solution)/shard_map/all_to_all | solution.py:34
  215.0 1.7 fusion.1
  218.4 1.5 fusion.34
  221.2 12.8 %all-to-all-done.9 = bf16[8,32,1024]{2,1,0:T(8,128)(2,1)S(1)} async-done(((bf16[8,32,1024]{2,1,0:T(8,128)(2,1)}), bf16[8,32,1024]{2,1,0:T(8,128)(2,1)S(1)}, u32[]{:S(2)}, u32[]{:S(2)}) %all-to-all-start.9) | async-done | bytes 524320 | tf_op jit(solution)/shard_map/all_to_all | solution.py:34
  236.4 1.6 fusion.36
  239.3 1.5 shard_map.161
  240.8 3.5 %all-to-all-start.10 = ((bf16[8,64,256]{2,1,0:T(8,128)(2,1)}), bf16[8,64,256]{2,1,0:T(8,128)(2,1)S(1)}, u32[]{:S(2)}, u32[]{:S(2)}) async-start(bf16[8,64,256]{2,1,0:T(8,128)(2,1)} %bitcast.26), calls=%async_computation.10 | async-start | bytes 524288 | tf_op jit(solution)/shard_map/all_to_all | solution.py:40
  244.4 1.6 fusion.5
  247.4 6.3 %reduce-scatter.2.cloned.1.call-done = bf16[32,1024]{1,0:T(8,128)(2,1)} async-done(((bf16[512,1024]{1,0:T(8,128)(2,1)}), bf16[32,1024]{1,0:T(8,128)(2,1)}) %reduce-scatter.2.cloned.1.call-update) | async-done | bytes 65552 | tf_op jit(solution)/shard_map/reduce_scatter | solution.py:456
  254.6 1.7 shard_map.162
  256.3 5.9 %all-to-all-start.11 = ((bf16[8,64,640]{2,1,0:T(8,128)(2,1)}), bf16[8,64,640]{2,1,0:T(8,128)(2,1)S(1)}, u32[]{:S(2)}, u32[]{:S(2)}) async-start(bf16[8,64,640]{2,1,0:T(8,128)(2,1)} %bitcast.28), calls=%async_computation.11 | async-start | bytes 1310720 | tf_op jit(solution)/shard_map/all_to_all | solution.py:40
  263.2 1.4 fusion.37
  264.6 5.4 %collective-permute-start.21 = (bf16[256,1024]{1,0:T(8,128)(2,1)}, bf16[256,1024]{1,0:T(8,128)(2,1)}, u32[]{:S(2)}, u32[]{:S(2)}) collective-permute-start(bf16[256,1024]{1,0:T(8,128)(2,1)} %get-tuple-element.75), channel_id=1, source_target_pairs={{16,0},{17,1},{18,2},{19,3},{20,4},{21,5},{22,6},{23,7},{24,8},{25... | collective-permute-start | bytes 1572872 | tf_op jit(solution)/shard_map/ppermute | solution.py:487
  270.1 3.1 all-to-all-done.11
  278.7 7.1 %all-to-all-start.12 = ((bf16[8,32,1024]{2,1,0:T(8,128)(2,1)}), bf16[8,32,1024]{2,1,0:T(8,128)(2,1)S(1)}, u32[]{:S(2)}, u32[]{:S(2)}) async-start(bf16[8,32,1024]{2,1,0:T(8,128)(2,1)} %bitcast.30), calls=%async_computation.12 | async-start | bytes 1048576 | tf_op jit(solution)/shard_map/all_to_all | solution.py:34
  285.9 2.5 fusion.35
  288.4 4.3 %collective-permute-start.13 = (bf16[1024,256]{1,0:T(8,128)(2,1)}, bf16[1024,256]{1,0:T(8,128)(2,1)}, u32[]{:S(2)}, u32[]{:S(2)}) collective-permute-start(bf16[1024,256]{1,0:T(8,128)(2,1)} %get-tuple-element.71), channel_id=1, source_target_pairs={{16,0},{17,1},{18,2},{19,3},{20,4},{21,5},{22,6},{23,7},{24,8},{25... | collective-permute-start | bytes 1572872 | tf_op jit(solution)/shard_map/ppermute | solution.py:487
  293.8 2.1 collective-permute-start.16
  295.9 2.5 select_bitcast_fusion
  298.4 4.1 %collective-permute-done.16 = bf16[64,1024]{1,0:T(8,128)(2,1)S(1)} collective-permute-done((bf16[64,1024]{1,0:T(8,128)(2,1)S(1)}, bf16[64,1024]{1,0:T(8,128)(2,1)S(1)}, u32[]{:S(2)}, u32[]{:S(2)}) %collective-permute-start.16) | collective-permute-done | bytes 131104 | tf_op jit(solution)/shard_map/ppermute | solution.py:25
  302.5 3.4 %collective-permute-start.17 = (bf16[64,1024]{1,0:T(8,128)(2,1)S(1)}, bf16[64,1024]{1,0:T(8,128)(2,1)S(1)}, u32[]{:S(2)}, u32[]{:S(2)}) collective-permute-start(bf16[64,1024]{1,0:T(8,128)(2,1)S(1)} %fusion.4), channel_id=1, source_target_pairs={{16,0},{17,1},{18,2},{19,3},{20,4},{21,5},{22,6},{23,7},{24,8},{25... | collective-permute-start | bytes 393224 | tf_op jit(solution)/shard_map/ppermute | solution.py:487
  307.9 3.7 %all-to-all-start.13 = ((bf16[16,8,1024]{2,1,0:T(8,128)(2,1)}), bf16[16,8,1024]{2,1,0:T(8,128)(2,1)S(1)}, u32[]{:S(2)}, u32[]{:S(2)}) async-start(bf16[16,8,1024]{2,1,0:T(8,128)(2,1)} %all_to_all.132), calls=%async_computation.14 | async-start | bytes 524288 | tf_op jit(solution)/shard_map/all_to_all | solution.py:495
  311.6 2.4 select_bitcast_fusion.1
  314.1 1.8 select_bitcast_fusion.2
  315.9 2.9 all-to-all-done.13
  (206 shorter events, 52.1 us)
Async XLA Ops:
  22.4 9.5 %copy-start.46 = (f32[1,1024,64]{1,2,0:T(8,128)S(1)}, f32[1,1024,64]{1,2,0:T(8,128)}, u32[]{:S(2)}) copy-start(f32[1,1024,64]{1,2,0:T(8,128)} %param.16) | copy-start | bytes 786436
  22.4 9.5 %copy-start.47 = (bf16[1,1024,64]{1,2,0:T(8,128)(2,1)S(1)}, bf16[1,1024,64]{1,2,0:T(8,128)(2,1)}, u32[]{:S(2)}) copy-start(bf16[1,1024,64]{1,2,0:T(8,128)(2,1)} %param.13) | copy-start | bytes 393220
  23.3 13.9 %copy-start.43 = (f32[1,1024,256]{2,1,0:T(8,128)S(1)}, f32[1,1024,256]{2,1,0:T(8,128)}, u32[]{:S(2)}) copy-start(f32[1,1024,256]{2,1,0:T(8,128)} %param.15) | copy-start | bytes 3145732
  23.3 25.7 %all-to-all-start.1 = ((bf16[8,32,1024]{2,1,0:T(8,128)(2,1)}), bf16[8,32,1024]{2,1,0:T(8,128)(2,1)S(1)}, u32[]{:S(2)}, u32[]{:S(2)}) async-start(bf16[8,32,1024]{2,1,0:T(8,128)(2,1)} %broadcast_in_dim.11), calls=%async_computation.1 | async-start | bytes 1048576 | tf_op jit(solution)/shard_map/all_to_all | solution.py:34
  31.9 59.8 %all-gather.2.cloned.1.call-start = ((), (), s32[]{:S(2)}) async-start(), calls=%async_computation.15 | async-start | bytes 1114112 | tf_op jit(solution)/shard_map/all_gather | solution.py:417
  32.0 5.1 %collective-permute-start.2 = (bf16[64,1024]{1,0:T(8,128)(2,1)S(1)}, bf16[64,1024]{1,0:T(8,128)(2,1)S(1)}, u32[]{:S(2)}, u32[]{:S(2)}) collective-permute-start(bf16[64,1024]{1,0:T(8,128)(2,1)S(1)} %bitcast.151), channel_id=1, source_target_pairs={{0,16},{16,0},{1,17},{17,1},{2,18},{18,2},{3,19},{19,3},{4,20},{20... | collective-permute-start | bytes 393224 | tf_op jit(solution)/shard_map/ppermute | solution.py:25
  37.1 1.7 collective-permute-start.3
  37.3 15.2 %copy-start.36 = (bf16[1,1024,256]{2,1,0:T(8,128)(2,1)}, bf16[1,1024,256]{2,1,0:T(8,128)(2,1)S(1)}, u32[]{:S(2)}) copy-start(bf16[1,1024,256]{2,1,0:T(8,128)(2,1)S(1)} %subtract_convert_fusion.1) | copy-start | bytes 1572868
  37.4 15.2 %collective-permute-start.1 = (bf16[1024,256]{1,0:T(8,128)(2,1)S(1)}, bf16[1024,256]{1,0:T(8,128)(2,1)S(1)}, u32[]{:S(2)}, u32[]{:S(2)}) collective-permute-start(bf16[1024,256]{1,0:T(8,128)(2,1)S(1)} %bitcast.144), channel_id=1, source_target_pairs={{0,16},{16,0},{1,17},{17,1},{2,18},{18,2},{3,19},{19,3},{4,20},{20... | collective-permute-start | bytes 1572872 | tf_op jit(solution)/shard_map/ppermute | solution.py:25
  38.9 12.5 %collective-permute-start.4 = (bf16[128,1024]{1,0:T(8,128)(2,1)S(1)}, bf16[128,1024]{1,0:T(8,128)(2,1)}, u32[]{:S(2)}, u32[]{:S(2)}) collective-permute-start(bf16[128,1024]{1,0:T(8,128)(2,1)S(1)} %maximum_select_fusion.2), channel_id=1, source_target_pairs={{0,2},{1,3},{2,0},{3,1},{4,6},{5,7},{6,4},{7,5},{8,10},{9,11},{10,... | collective-permute-start | bytes 786440 | tf_op jit(solution)/shard_map/ppermute | solution.py:25
  49.0 4.5 %collective-permute-start = (bf16[256,1024]{1,0:T(8,128)(2,1)S(1)}, bf16[256,1024]{1,0:T(8,128)(2,1)S(1)}, u32[]{:S(2)}, u32[]{:S(2)}) collective-permute-start(bf16[256,1024]{1,0:T(8,128)(2,1)S(1)} %bitcast.111), channel_id=1, source_target_pairs={{0,1},{1,0},{2,3},{3,2},{4,5},{5,4},{6,7},{7,6},{8,9},{9,8},{10,11... | collective-permute-start | bytes 1572872 | tf_op jit(solution)/shard_map/ppermute | solution.py:25
  50.5 31.2 %copy-start.37 = (bf16[1,256,1024]{2,1,0:T(8,128)(2,1)}, bf16[1,256,1024]{2,1,0:T(8,128)(2,1)S(1)}, u32[]{:S(2)}) copy-start(bf16[1,256,1024]{2,1,0:T(8,128)(2,1)S(1)} %subtract_convert_fusion) | copy-start | bytes 1572868
  56.4 6.0 %collective-permute-start.6 = (bf16[64,1024]{1,0:T(8,128)(2,1)S(1)}, bf16[64,1024]{1,0:T(8,128)(2,1)S(1)}, u32[]{:S(2)}, u32[]{:S(2)}) collective-permute-start(bf16[64,1024]{1,0:T(8,128)(2,1)S(1)} %get-tuple-element.37), channel_id=1, source_target_pairs={{0,1},{1,0},{2,3},{3,2},{4,5},{5,4},{6,7},{7,6},{8,9},{9,8},{10,11... | collective-permute-start | bytes 393224 | tf_op jit(solution)/shard_map/ppermute | solution.py:25
  57.1 17.0 %all-to-all-start.2 = ((bf16[8,64,640]{2,1,0:T(8,128)(2,1)}), bf16[8,64,640]{2,1,0:T(8,128)(2,1)S(1)}, u32[]{:S(2)}, u32[]{:S(2)}) async-start(bf16[8,64,640]{2,1,0:T(8,128)(2,1)} %bitcast.8), calls=%async_computation.2 | async-start | bytes 1310720 | tf_op jit(solution)/shard_map/all_to_all | solution.py:40
  60.6 21.1 %collective-permute-start.5 = (bf16[256,1024]{1,0:T(8,128)(2,1)S(1)}, bf16[256,1024]{1,0:T(8,128)(2,1)}, u32[]{:S(2)}, u32[]{:S(2)}) collective-permute-start(bf16[256,1024]{1,0:T(8,128)(2,1)S(1)} %bitcast.145), channel_id=1, source_target_pairs={{0,16},{16,0},{1,17},{17,1},{2,18},{18,2},{3,19},{19,3},{4,20},{20... | collective-permute-start | bytes 1572872 | tf_op jit(solution)/shard_map/ppermute | solution.py:25
  62.4 9.4 %collective-permute-start.7 = (bf16[128,1024]{1,0:T(8,128)(2,1)S(1)}, bf16[128,1024]{1,0:T(8,128)(2,1)S(1)}, u32[]{:S(2)}, u32[]{:S(2)}) collective-permute-start(bf16[128,1024]{1,0:T(8,128)(2,1)S(1)} %maximum_select_fusion.3), channel_id=1, source_target_pairs={{0,2},{1,3},{2,0},{3,1},{4,6},{5,7},{6,4},{7,5},{8,10},{9,11},{10,... | collective-permute-start | bytes 786440 | tf_op jit(solution)/shard_map/ppermute | solution.py:25
  76.0 13.7 %all-to-all-start.3 = ((bf16[8,64,256]{2,1,0:T(8,128)(2,1)}), bf16[8,64,256]{2,1,0:T(8,128)(2,1)S(1)}, u32[]{:S(2)}, u32[]{:S(2)}) async-start(bf16[8,64,256]{2,1,0:T(8,128)(2,1)} %bitcast.11), calls=%async_computation.3 | async-start | bytes 524288 | tf_op jit(solution)/shard_map/all_to_all | solution.py:40
  82.8 11.8 %copy-start.1 = (bf16[256,1024]{1,0:T(8,128)(2,1)}, bf16[256,1024]{1,0:T(8,128)(2,1)S(1)}, u32[]{:S(2)}) copy-start(bf16[256,1024]{1,0:T(8,128)(2,1)S(1)} %get-tuple-element.57.refs_2_.refs_3_) | copy-start | bytes 1572868
  94.6 2.0 collective-permute-start.8
  119.2 19.4 %copy-start = (bf16[512,1024]{1,0:T(8,128)(2,1)S(1)}, bf16[512,1024]{1,0:T(8,128)(2,1)}, u32[]{:S(2)}) copy-start(bf16[512,1024]{1,0:T(8,128)(2,1)} %all-gather.2.cloned.1.call-done.refs_1_) | copy-start | bytes 3145732
  138.5 1.9 collective-permute-start.9
  140.4 42.6 %copy-start.3 = (bf16[256,1024]{1,0:T(8,128)(2,1)}, bf16[256,1024]{1,0:T(8,128)(2,1)S(1)}, u32[]{:S(2)}) copy-start(bf16[256,1024]{1,0:T(8,128)(2,1)S(1)} %collective-permute-done.9.refs_2_.refs_3_) | copy-start | bytes 1572868
  184.2 2.0 collective-permute-start.10
  187.2 22.4 %all-to-all-start.8 = ((bf16[8,32,1024]{2,1,0:T(8,128)(2,1)}), bf16[8,32,1024]{2,1,0:T(8,128)(2,1)}, u32[]{:S(2)}, u32[]{:S(2)}) async-start(bf16[8,32,1024]{2,1,0:T(8,128)(2,1)} %bitcast.147), calls=%async_computation.8 | async-start | bytes 1048576 | tf_op jit(solution)/shard_map/all_to_all | solution.py:34
  191.3 62.4 %reduce-scatter.2.cloned.1.call-start = ((), (), s32[]{:S(2)}) async-start(), calls=%async_computation.16 | async-start | bytes 1114112 | tf_op jit(solution)/shard_map/reduce_scatter | solution.py:456
  195.9 13.6 %copy-start.10 = (bf16[32,1024]{1,0:T(8,128)(2,1)S(1)}, bf16[32,1024]{1,0:T(8,128)(2,1)}, u32[]{:S(2)}) copy-start(bf16[32,1024]{1,0:T(8,128)(2,1)} %reshape_squeeze.4.refs_1_) | copy-start | bytes 196612
  211.5 22.5 %all-to-all-start.9 = ((bf16[8,32,1024]{2,1,0:T(8,128)(2,1)}), bf16[8,32,1024]{2,1,0:T(8,128)(2,1)S(1)}, u32[]{:S(2)}, u32[]{:S(2)}) async-start(bf16[8,32,1024]{2,1,0:T(8,128)(2,1)} %bitcast.134), calls=%async_computation.9 | async-start | bytes 1048576 | tf_op jit(solution)/shard_map/all_to_all | solution.py:34
  217.6 16.4 %collective-permute-start.18 = (bf16[2,64,1024]{2,1,0:T(8,128)(2,1)}, bf16[2,64,1024]{2,1,0:T(8,128)(2,1)}, u32[]{:S(2)}, u32[]{:S(2)}) collective-permute-start(bf16[2,64,1024]{2,1,0:T(8,128)(2,1)} %dynamic-slice_bitcast_fusion), channel_id=1, source_target_pairs={{0,1},{1,0},{2,3},{3,2},{4,5},{5,4},{6,7},{7,6},{8,9},{9,8},{10,11... | collective-permute-start | bytes 786440 | tf_op jit(solution)/shard_map/ppermute | solution.py:25
  219.9 91.7 %collective-permute-start.14 = (bf16[1024,256]{1,0:T(8,128)(2,1)}, bf16[1024,256]{1,0:T(8,128)(2,1)}, u32[]{:S(2)}, u32[]{:S(2)}) collective-permute-start(bf16[1024,256]{1,0:T(8,128)(2,1)} %get-tuple-element.69), channel_id=1, source_target_pairs={{0,16},{1,17},{2,18},{3,19},{4,20},{5,21},{6,22},{7,23},{8,24},{9,... | collective-permute-start | bytes 1572872 | tf_op jit(solution)/shard_map/ppermute | solution.py:486
  234.0 5.3 %collective-permute-start.11 = (bf16[256,1024]{1,0:T(8,128)(2,1)S(1)}, bf16[256,1024]{1,0:T(8,128)(2,1)S(1)}, u32[]{:S(2)}, u32[]{:S(2)}) collective-permute-start(bf16[256,1024]{1,0:T(8,128)(2,1)S(1)} %bitcast.121), channel_id=1, source_target_pairs={{0,1},{1,0},{2,3},{3,2},{4,5},{5,4},{6,7},{7,6},{8,9},{9,8},{10,11... | collective-permute-start | bytes 1572872 | tf_op jit(solution)/shard_map/ppermute | solution.py:25
  235.8 8.5 %collective-permute-start.19 = (bf16[64,1024]{1,0:T(8,128)(2,1)}, bf16[64,1024]{1,0:T(8,128)(2,1)}, u32[]{:S(2)}, u32[]{:S(2)}) collective-permute-start(bf16[64,1024]{1,0:T(8,128)(2,1)} %dynamic-slice_bitcast_fusion.2), channel_id=1, source_target_pairs={{0,2},{1,3},{2,0},{3,1},{4,6},{5,7},{6,4},{7,5},{8,10},{9,11},{10,... | collective-permute-start | bytes 393224 | tf_op jit(solution)/shard_map/ppermute | solution.py:25
  238.0 55.8 %collective-permute-start.22 = (bf16[256,1024]{1,0:T(8,128)(2,1)}, bf16[256,1024]{1,0:T(8,128)(2,1)}, u32[]{:S(2)}, u32[]{:S(2)}) collective-permute-start(bf16[256,1024]{1,0:T(8,128)(2,1)} %get-tuple-element.73), channel_id=1, source_target_pairs={{0,16},{1,17},{2,18},{3,19},{4,20},{5,21},{6,22},{7,23},{8,24},{9,... | collective-permute-start | bytes 1572872 | tf_op jit(solution)/shard_map/ppermute | solution.py:486
  240.8 13.8 %all-to-all-start.10 = ((bf16[8,64,256]{2,1,0:T(8,128)(2,1)}), bf16[8,64,256]{2,1,0:T(8,128)(2,1)S(1)}, u32[]{:S(2)}, u32[]{:S(2)}) async-start(bf16[8,64,256]{2,1,0:T(8,128)(2,1)} %bitcast.26), calls=%async_computation.10 | async-start | bytes 524288 | tf_op jit(solution)/shard_map/all_to_all | solution.py:40
  246.0 8.6 %copy-start.29 = (f32[64,640]{1,0:T(8,128)S(1)}, f32[64,640]{1,0:T(8,128)}, u32[]{:S(2)}) copy-start(f32[64,640]{1,0:T(8,128)} %copy-done.28) | copy-start | bytes 491524
  246.0 68.1 %collective-permute-start.20 = (bf16[64,1024]{1,0:T(8,128)(2,1)}, bf16[64,1024]{1,0:T(8,128)(2,1)}, u32[]{:S(2)}, u32[]{:S(2)}) collective-permute-start(bf16[64,1024]{1,0:T(8,128)(2,1)} %fusion.5), channel_id=1, source_target_pairs={{0,16},{1,17},{2,18},{3,19},{4,20},{5,21},{6,22},{7,23},{8,24},{9,... | collective-permute-start | bytes 393224 | tf_op jit(solution)/shard_map/ppermute | solution.py:486
  256.3 16.9 %all-to-all-start.11 = ((bf16[8,64,640]{2,1,0:T(8,128)(2,1)}), bf16[8,64,640]{2,1,0:T(8,128)(2,1)S(1)}, u32[]{:S(2)}, u32[]{:S(2)}) async-start(bf16[8,64,640]{2,1,0:T(8,128)(2,1)} %bitcast.28), calls=%async_computation.11 | async-start | bytes 1310720 | tf_op jit(solution)/shard_map/all_to_all | solution.py:40
  263.2 10.0 %copy-start.12 = (bf16[1024,256]{1,0:T(8,128)(2,1)S(1)}, bf16[1024,256]{1,0:T(8,128)(2,1)}, u32[]{:S(2)}) copy-start(bf16[1024,256]{1,0:T(8,128)(2,1)} %copy-done.11) | copy-start | bytes 1572868
  263.2 10.0 %copy-start.16 = (bf16[256,1024]{1,0:T(8,128)(2,1)S(1)}, bf16[256,1024]{1,0:T(8,128)(2,1)}, u32[]{:S(2)}) copy-start(bf16[256,1024]{1,0:T(8,128)(2,1)} %copy-done.15) | copy-start | bytes 1572868
  264.6 31.3 %collective-permute-start.21 = (bf16[256,1024]{1,0:T(8,128)(2,1)}, bf16[256,1024]{1,0:T(8,128)(2,1)}, u32[]{:S(2)}, u32[]{:S(2)}) collective-permute-start(bf16[256,1024]{1,0:T(8,128)(2,1)} %get-tuple-element.75), channel_id=1, source_target_pairs={{16,0},{17,1},{18,2},{19,3},{20,4},{21,5},{22,6},{23,7},{24,8},{25... | collective-permute-start | bytes 1572872 | tf_op jit(solution)/shard_map/ppermute | solution.py:487
  274.4 2.9 collective-permute-start.12
  277.2 11.1 %collective-permute-start.15 = (bf16[2,64,1024]{2,1,0:T(8,128)(2,1)}, bf16[2,64,1024]{2,1,0:T(8,128)(2,1)}, u32[]{:S(2)}, u32[]{:S(2)}) collective-permute-start(bf16[2,64,1024]{2,1,0:T(8,128)(2,1)} %dynamic-slice_bitcast_fusion.1), channel_id=1, source_target_pairs={{0,1},{1,0},{2,3},{3,2},{4,5},{5,4},{6,7},{7,6},{8,9},{9,8},{10,11... | collective-permute-start | bytes 786440 | tf_op jit(solution)/shard_map/ppermute | solution.py:25
  278.7 27.2 %all-to-all-start.12 = ((bf16[8,32,1024]{2,1,0:T(8,128)(2,1)}), bf16[8,32,1024]{2,1,0:T(8,128)(2,1)S(1)}, u32[]{:S(2)}, u32[]{:S(2)}) async-start(bf16[8,32,1024]{2,1,0:T(8,128)(2,1)} %bitcast.30), calls=%async_computation.12 | async-start | bytes 1048576 | tf_op jit(solution)/shard_map/all_to_all | solution.py:34
  285.9 10.0 %copy-start.32 = (f32[256,1024]{1,0:T(8,128)S(1)}, f32[256,1024]{1,0:T(8,128)}, u32[]{:S(2)}) copy-start(f32[256,1024]{1,0:T(8,128)} %get-tuple-element.74) | copy-start | bytes 3145732
  288.4 23.2 %collective-permute-start.13 = (bf16[1024,256]{1,0:T(8,128)(2,1)}, bf16[1024,256]{1,0:T(8,128)(2,1)}, u32[]{:S(2)}, u32[]{:S(2)}) collective-permute-start(bf16[1024,256]{1,0:T(8,128)(2,1)} %get-tuple-element.71), channel_id=1, source_target_pairs={{16,0},{17,1},{18,2},{19,3},{20,4},{21,5},{22,6},{23,7},{24,8},{25... | collective-permute-start | bytes 1572872 | tf_op jit(solution)/shard_map/ppermute | solution.py:487
  293.7 8.7 %copy-start.41 = (bf16[2,64,1024]{2,1,0:T(8,128)(2,1)}, bf16[2,64,1024]{2,1,0:T(8,128)(2,1)S(1)}, u32[]{:S(2)}) copy-start(bf16[2,64,1024]{2,1,0:T(8,128)(2,1)S(1)} %fusion.3) | copy-start | bytes 786436
  293.8 8.7 %collective-permute-start.16 = (bf16[64,1024]{1,0:T(8,128)(2,1)S(1)}, bf16[64,1024]{1,0:T(8,128)(2,1)S(1)}, u32[]{:S(2)}, u32[]{:S(2)}) collective-permute-start(bf16[64,1024]{1,0:T(8,128)(2,1)S(1)} %dynamic-slice_bitcast_fusion.3), channel_id=1, source_target_pairs={{0,2},{1,3},{2,0},{3,1},{4,6},{5,7},{6,4},{7,5},{8,10},{9,11},{10,... | collective-permute-start | bytes 393224 | tf_op jit(solution)/shard_map/ppermute | solution.py:25
  302.5 11.6 %collective-permute-start.17 = (bf16[64,1024]{1,0:T(8,128)(2,1)S(1)}, bf16[64,1024]{1,0:T(8,128)(2,1)S(1)}, u32[]{:S(2)}, u32[]{:S(2)}) collective-permute-start(bf16[64,1024]{1,0:T(8,128)(2,1)S(1)} %fusion.4), channel_id=1, source_target_pairs={{16,0},{17,1},{18,2},{19,3},{20,4},{21,5},{22,6},{23,7},{24,8},{25... | collective-permute-start | bytes 393224 | tf_op jit(solution)/shard_map/ppermute | solution.py:487
  307.9 10.9 %all-to-all-start.13 = ((bf16[16,8,1024]{2,1,0:T(8,128)(2,1)}), bf16[16,8,1024]{2,1,0:T(8,128)(2,1)S(1)}, u32[]{:S(2)}, u32[]{:S(2)}) async-start(bf16[16,8,1024]{2,1,0:T(8,128)(2,1)} %all_to_all.132), calls=%async_computation.14 | async-start | bytes 524288 | tf_op jit(solution)/shard_map/all_to_all | solution.py:495
  (35 other events, 87.1 us)
Sparse Core Ops, SparseCore 0:
  55.8 35.8 all-gather.1
  195.3 58.4 reduce-scatter.1
